TPU v7x, 32 devices: a whole 2x2x4 slice. The times are simulated.
32 devices in a mesh: dp: 4 (over y, x), row: 4 (over z), col: 2 (over core).
Axes of the slice: x: 2, y: 2, z: 4, core: 2. Of those that a mesh axis runs over, the one named last changes fastest.
Arguments:
- activations: bfloat16 [2048, 2048], P(('dp', 'row'), 'col'), may hold values from -6 to 6
- cotangent: bfloat16 [2048, 2048], P(('dp', 'row'), 'col'), may hold values from -6 to 6
- routing: int32 [2048, 6], P(('dp', 'row')), may hold values from 0 to 15, all different within a row; in each aligned block of 128 rows (0 to 127, 128 to 255, ...) at most 64 rows name the same one
- segments: int32 [2048], P('dp'), may hold values from 0 to 15, never falling along the last dimension, each value on 1 to 256 neighbouring positions
- scaling: float32 [2048], P('col'), may hold values from 0.25 to 1.75
- queries: bfloat16 [2048, 3072], P('col', 'row'), may hold values from -0.1875 to 0.1875
- compress: bfloat16 [2048, 576], P('col', 'row'), may hold values from -0.125 to 0.125
- rescale: float32 [512], replicated, may hold values from 0.25 to 1.75
- expand: bfloat16 [512, 4096], P(None, 'row'), may hold values from -0.25 to 0.25
- combine: bfloat16 [2048, 2048], P('row', 'col'), may hold values from -1.5 to 1.5
- premix: float32 [2048], P('col'), may hold values from 0.25 to 1.75
- router: bfloat16 [2048, 16], P('col'), may hold values from -0.0625 to 0.0625
- widening: bfloat16 [2, 2048, 2816], P(None, 'col', 'row'), may hold values from -0.125 to 0.125
- narrowing: bfloat16 [2816, 2048], P('row', 'col'), may hold values from -0.109375 to 0.109375
- fanout: bfloat16 [16, 2, 2048, 1408], P(('dp', 'row'), None, None, 'col'), may hold values from -0.125 to 0.125
- funnel: bfloat16 [16, 1408, 2048], P(('dp', 'row'), 'col'), may hold values from -2.5 to 2.5
Outputs:
- layer_output: bfloat16 [2048, 2048], P(('dp', 'row'), 'col')
- input_grad: float32 [2048, 2048], P(('dp', 'row'), 'col')
- scaling_grad: float32 [2048], P('col')
- queries_grad: float32 [2048, 3072], P('col', 'row')
- compress_grad: float32 [2048, 576], P('col', 'row')
- rescale_grad: float32 [512], replicated
- expand_grad: float32 [512, 4096], P(None, 'row')
- combine_grad: float32 [2048, 2048], P('row', 'col')
- premix_grad: float32 [2048], P('col')
- router_grad: float32 [2048, 16], P('col')
- widening_grad: float32 [2, 2048, 2816], P(None, 'col', 'row')
- narrowing_grad: float32 [2816, 2048], P('row', 'col')
- fanout_grad: float32 [16, 2, 2048, 1408], P(('dp', 'row'), None, None, 'col')
- funnel_grad: float32 [16, 1408, 2048], P(('dp', 'row'), 'col')
Inputs may be any that keep to these rules, and one draw needn't show every extreme that they name: `routing`: each row names 6 different experts. In each aligned block of 128 rows (the tokens of one index of dp and row) no expert is named by more than 64 rows, a bound that some block reaches. `segments`: never falling along the tokens; each value covers 1 to 256 consecutive tokens, and some value covers exactly 256.
All inputs are finite; a program needn't handle non-finite values.
Results may differ from a plain program's by a relative error of at most 0.03.
Values may be sent and summed in bfloat16 or wider, within the bound.
A program may use at most 256 MiB of HBM per device.

v0:
```python
import jax
import jax.numpy as jnp
from jax import lax
from jax.sharding import PartitionSpec as P

D = 2048
NOPE = 128
ROPE = 64
HEADV = 128
RANK = 512
TOP = 6


epsilon = 1e-06
masked_score = -1e30


def for_sending(x):

    def short(part):
        return part.astype(jnp.bfloat16) if part.dtype == jnp.float32 else part

    return jax.tree.map(short, x)


def silu_slope(values):
    sigmoid = jax.nn.sigmoid(values)
    return sigmoid * (1.0 + values * (1.0 - sigmoid))


def rotation(positions, rope_width):
    half_width = rope_width // 2
    frequency = 10000.0 ** (-jnp.arange(half_width, dtype=jnp.float32) * 2.0 / rope_width)
    angles = positions.astype(jnp.float32)[:, None] * frequency[None, :]
    return (jnp.cos(angles), jnp.sin(angles))


def rotate(values, cosine, sine_table, direction):
    half_width = values.shape[-1] // 2
    first_half = values[..., :half_width]
    second_half = values[..., half_width:]
    return jnp.concatenate(
        [
            first_half * cosine - direction * second_half * sine_table,
            second_half * cosine + direction * first_half * sine_table,
        ],
        axis=-1,
    )


def col_totals(values):
    return lax.psum(values, "col")


def row_totals(values):
    return jax.tree.map(lambda part: part.astype(jnp.float32), lax.psum(for_sending(values), "row"))


def row_gather(values):
    return (lax.all_gather(values[0], "row", axis=0, tiled=True),)


def col_gather(values):
    return jax.tree.map(
        lambda part, own: part.astype(own.dtype),
        lax.all_gather(for_sending(values), "col", axis=0, tiled=True),
        values,
    )


def col_scatter(values):
    return lax.psum_scatter(values, "col", scatter_dimension=0, tiled=True)


def row_scatter(values):
    return (
        lax.psum_scatter(
            values[0].astype(jnp.bfloat16), "row", scatter_dimension=0, tiled=True
        ).astype(jnp.float32),
    )


def expert_exchange(values):
    return lax.all_to_all(values, ("dp", "row"), split_axis=0, concat_axis=0, tiled=True)


def expert_gather(values):
    return lax.all_gather(values, "col", axis=2, tiled=True)


def expert_scatter(values):
    return lax.psum_scatter(
        values.astype(jnp.bfloat16), "col", scatter_dimension=2, tiled=True
    ).astype(jnp.float32)


def norm_scale(values):
    square_sum = col_totals(jnp.sum(values * values, axis=1))
    return lax.rsqrt(square_sum / D + epsilon)


def norm_back(values, row_scale, gain_vector, upstream):
    weighted = upstream * gain_vector
    inner_mean = col_totals(jnp.sum(weighted * values, axis=1)) / D
    gain_grad = jnp.sum(upstream * values * row_scale[:, None], axis=0)
    values_grad = weighted * row_scale[:, None] - values * (row_scale**3 * inner_mean)[:, None]
    return (values_grad, gain_grad)


def local(
    activations,
    cotangent,
    routing,
    segments,
    scaling,
    queries,
    compress,
    rescale,
    expand,
    combine,
    premix,
    router,
    widening,
    narrowing,
    fanout,
    funnel,
):
    row_count = lax.axis_size("row")
    col_count = lax.axis_size("col")
    row_index = lax.axis_index("row")
    col_index = lax.axis_index("col")
    local_rows = activations.shape[0]
    col_width = activations.shape[1]
    seq_length = local_rows * row_count
    half_length = seq_length // col_count
    head_width = NOPE + ROPE
    pair_width = NOPE + HEADV
    local_heads = queries.shape[1] // head_width
    slice_width = compress.shape[1]
    expert_total = router.shape[1]
    capacity = local_rows * TOP * 4 // (3 * expert_total)
    block_rows = min(512, half_length)
    block_count = half_length // block_rows
    score_scale = head_width ** (-0.5)
    inputs = activations.astype(jnp.float32)
    scale_one = norm_scale(inputs)
    normed_one = (inputs * scale_one[:, None] * scaling).astype(jnp.bfloat16)
    (gathered_one,) = row_gather((normed_one,))
    query_part = jnp.dot(gathered_one, queries, preferred_element_type=jnp.float32)
    latent_part = jnp.dot(gathered_one, compress, preferred_element_type=jnp.float32)
    query_raw, latent_slice = col_scatter((query_part, latent_part))
    latent_raw = lax.all_gather(latent_slice, "row", axis=1, tiled=True)
    latent_plain = latent_raw[:, :RANK]
    latent_scale = lax.rsqrt(jnp.mean(latent_plain * latent_plain, axis=1) + epsilon)
    latent_normed = (latent_plain * latent_scale[:, None] * rescale).astype(jnp.bfloat16)
    expanded = jnp.dot(latent_normed, expand, preferred_element_type=jnp.float32).reshape(
        half_length, local_heads, pair_width
    )
    positions = col_index * half_length + jnp.arange(half_length, dtype=jnp.int32)
    cosine, sine_table = rotation(positions, ROPE)
    key_shared = rotate(latent_raw[:, RANK:], cosine, sine_table, 1.0)
    query_heads = query_raw.reshape(half_length, local_heads, head_width)
    query_local = jnp.concatenate(
        [
            query_heads[..., :NOPE],
            rotate(query_heads[..., NOPE:], cosine[:, None, :], sine_table[:, None, :], 1.0),
        ],
        axis=2,
    ).astype(jnp.bfloat16)
    key_local = jnp.concatenate(
        [
            expanded[..., :NOPE],
            jnp.broadcast_to(key_shared[:, None, :], (half_length, local_heads, ROPE)),
        ],
        axis=2,
    ).astype(jnp.bfloat16)
    value_local = expanded[..., NOPE:].astype(jnp.bfloat16)
    key_flat, value_flat = col_gather(
        (
            key_local.reshape(half_length, local_heads * head_width),
            value_local.reshape(half_length, local_heads * HEADV),
        )
    )
    key_heads = key_flat.reshape(seq_length, local_heads, head_width)
    value_heads = value_flat.reshape(seq_length, local_heads, HEADV)
    own_segments = lax.dynamic_slice_in_dim(
        segments, col_index * half_length, half_length, 0
    ).reshape(block_count, block_rows)
    query_blocks = query_local.reshape(block_count, block_rows, local_heads, head_width)

    def attend_block(inputs_block):
        query_block, segment_block = inputs_block
        scores = (
            jnp.einsum("qhd,khd->hqk", query_block, key_heads, preferred_element_type=jnp.float32)
            * score_scale
        )
        visible = segments[None, None, :] <= segment_block[None, :, None]
        scores = jnp.where(visible, scores, masked_score)
        largest = jnp.max(scores, axis=2, keepdims=True)
        weight = jnp.exp(scores - largest)
        totals = jnp.sum(weight, axis=2, keepdims=True)
        probability = (weight / totals).astype(jnp.bfloat16)
        result = jnp.einsum(
            "hqk,khd->qhd", probability, value_heads, preferred_element_type=jnp.float32
        )
        return (result.astype(jnp.bfloat16), (largest + jnp.log(totals))[..., 0])

    attended_blocks, log_totals = lax.map(attend_block, (query_blocks, own_segments))
    attended = attended_blocks.reshape(half_length, local_heads * HEADV)
    (attended_all,) = col_gather((attended,))
    (branch,) = row_scatter((jnp.dot(attended_all, combine, preferred_element_type=jnp.float32),))
    residual = inputs + branch
    scale_two = norm_scale(residual)
    normed_two = (residual * scale_two[:, None] * premix).astype(jnp.bfloat16)
    logits = col_totals(jnp.dot(normed_two, router, preferred_element_type=jnp.float32))
    router_probs = jax.nn.softmax(logits, axis=1)
    expert_range = jnp.arange(expert_total, dtype=jnp.int32)
    chosen = routing[:, :, None] == expert_range[None, None, :]
    gate_values = jnp.sum(jnp.where(chosen, router_probs[:, None, :], 0.0), axis=2)
    flat_expert = routing.reshape(-1)
    matches = (flat_expert[:, None] == expert_range[None, :]).astype(jnp.int32)
    earlier = jnp.cumsum(matches, axis=0) - matches
    places = flat_expert * capacity + jnp.sum(earlier * matches, axis=1)
    pair_count = flat_expert.shape[0]
    outgoing = (
        jnp.zeros((expert_total * capacity, col_width), jnp.bfloat16)
        .at[places]
        .set(jnp.repeat(normed_two, TOP, axis=0))
    )
    incoming = expert_exchange(outgoing.reshape(expert_total, capacity, col_width))
    expert_rows = expert_gather(incoming).reshape(expert_total * capacity, col_width * col_count)
    inner_weight = fanout[0]
    outer_weight = funnel[0]
    expert_gate_up = jnp.einsum(
        "rd,gdf->grf", expert_rows, inner_weight, preferred_element_type=jnp.float32
    )
    expert_hidden = (jax.nn.silu(expert_gate_up[0]) * expert_gate_up[1]).astype(jnp.bfloat16)
    reply_part = jnp.dot(expert_hidden, outer_weight, preferred_element_type=jnp.float32).reshape(
        expert_total, capacity, col_width * col_count
    )
    reply_sum = expert_scatter(reply_part)
    replies = expert_exchange(reply_sum.astype(jnp.bfloat16)).reshape(
        expert_total * capacity, col_width
    )
    reply_rows = replies[places].reshape(local_rows, TOP, col_width)
    routed = jnp.sum(gate_values[:, :, None] * reply_rows, axis=1)
    (gathered_two,) = row_gather((normed_two,))
    (shared_gate_up,) = col_scatter(
        (jnp.einsum("td,gdf->tgf", gathered_two, widening, preferred_element_type=jnp.float32),)
    )
    shared_hidden = (jax.nn.silu(shared_gate_up[:, 0]) * shared_gate_up[:, 1]).astype(jnp.bfloat16)
    (hidden_all,) = col_gather((shared_hidden,))
    (shared_out,) = row_scatter(
        (jnp.dot(hidden_all, narrowing, preferred_element_type=jnp.float32),)
    )
    layer_output = (residual + shared_out + routed).astype(jnp.bfloat16)
    upstream = cotangent.astype(jnp.float32)
    gate_grad = col_totals(jnp.sum(upstream[:, None, :] * reply_rows, axis=2))
    reply_grads = (
        (gate_values[:, :, None] * upstream[:, None, :])
        .astype(jnp.bfloat16)
        .reshape(pair_count, col_width)
    )
    back_out = (
        jnp.zeros((expert_total * capacity, col_width), jnp.bfloat16).at[places].set(reply_grads)
    )
    back_in = expert_exchange(back_out.reshape(expert_total, capacity, col_width))
    reply_grad_rows = expert_gather(back_in).reshape(expert_total * capacity, col_width * col_count)
    funnel_grad = jnp.einsum(
        "rf,rd->fd", expert_hidden, reply_grad_rows, preferred_element_type=jnp.float32
    )[None]
    hidden_grad = jnp.einsum(
        "rd,fd->rf", reply_grad_rows, outer_weight, preferred_element_type=jnp.float32
    )
    gate_input = expert_gate_up[0]
    up_input = expert_gate_up[1]
    expert_gu_grad = jnp.stack(
        [hidden_grad * up_input * silu_slope(gate_input), hidden_grad * jax.nn.silu(gate_input)]
    ).astype(jnp.bfloat16)
    fanout_grad = jnp.einsum(
        "rd,grf->gdf", expert_rows, expert_gu_grad, preferred_element_type=jnp.float32
    )[None]
    input_part = jnp.einsum(
        "grf,gdf->rd", expert_gu_grad, inner_weight, preferred_element_type=jnp.float32
    ).reshape(expert_total, capacity, col_width * col_count)
    input_sum = expert_scatter(input_part)
    returned = expert_exchange(input_sum.astype(jnp.bfloat16)).reshape(
        expert_total * capacity, col_width
    )
    normed_grad = jnp.sum(
        returned[places].astype(jnp.float32).reshape(local_rows, TOP, col_width), axis=1
    )
    probs_grad = jnp.sum(jnp.where(chosen, gate_grad[:, :, None], 0.0), axis=1)
    logit_grad = router_probs * (
        probs_grad - jnp.sum(router_probs * probs_grad, axis=1, keepdims=True)
    )
    router_part = jnp.einsum(
        "td,te->de", normed_two, logit_grad, preferred_element_type=jnp.float32
    )
    normed_grad = normed_grad + jnp.einsum(
        "te,de->td", logit_grad, router, preferred_element_type=jnp.float32
    )
    (cotangent_all,) = row_gather((cotangent,))
    narrowing_grad = jnp.einsum(
        "tf,td->fd", hidden_all, cotangent_all, preferred_element_type=jnp.float32
    )
    (shared_hidden_grad,) = col_scatter(
        (jnp.einsum("td,fd->tf", cotangent_all, narrowing, preferred_element_type=jnp.float32),)
    )
    shared_gu_grad = jnp.stack(
        [
            shared_hidden_grad * shared_gate_up[:, 1] * silu_slope(shared_gate_up[:, 0]),
            shared_hidden_grad * jax.nn.silu(shared_gate_up[:, 0]),
        ],
        axis=1,
    ).astype(jnp.bfloat16)
    (gu_grad_all,) = col_gather((shared_gu_grad,))
    widening_grad = jnp.einsum(
        "td,tgf->gdf", gathered_two, gu_grad_all, preferred_element_type=jnp.float32
    )
    (shared_input_grad,) = row_scatter(
        (jnp.einsum("tgf,gdf->td", gu_grad_all, widening, preferred_element_type=jnp.float32),)
    )
    normed_grad = normed_grad + shared_input_grad
    residual_norm_grad, premix_part = norm_back(residual, scale_two, premix, normed_grad)
    residual_grad = upstream + residual_norm_grad
    (branch_all,) = row_gather((residual_grad.astype(jnp.bfloat16),))
    combine_grad = jnp.einsum(
        "tv,td->vd", attended_all, branch_all, preferred_element_type=jnp.float32
    )
    (attended_grad,) = col_scatter(
        (jnp.einsum("td,vd->tv", branch_all, combine, preferred_element_type=jnp.float32),)
    )
    attended_grad_blocks = attended_grad.astype(jnp.bfloat16).reshape(
        block_count, block_rows, local_heads, HEADV
    )

    def attend_back(carried, inputs_block):
        key_sum, value_sum = carried
        query_block, grad_block, log_block, segment_block = inputs_block
        scores = (
            jnp.einsum("qhd,khd->hqk", query_block, key_heads, preferred_element_type=jnp.float32)
            * score_scale
        )
        visible = segments[None, None, :] <= segment_block[None, :, None]
        probability = jnp.where(visible, jnp.exp(scores - log_block[..., None]), 0.0)
        weight_grad = jnp.einsum(
            "qhd,khd->hqk", grad_block, value_heads, preferred_element_type=jnp.float32
        )
        inner_sum = jnp.sum(probability * weight_grad, axis=2, keepdims=True)
        score_grad = (probability * (weight_grad - inner_sum)).astype(jnp.bfloat16)
        query_grad_block = (
            jnp.einsum("hqk,khd->qhd", score_grad, key_heads, preferred_element_type=jnp.float32)
            * score_scale
        )
        key_sum = (
            key_sum
            + jnp.einsum(
                "hqk,qhd->khd", score_grad, query_block, preferred_element_type=jnp.float32
            )
            * score_scale
        )
        value_sum = value_sum + jnp.einsum(
            "hqk,qhd->khd",
            probability.astype(jnp.bfloat16),
            grad_block,
            preferred_element_type=jnp.float32,
        )
        return ((key_sum, value_sum), query_grad_block)

    key_start = jnp.zeros((seq_length, local_heads, head_width), jnp.float32)
    value_start = jnp.zeros((seq_length, local_heads, HEADV), jnp.float32)
    (key_grad_all, value_grad_all), query_grad_blocks = lax.scan(
        attend_back,
        (key_start, value_start),
        (query_blocks, attended_grad_blocks, log_totals, own_segments),
    )
    key_grad, value_grad = col_scatter(
        (
            key_grad_all.reshape(seq_length, local_heads * head_width),
            value_grad_all.reshape(seq_length, local_heads * HEADV),
        )
    )
    key_grad = key_grad.reshape(half_length, local_heads, head_width)
    value_grad = value_grad.reshape(half_length, local_heads, HEADV)
    query_grad = query_grad_blocks.reshape(half_length, local_heads, head_width)
    query_raw_grad = (
        jnp.concatenate(
            [
                query_grad[..., :NOPE],
                rotate(query_grad[..., NOPE:], cosine[:, None, :], sine_table[:, None, :], -1.0),
            ],
            axis=2,
        )
        .astype(jnp.bfloat16)
        .reshape(half_length, local_heads * head_width)
    )
    expanded_grad = (
        jnp.concatenate([key_grad[..., :NOPE], value_grad], axis=2)
        .astype(jnp.bfloat16)
        .reshape(half_length, local_heads * pair_width)
    )
    shared_rope_grad = rotate(jnp.sum(key_grad[..., NOPE:], axis=1), cosine, sine_table, -1.0)
    expand_part = jnp.einsum(
        "tr,tc->rc", latent_normed, expanded_grad, preferred_element_type=jnp.float32
    )
    normed_latent_grad = jnp.einsum(
        "tc,rc->tr", expanded_grad, expand, preferred_element_type=jnp.float32
    )
    latent_grad_full = row_totals(jnp.concatenate([normed_latent_grad, shared_rope_grad], axis=1))
    latent_weighted = latent_grad_full[:, :RANK] * rescale
    latent_inner = jnp.mean(latent_weighted * latent_plain, axis=1)
    rescale_part = jnp.sum(
        latent_grad_full[:, :RANK] * latent_plain * latent_scale[:, None], axis=0
    )
    plain_grad = (
        latent_weighted * latent_scale[:, None]
        - latent_plain * (latent_scale**3 * latent_inner)[:, None]
    )
    latent_raw_grad = jnp.concatenate([plain_grad, latent_grad_full[:, RANK:]], axis=1)
    own_latent_grad = lax.dynamic_slice_in_dim(
        latent_raw_grad, row_index * slice_width, slice_width, 1
    ).astype(jnp.bfloat16)
    query_grad_all, latent_grad_all = col_gather((query_raw_grad, own_latent_grad))
    queries_part = jnp.einsum(
        "td,tc->dc", gathered_one, query_grad_all, preferred_element_type=jnp.float32
    )
    compress_part = jnp.einsum(
        "td,tc->dc", gathered_one, latent_grad_all, preferred_element_type=jnp.float32
    )
    first_part = jnp.einsum(
        "tc,dc->td", query_grad_all, queries, preferred_element_type=jnp.float32
    ) + jnp.einsum("tc,dc->td", latent_grad_all, compress, preferred_element_type=jnp.float32)
    (first_grad,) = row_scatter((first_part,))
    input_norm_grad, scaling_part = norm_back(inputs, scale_one, scaling, first_grad)
    input_grad = residual_grad + input_norm_grad
    expand_sum, rescale_sum = col_totals((expand_part, rescale_part))
    router_sum, scaling_sum, premix_sum = row_totals((router_part, scaling_part, premix_part))
    gradients = (
        lax.psum(scaling_sum.astype(jnp.bfloat16), "dp").astype(jnp.float32),
        lax.psum(queries_part.astype(jnp.bfloat16), "dp").astype(jnp.float32),
        lax.psum(compress_part.astype(jnp.bfloat16), "dp").astype(jnp.float32),
        lax.psum(rescale_sum.astype(jnp.bfloat16), "dp").astype(jnp.float32),
        lax.psum(expand_sum.astype(jnp.bfloat16), "dp").astype(jnp.float32),
        lax.psum(combine_grad.astype(jnp.bfloat16), "dp").astype(jnp.float32),
        lax.psum(premix_sum.astype(jnp.bfloat16), "dp").astype(jnp.float32),
        lax.psum(router_sum.astype(jnp.bfloat16), "dp").astype(jnp.float32),
        lax.psum(widening_grad.astype(jnp.bfloat16), "dp").astype(jnp.float32),
        lax.psum(narrowing_grad.astype(jnp.bfloat16), "dp").astype(jnp.float32),
    )
    return (
        layer_output,
        input_grad,
        gradients[0],
        gradients[1],
        gradients[2],
        gradients[3],
        gradients[4],
        gradients[5],
        gradients[6],
        gradients[7],
        gradients[8],
        gradients[9],
        fanout_grad,
        funnel_grad,
    )


def solution(mesh):
    placed = (
        P(("dp", "row"), "col"),
        P(("dp", "row"), "col"),
        P(("dp", "row"), None),
        P("dp"),
        P("col"),
        P("col", "row"),
        P("col", "row"),
        P(),
        P(None, "row"),
        P("row", "col"),
        P("col"),
        P("col", None),
        P(None, "col", "row"),
        P("row", "col"),
        P(("dp", "row"), None, None, "col"),
        P(("dp", "row"), "col", None),
    )
    return jax.shard_map(
        local,
        mesh=mesh,
        in_specs=placed,
        out_specs=(
            P(("dp", "row"), "col"),
            P(("dp", "row"), "col"),
            P("col"),
            P("col", "row"),
            P("col", "row"),
            P(),
            P(None, "row"),
            P("row", "col"),
            P("col"),
            P("col", None),
            P(None, "col", "row"),
            P("row", "col"),
            P(("dp", "row"), None, None, "col"),
            P(("dp", "row"), "col", None),
        ),
        check_vma=False,
    )
```

profile of v0, /device:TPU:9, one launch (start us, length us, event | category | flops | bytes accessed | tf_op | source)
XLA Modules:
  0.0 871.5 jit_solution(10952027806312588131)
XLA Ops:
  13.1 28.6 %all-gather.8.cloned.1.call-done = bf16[512,1024]{1,0:T(8,128)(2,1)} async-done(((bf16[128,1024]{1,0:T(8,128)(2,1)}), bf16[512,1024]{1,0:T(8,128)(2,1)}) %all-gather.8.cloned.1.call-update) | async-done | bytes 1048592 | tf_op jit(solution)/shard_map/all_gather | solution.py:60
  44.3 3.9 fusion.97
  52.7 13.7 %all_gather.43 = f32[256,576]{0,1:T(8,128)S(1)} all-gather(f32[256,144]{0,1:T(8,128)} %reduce-scatter.14.cloned.1.call-done), channel_id=1, replica_groups=mesh['dp'=4,'row'=4,'col'=2] {'row'}, dimensions={1}, use_global_device_ids=true | all-gather | bytes 737280 | tf_op jit(solution)/shard_map/all_gather | solution.py:152
  79.3 7.1 all_gather.44
  108.5 19.6 %reduce-scatter.18.cloned.1.call-done = bf16[128,1024]{1,0:T(8,128)(2,1)} async-done(((bf16[512,1024]{1,0:T(8,128)(2,1)}), bf16[128,1024]{1,0:T(8,128)(2,1)}) %reduce-scatter.18.cloned.1.call-update) | async-done | bytes 262160 | tf_op jit(solution)/shard_map/reduce_scatter | solution.py:77
  136.5 3.7 reshape.351
  140.2 8.1 scatter_custom_fusion
  148.4 52.6 %all_to_all.20 = bf16[16,64,1024]{2,1,0:T(8,128)(2,1)} all-to-all(bf16[16,64,1024]{2,1,0:T(8,128)(2,1)} %bitcast.213), channel_id=1, replica_groups=mesh['dp'=4,'row'=4,'col'=2] {'dp','row'}, dimensions={0} | all-to-all | bytes 4194304 | tf_op jit(solution)/shard_map/all_to_all | solution.py:84
  201.0 3.5 mul.471
  204.5 4.7 mul.472
  210.4 4.4 psum.156
  217.5 8.8 %scatter_custom_fusion.1 = bf16[1024,1024]{1,0:T(8,128)(2,1)} fusion(s32[768]{0:T(1024)} %copy-done.71, f32[768,1024]{1,0:T(8,128)} %mul.472, f32[768]{0:T(1024)} %mul.469, bf16[]{:T(256)} %constant.66.clone.1), kind=kCustom, calls=%fused_computation.47 | custom fusion | flops 1572864 | bytes 5247488 | tf_op jit(solution)/shard_map/scatter | solution.py:265
  226.3 7.2 all-to-all-start.2
  234.9 62.1 %all-to-all-done.2 = bf16[16,64,1024]{2,1,0:T(8,128)(2,1)} async-done(((bf16[16,64,1024]{2,1,0:T(8,128)(2,1)}), bf16[16,64,1024]{2,1,0:T(8,128)(2,1)}, u32[]{:S(2)}, u32[]{:S(2)}) %all-to-all-start.2) | async-done | bytes 2097184 | tf_op jit(solution)/shard_map/all_to_all | solution.py:84
  297.0 9.6 %fusion.18 = f32[2,1024,704]{1,2,0:T(8,128)S(1)} fusion(bf16[1024,2048,1]{1,0,2:T(8,128)(2,1)} %bitcast.236, bf16[1,2,2048,704]{2,3,1,0:T(8,128)(2,1)} %param.30), kind=kOutput, calls=%fused_computation.34 | convolution fusion | flops 5905580032 | bytes 15728640 | tf_op jit(solution)/shard_map/rd,gdf->grf/dot_general | solution.py:234
  313.7 6.3 convolution_convert_fusion
  320.6 3.7 fusion.99
  324.4 5.9 fusion.34
  333.0 7.3 fusion.27
  345.0 12.3 %bitcast_convert_fusion = bf16[16,64,2048]{2,1,0:T(8,128)(2,1)} fusion(bf16[16,64,704,2]{2,1,0,3:T(8,128)(2,1)} %bitcast.216, bf16[1,2,2048,704]{2,3,1,0:T(8,128)(2,1)} %param.30), kind=kOutput, calls=%fused_computation.4 | convolution fusion | flops 5907677184 | bytes 12845056 | tf_op jit(solution)/shard_map/grf,gdf->rd/dot_general | solution.py:283
  357.3 6.4 all-to-all-start.1
  363.8 12.9 %reduce-scatter.20.cloned.1.call-done = f32[256,2,704]{0,2,1:T(8,128)} async-done(((f32[512,2,704]{0,2,1:T(8,128)}), f32[256,2,704]{0,2,1:T(8,128)}) %reduce-scatter.20.cloned.1.call-update) | async-done | bytes 1441808 | tf_op jit(solution)/shard_map/reduce_scatter | solution.py:72
  379.4 13.5 %reduce-scatter.26.cloned.1.call-done = bf16[16,64,1024]{2,1,0:T(8,128)(2,1)} async-done(((bf16[16,64,2048]{2,1,0:T(8,128)(2,1)}), bf16[16,64,1024]{2,1,0:T(8,128)(2,1)}) %reduce-scatter.26.cloned.1.call-update) | async-done | bytes 2097168 | tf_op jit(solution)/shard_map/reduce_scatter | solution.py:92
  392.9 17.5 %all-to-all-done.1 = bf16[16,64,1024]{2,1,0:T(8,128)(2,1)S(1)} async-done(((bf16[16,64,1024]{2,1,0:T(8,128)(2,1)}), bf16[16,64,1024]{2,1,0:T(8,128)(2,1)S(1)}, u32[]{:S(2)}, u32[]{:S(2)}) %all-to-all-start.1) | async-done | bytes 2097184 | tf_op jit(solution)/shard_map/all_to_all | solution.py:84
  410.3 7.5 all-to-all-start.3
  418.9 14.0 %all-gather.18.cloned.1.call-done = bf16[512,2,704]{0,2,1:T(8,128)(2,1)} async-done(((bf16[256,2,704]{0,2,1:T(8,128)(2,1)}), bf16[512,2,704]{0,2,1:T(8,128)(2,1)}) %all-gather.18.cloned.1.call-update) | async-done | bytes 1441808 | tf_op jit(solution)/shard_map/all_gather | solution.py:66
  432.9 5.0 bitcast_convert_fusion.1
  439.5 3.7 gather_fusion
  443.2 3.9 reshape.329
  447.1 4.8 multiply_reduce_fusion
  451.9 3.7 psum.157
  455.7 24.5 %all-to-all-done.3 = bf16[16,64,1024]{2,1,0:T(8,128)(2,1)} async-done(((bf16[16,64,1024]{2,1,0:T(8,128)(2,1)}), bf16[16,64,1024]{2,1,0:T(8,128)(2,1)}, u32[]{:S(2)}, u32[]{:S(2)}) %all-to-all-start.3) | async-done | bytes 2097184 | tf_op jit(solution)/shard_map/all_to_all | solution.py:84
  480.2 5.7 gather_fusion.1
  488.1 3.6 reduce_sum.193
  497.4 29.1 %all-gather.20.cloned.1.call-done = bf16[512,1024]{1,0:T(8,128)(2,1)} async-done(((bf16[128,1024]{1,0:T(8,128)(2,1)}), bf16[512,1024]{1,0:T(8,128)(2,1)}) %all-gather.20.cloned.1.call-update) | async-done | bytes 1048592 | tf_op jit(solution)/shard_map/all_gather | solution.py:60
  529.8 9.1 %reduce-scatter.32.cloned.1.call-done = f32[256,512]{1,0:T(8,128)} async-done(((f32[512,512]{1,0:T(8,128)}), f32[256,512]{1,0:T(8,128)}) %reduce-scatter.32.cloned.1.call-update) | async-done | bytes 524304 | tf_op jit(solution)/shard_map/reduce_scatter | solution.py:72
  556.0 11.9 %reduce-scatter.34.cloned.1.call-done = f32[256,768]{0,1:T(8,128)} async-done(((f32[512,768]{0,1:T(8,128)}), f32[256,768]{0,1:T(8,128)}) %reduce-scatter.34.cloned.1.call-update) | async-done | bytes 786448 | tf_op jit(solution)/shard_map/reduce_scatter | solution.py:72
  575.9 4.0 fusion.101
  580.0 28.1 %all-reduce.8.cloned.1.call-done = bf16[256,576]{0,1:T(8,128)(2,1)} async-done(((bf16[256,576]{0,1:T(8,128)(2,1)}), bf16[256,576]{0,1:T(8,128)(2,1)}) %all-reduce.8.cloned.1.call-update) | async-done | bytes 294928 | tf_op jit(solution)/shard_map/psum | solution.py:56
  609.8 3.7 all_gather.55
  620.7 3.4 convolution_convert_fusion.2
  633.8 5.9 reduce-scatter.38.cloned.1.call-done
  640.9 9.7 %all-reduce.11 = (f32[128]{0:T(128)S(1)}, bf16[512]{0:T(512)(128)(2,1)S(1)}, bf16[512,1024]{1,0:T(8,128)(2,1)}) all-reduce(f32[128]{0:T(128)S(1)} %get-tuple-element.78, f32[512]{0:T(512)S(1)} %get-tuple-element.62, f32[512,1024]{1,0:T(8,128)S(1)} %fusion.91), channel_id=1, replica_groups=mesh['dp'=4,'row'=4,'col'=2] {'col'}, use_global_device_ids=true, to_apply=%region_42.43 | all-reduce | flops 524928 | bytes 3149824 | tf_op jit(solution)/shard_map/psum | solution.py:52
  652.0 7.3 convolution_bitcast_fusion.1
  659.4 8.9 %convolution_bitcast_fusion = f32[1,2,2048,704]{2,3,1,0:T(8,128)} fusion(bf16[1024,2048,1]{1,0,2:T(8,128)(2,1)S(1)} %bitcast.237, bf16[1,1024,704]{1,2,0:T(8,128)(2,1)S(1)} %copy-done.31, bf16[1,1024,704]{1,2,0:T(8,128)(2,1)S(1)} %copy-done.29), kind=kOutput, calls=%fused_computation.9 | convolution fusion | flops 5907021824 | bytes 18612224 | tf_op jit(solution)/shard_map/rd,grf->gdf/dot_general | solution.py:280
  668.4 13.2 %all-reduce.1 = (bf16[1024]{0:T(1024)(128)(2,1)S(1)}, bf16[1024]{0:T(1024)(128)(2,1)S(1)}, bf16[1024,16]{0,1:T(8,128)(2,1)S(1)}) all-reduce(bf16[1024]{0:T(1024)(128)(2,1)S(1)} %get-tuple-element.77, bf16[1024]{0:T(1024)(128)(2,1)S(1)} %get-tuple-element.64, ...), channel_id=1, replica_groups=mesh['dp'=4,'row'=4,'col'=2] {'row'}, use_global_device_ids=true, to_apply=%region_44.45 | all-reduce | flops 18432 | bytes 73728 | tf_op jit(solution)/shard_map/psum | solution.py:56
  681.6 14.5 %all-reduce.2 = (bf16[1024]{0:T(1024)(128)(2,1)S(1)}, bf16[512]{0:T(512)(128)(2,1)S(1)}, bf16[1024]{0:T(1024)(128)(2,1)S(1)}, bf16[1024,16]{0,1:T(8,128)(2,1)S(1)}) all-reduce(bf16[1024]{0:T(1024)(128)(2,1)S(1)} %get-tuple-element.82, bf16[512]{0:T(512)(128)(2,1)S(1)} %get-tuple-element.80, ...), channel_id=1, replica_groups=mesh['dp'=4,'row'=4,'col'=2] {'dp'}, use_global_device_ids=true, to_apply=%region_45.46 | all-reduce | flops 18944 | bytes 75776 | tf_op jit(solution)/shard_map/psum | solution.py:440
  700.9 148.6 %all-reduce.10.cloned.1.call-done = (bf16[1024,768]{1,0:T(8,128)(2,1)}, bf16[1024,144]{0,1:T(8,128)(2,1)}, bf16[512,1024]{1,0:T(8,128)(2,1)}, bf16[512,1024]{1,0...) async-done(((bf16[1024,768]{1,0:T(8,128)(2,1)}, bf16[1024,144]{0,1:T(8,128)(2,1)}, bf16[512,1024]{1,0:T(8,128)(2,1)}, bf16[512,1024]{1,0:T(8,128)(2,1)}, ...) | async-done | bytes 8290320 | tf_op jit(solution)/shard_map/psum | solution.py:441
  (376 shorter events, 158.2 us)
Async XLA Ops:
  7.2 306.5 %copy-start = (bf16[1,704,2048]{2,1,0:T(8,128)(2,1)S(1)}, bf16[1,704,2048]{2,1,0:T(8,128)(2,1)}, u32[]{:S(2)}) copy-start(bf16[1,704,2048]{2,1,0:T(8,128)(2,1)} %param.31) | copy-start | bytes 8650756
  7.2 34.6 %all-gather.8.cloned.1.call-start = ((), (), s32[]{:S(2)}) async-start(), calls=%async_computation.17 | async-start | bytes 1310720 | tf_op jit(solution)/shard_map/all_gather | solution.py:60
  11.3 36.9 %copy-start.97 = (f32[128]{0:T(128)}, f32[128]{0:T(128)S(1)}, u32[]{:S(2)}) copy-start(f32[128]{0:T(128)S(1)} %psum.154) | copy-start | bytes 1540
  11.3 33.0 %copy-start.88 = (f32[128]{0:T(128)}, f32[128]{0:T(128)S(1)}, u32[]{:S(2)}) copy-start(f32[128]{0:T(128)S(1)} %add_rsqrt_fusion.2) | copy-start | bytes 1540
  13.1 39.6 %reduce-scatter.14.cloned.1.call-start = ((), (), s32[]{:S(2)}) async-start(), calls=%async_computation.18 | async-start | bytes 442368 | tf_op jit(solution)/shard_map/reduce_scatter | solution.py:72
  44.3 44.5 %reduce-scatter.16.cloned.1.call-start = ((), (), s32[]{:S(2)}) async-start(), calls=%async_computation.19 | async-start | bytes 2359296 | tf_op jit(solution)/shard_map/reduce_scatter | solution.py:72
  48.2 79.9 %reduce-scatter.18.cloned.1.call-start = ((), (), s32[]{:S(2)}) async-start(), calls=%async_computation.20 | async-start | bytes 1310720 | tf_op jit(solution)/shard_map/reduce_scatter | solution.py:77
  48.6 43.6 %copy-start.43 = (f32[256,32]{0,1:T(8,128)}, f32[256,32]{0,1:T(8,128)S(1)}, u32[]{:S(2)}) copy-start(f32[256,32]{0,1:T(8,128)S(1)} %get-tuple-element.113) | copy-start | bytes 98308
  102.3 194.7 %all-gather.12.cloned.1.call-start = ((), (), s32[]{:S(2)}) async-start(), calls=%async_computation.24 | async-start | bytes 6291456 | tf_op jit(solution)/shard_map/all_gather | solution.py:88
  226.3 70.7 %all-to-all-start.2 = ((bf16[16,64,1024]{2,1,0:T(8,128)(2,1)}), bf16[16,64,1024]{2,1,0:T(8,128)(2,1)}, u32[]{:S(2)}, u32[]{:S(2)}) async-start(bf16[16,64,1024]{2,1,0:T(8,128)(2,1)} %bitcast.212), calls=%async_computation.8 | async-start | bytes 4194304 | tf_op jit(solution)/shard_map/all_to_all | solution.py:84
  233.5 87.0 %all-gather.16.cloned.1.call-start = ((), (), s32[]{:S(2)}) async-start(), calls=%async_computation.28 | async-start | bytes 1310720 | tf_op jit(solution)/shard_map/all_gather | solution.py:60
  234.1 90.3 %all-gather.10.cloned.1.call-start = ((), (), s32[]{:S(2)}) async-start(), calls=%async_computation.21 | async-start | bytes 1310720 | tf_op jit(solution)/shard_map/all_gather | solution.py:60
  234.8 98.2 %all-gather.14.cloned.1.call-start = ((), (), s32[]{:S(2)}) async-start(), calls=%async_computation.26 | async-start | bytes 6291456 | tf_op jit(solution)/shard_map/all_gather | solution.py:88
  297.0 60.4 %reduce-scatter.24.cloned.1.call-start = ((), (), s32[]{:S(2)}) async-start(), calls=%async_computation.25 | async-start | bytes 6291456 | tf_op jit(solution)/shard_map/reduce_scatter | solution.py:92
  320.1 43.7 %reduce-scatter.28.cloned.1.call-start = ((), (), s32[]{:S(2)}) async-start(), calls=%async_computation.29 | async-start | bytes 2162688 | tf_op jit(solution)/shard_map/reduce_scatter | solution.py:72
  324.3 52.4 %reduce-scatter.20.cloned.1.call-start = ((), (), s32[]{:S(2)}) async-start(), calls=%async_computation.22 | async-start | bytes 4325376 | tf_op jit(solution)/shard_map/reduce_scatter | solution.py:72
  330.3 62.5 %reduce-scatter.26.cloned.1.call-start = ((), (), s32[]{:S(2)}) async-start(), calls=%async_computation.27 | async-start | bytes 6291456 | tf_op jit(solution)/shard_map/reduce_scatter | solution.py:92
  357.3 53.0 %all-to-all-start.1 = ((bf16[16,64,1024]{2,1,0:T(8,128)(2,1)}), bf16[16,64,1024]{2,1,0:T(8,128)(2,1)S(1)}, u32[]{:S(2)}, u32[]{:S(2)}) async-start(bf16[16,64,1024]{2,1,0:T(8,128)(2,1)} %reduce-scatter.24.cloned.1.call-done), calls=%async_computation.7 | async-start | bytes 4194304 | tf_op jit(solution)/shard_map/all_to_all | solution.py:84
  410.3 69.8 %all-to-all-start.3 = ((bf16[16,64,1024]{2,1,0:T(8,128)(2,1)}), bf16[16,64,1024]{2,1,0:T(8,128)(2,1)}, u32[]{:S(2)}, u32[]{:S(2)}) async-start(bf16[16,64,1024]{2,1,0:T(8,128)(2,1)} %reduce-scatter.26.cloned.1.call-done), calls=%async_computation.10 | async-start | bytes 4194304 | tf_op jit(solution)/shard_map/all_to_all | solution.py:84
  417.8 15.1 %all-gather.18.cloned.1.call-start = ((), (), s32[]{:S(2)}) async-start(), calls=%async_computation.30 | async-start | bytes 2162688 | tf_op jit(solution)/shard_map/all_gather | solution.py:66
  418.8 73.0 %reduce-scatter.30.cloned.1.call-start = ((), (), s32[]{:S(2)}) async-start(), calls=%async_computation.31 | async-start | bytes 1310720 | tf_op jit(solution)/shard_map/reduce_scatter | solution.py:77
  437.9 88.5 %all-gather.20.cloned.1.call-start = ((), (), s32[]{:S(2)}) async-start(), calls=%async_computation.32 | async-start | bytes 1310720 | tf_op jit(solution)/shard_map/all_gather | solution.py:60
  447.1 33.1 %copy-start.62 = (s32[1024]{0:T(1024)S(1)}, s32[1024]{0:T(1024)}, u32[]{:S(2)}) copy-start(s32[1024]{0:T(1024)} %pad_clamp_fusion) | copy-start | bytes 12292
  491.8 38.0 %copy-start.53 = (f32[128,16]{0,1:T(8,128)}, f32[128,16]{0,1:T(8,128)S(1)}, u32[]{:S(2)}) copy-start(f32[128,16]{0,1:T(8,128)S(1)} %select_reduce_fusion.1) | copy-start | bytes 24580
  491.8 37.9 %copy-start.83 = (f32[128]{0:T(128)}, f32[128]{0:T(128)S(1)}, u32[]{:S(2)}) copy-start(f32[128]{0:T(128)S(1)} %multiply_reduce_fusion.9) | copy-start | bytes 1540
  496.3 33.4 %copy-start.90 = (f32[128]{0:T(128)}, f32[128]{0:T(128)S(1)}, u32[]{:S(2)}) copy-start(f32[128]{0:T(128)S(1)} %fusion.82) | copy-start | bytes 1540
  497.3 32.6 %copy-start.68 = (f32[4,256]{1,0:T(4,128)S(1)}, f32[4,256]{1,0:T(4,128)}, u32[]{:S(2)}) copy-start(f32[4,256]{1,0:T(4,128)} %copy-done.67) | copy-start | bytes 12292
  497.3 45.2 %copy-start.3 = (f32[4,256,512]{2,1,0:T(8,128)S(1)}, f32[4,256,512]{2,1,0:T(8,128)}, u32[]{:S(2)}) copy-start(f32[4,256,512]{2,1,0:T(8,128)} %copy-done.2) | copy-start | bytes 6291460
  497.3 45.2 %copy-start.17 = (pred[256,512]{1,0:T(8,128)(4,1)S(1)}, pred[256,512]{1,0:T(8,128)(4,1)}, u32[]{:S(2)}) copy-start(pred[256,512]{1,0:T(8,128)(4,1)} %broadcast_compare_fusion) | copy-start | bytes 393220
  497.3 41.6 %reduce-scatter.32.cloned.1.call-start = ((), (), s32[]{:S(2)}) async-start(), calls=%async_computation.33 | async-start | bytes 1572864 | tf_op jit(solution)/shard_map/reduce_scatter | solution.py:72
  529.8 25.2 %reduce-scatter.36.cloned.1.call-start = ((), (), s32[]{:S(2)}) async-start(), calls=%async_computation.35 | async-start | bytes 1572864 | tf_op jit(solution)/shard_map/reduce_scatter | solution.py:72
  545.1 22.9 %reduce-scatter.34.cloned.1.call-start = ((), (), s32[]{:S(2)}) async-start(), calls=%async_computation.34 | async-start | bytes 2359296 | tf_op jit(solution)/shard_map/reduce_scatter | solution.py:72
  550.4 57.6 %all-reduce.8.cloned.1.call-start = ((), (), s32[]{:S(2)}) async-start(), calls=%async_computation.36 | async-start | bytes 589824 | tf_op jit(solution)/shard_map/psum | solution.py:56
  573.2 66.5 %reduce-scatter.38.cloned.1.call-start = ((), (), s32[]{:S(2)}) async-start(), calls=%async_computation.37 | async-start | bytes 1310720 | tf_op jit(solution)/shard_map/reduce_scatter | solution.py:77
  575.9 33.3 %copy-start.64 = (f32[512]{0:T(512)S(1)}, f32[512]{0:T(512)}, u32[]{:S(2)}) copy-start(f32[512]{0:T(512)} %param.23) | copy-start | bytes 6148
  575.9 33.3 %copy-start.66 = (f32[256]{0:T(256)S(1)}, f32[256]{0:T(256)}, u32[]{:S(2)}) copy-start(f32[256]{0:T(256)} %copy-done.65) | copy-start | bytes 3076
  575.9 33.6 %copy-start.75 = (f32[256]{0:T(256)S(1)}, f32[256]{0:T(256)}, u32[]{:S(2)}) copy-start(f32[256]{0:T(256)} %copy-done.74) | copy-start | bytes 3076
  580.0 33.5 %copy-start.32 = (bf16[1024,144]{0,1:T(8,128)(2,1)S(1)}, bf16[1024,144]{0,1:T(8,128)(2,1)}, u32[]{:S(2)}) copy-start(bf16[1024,144]{0,1:T(8,128)(2,1)} %param.22) | copy-start | bytes 884740
  614.9 83.7 %reduce-scatter.22.cloned.1.call-start = ((), (), s32[]{:S(2)}) async-start(), calls=%async_computation.23 | async-start | bytes 1310720 | tf_op jit(solution)/shard_map/reduce_scatter | solution.py:77
  620.7 228.8 %all-reduce.10.cloned.1.call-start = ((), (), s32[]{:S(2)}) async-start(), calls=%async_computation.38 | async-start | bytes 16580608 | tf_op jit(solution)/shard_map/psum | solution.py:441
  659.3 39.3 %copy-start.98 = (f32[128]{0:T(128)S(1)}, f32[128]{0:T(128)}, u32[]{:S(2)}) copy-start(f32[128]{0:T(128)} %copy-done.97) | copy-start | bytes 1540
  659.3 39.3 %copy-start.10 = (bf16[128,1024]{1,0:T(8,128)(2,1)S(1)}, bf16[128,1024]{1,0:T(8,128)(2,1)}, u32[]{:S(2)}) copy-start(bf16[128,1024]{1,0:T(8,128)(2,1)} %reduce-scatter.18.cloned.1.call-done) | copy-start | bytes 786436
  659.3 39.3 %copy-start.14 = (f32[128,1024]{1,0:T(8,128)S(1)}, f32[128,1024]{1,0:T(8,128)}, u32[]{:S(2)}) copy-start(f32[128,1024]{1,0:T(8,128)} %copy-done.13) | copy-start | bytes 1572868
  659.3 39.3 %copy-start.25 = (f32[128,1024]{1,0:T(8,128)S(1)}, f32[128,1024]{1,0:T(8,128)}, u32[]{:S(2)}) copy-start(f32[128,1024]{1,0:T(8,128)} %get-tuple-element.61) | copy-start | bytes 1572868
  659.3 39.3 %copy-start.38 = (bf16[128,1024]{1,0:T(8,128)(2,1)S(1)}, bf16[128,1024]{1,0:T(8,128)(2,1)}, u32[]{:S(2)}) copy-start(bf16[128,1024]{1,0:T(8,128)(2,1)} %reduce-scatter.38.cloned.1.call-done) | copy-start | bytes 786436
  659.3 39.3 %copy-start.57 = (f32[1024]{0:T(1024)S(1)}, f32[1024]{0:T(1024)}, u32[]{:S(2)}) copy-start(f32[1024]{0:T(1024)} %param.26) | copy-start | bytes 12292
  659.3 39.3 %copy-start.80 = (f32[128]{0:T(128)S(1)}, f32[128]{0:T(128)}, u32[]{:S(2)}) copy-start(f32[128]{0:T(128)} %copy-done.78) | copy-start | bytes 1540
  659.4 39.3 %copy-start.91 = (f32[128]{0:T(128)S(1)}, f32[128]{0:T(128)}, u32[]{:S(2)}) copy-start(f32[128]{0:T(128)} %copy-done.90) | copy-start | bytes 1540
  (79 other events, 502.9 us)
Sparse Core Ops, SparseCore 0:
  13.2 28.4 all-gather.7
  44.6 8.1 reduce-scatter.13
  55.6 10.2 reduce-scatter.15
  102.4 25.6 reduce-scatter.17
  201.1 15.7 all-gather.11
  235.6 52.7 all-gather.15
  290.5 26.7 all-gather.9
  318.9 14.1 all-gather.13
  335.9 13.2 reduce-scatter.23
  351.9 10.2 reduce-scatter.27
  365.0 11.6 reduce-scatter.19
  379.5 13.2 reduce-scatter.25
  420.8 12.0 all-gather.17
  438.1 39.9 reduce-scatter.29
  497.4 29.0 all-gather.19
  529.9 8.9 reduce-scatter.31
  545.2 9.6 reduce-scatter.35
  557.7 10.1 reduce-scatter.33
  573.3 34.6 all-reduce.7
  615.1 24.6 reduce-scatter.37
  642.7 25.8 reduce-scatter.21
  674.2 175.2 all-reduce.9
where the time goes:
time: 884 us; the launch traced here: 871 us
  waiting for transfers between devices  435 us (49%)
  blocking collectives  141 us (16%)
  matrix products  114 us (13%)
  local copies, waits for them, and re-layouts  74.7 us (8%)
  other arithmetic  68.9 us (8%)
  starting transfers between devices  22.6 us (3%)
  between operations  16 us (2%)
    psum x1, waiting for transfers between devices, local(): lax.psum(queries_part.astype(jnp.bfloat16), 'dp').astype(jnp.float32)  149 us
    all_to_all x3, waiting for transfers between devices, expert_exchange(): lax.all_to_all(values, ('dp', 'row'), split_axis=0, concat_axis=0, tiled=...  104 us
    all_gather x4, waiting for transfers between devices, row_gather(): return (lax.all_gather(values[0], 'row', axis=0, tiled=True),)  57.8 us
    all_to_all x1, blocking collectives, expert_exchange(): lax.all_to_all(values, ('dp', 'row'), split_axis=0, concat_axis=0, tiled=...  52.6 us
    reduce_scatter x7, waiting for transfers between devices, col_scatter(): return lax.psum_scatter(values, 'col', scatter_dimension=0, tiled=True)  39.2 us
    psum x1, waiting for transfers between devices, row_totals(): lax.psum(for_sending(values), 'row')  28.1 us
    psum x6, blocking collectives, col_totals(): return lax.psum(values, 'col')  26.3 us
    reduce_scatter x4, waiting for transfers between devices, row_scatter(): lax.psum_scatter(values[0].astype(jnp.bfloat16), 'row', scatter_dimension...  25.5 us
  transfers between devices with their start and end apart: 25, of which 17 were waited for; matrix products, arithmetic and copies ran while one was open for 20% of the time, Pallas kernels for 0%

commit v1 on v0

v1 whole, which is shorter than its diff:
```python
import jax
import jax.numpy as jnp
import numpy as np
from jax import lax
from jax.experimental import pallas as pl
from jax.experimental.pallas import tpu as pltpu
from jax.sharding import PartitionSpec as P

D = 2048
NOPE = 128
ROPE = 64
HEADV = 128
RANK = 512
TOP = 6


epsilon = 1e-06
masked_score = -1e30
f32 = jnp.float32
bf16 = jnp.bfloat16


def after(value, *earlier):
    return lax.optimization_barrier((value,) + earlier)[0]


def silu_slope(values):
    sigmoid = jax.nn.sigmoid(values)
    return sigmoid * (1.0 + values * (1.0 - sigmoid))


def rotation(positions, rope_width):
    half_width = rope_width // 2
    frequency = 10000.0 ** (-jnp.arange(half_width, dtype=jnp.float32) * 2.0 / rope_width)
    angles = positions.astype(jnp.float32)[:, None] * frequency[None, :]
    return (jnp.cos(angles), jnp.sin(angles))


def rotate(values, cosine, sine_table, direction):
    half_width = values.shape[-1] // 2
    first_half = values[..., :half_width]
    second_half = values[..., half_width:]
    return jnp.concatenate(
        [
            first_half * cosine - direction * second_half * sine_table,
            second_half * cosine + direction * first_half * sine_table,
        ],
        axis=-1,
    )


def dot(left, right):
    return jnp.dot(left, right, preferred_element_type=f32)


def dot_tn(left, right):
    return lax.dot_general(left, right, (((0,), (0,)), ((), ())), preferred_element_type=f32)


def dot_nt(left, right):
    return lax.dot_general(left, right, (((1,), (1,)), ((), ())), preferred_element_type=f32)


def col_totals(values):
    return lax.psum(values, "col")


def row_gather(values):
    return lax.all_gather(values, "row", axis=0, tiled=True)


def col_gather(values, axis=0):
    return lax.all_gather(values, "col", axis=axis, tiled=True)


def col_scatter(values, axis=0):
    return lax.psum_scatter(values, "col", scatter_dimension=axis, tiled=True)


def row_scatter(values):
    return lax.psum_scatter(
        values.astype(bf16), "row", scatter_dimension=0, tiled=True
    ).astype(f32)


def send_out(parts):
    count = len(parts)
    return [parts[0]] + [
        lax.ppermute(parts[k], "dp", [(i, (i + k) % count) for i in range(count)])
        for k in range(1, count)
    ]


def send_back(parts):
    count = len(parts)
    return [parts[0]] + [
        lax.ppermute(parts[k], "dp", [(i, (i - k) % count) for i in range(count)])
        for k in range(1, count)
    ]


def norm_scale(values):
    square_sum = col_totals(jnp.sum(values * values, axis=1))
    return lax.rsqrt(square_sum / D + epsilon)


def norm_back(values, row_scale, gain_vector, upstream):
    weighted = upstream * gain_vector
    inner_mean = col_totals(jnp.sum(weighted * values, axis=1)) / D
    return weighted * row_scale[:, None] - values * (row_scale**3 * inner_mean)[:, None]


MESH = pl.DeviceIdType.MESH
VMEM = pltpu.VMEM
DMA = pltpu.SemaphoreType.DMA
MIB = 1024 * 1024
ROWS = 4
SQUARE = 4
COLS = 2
SPLIT = 2


def nn(left, right):
    return lax.dot_general(left, right, (((1,), (0,)), ((), ())), preferred_element_type=f32)


def tn(left, right):
    return lax.dot_general(left, right, (((0,), (0,)), ((), ())), preferred_element_type=f32)


def nt(left, right):
    return lax.dot_general(left, right, (((1,), (1,)), ((), ())), preferred_element_type=f32)


def block_at(row, turn):
    swapped = jnp.where(turn < 2, 1 - turn, turn)
    inner = jnp.logical_or(row == 1, row == 2)
    near = jnp.where(inner, swapped, turn)
    return jnp.where(row < 2, near, ROWS - 1 - near)


def partner(place, step):
    across, along = lax.rem(place, 2), lax.div(place, 2)
    across = lax.rem(across + step % 2, 2)
    along = lax.rem(along + step // 2, 2)
    return along * 2 + across


def remote(source, target, sent, arrived, where):
    return pltpu.make_async_remote_copy(
        src_ref=source,
        dst_ref=target,
        send_sem=sent,
        recv_sem=arrived,
        device_id=where,
        device_id_type=MESH,
    )


def greet(row, place, col, square=True):
    barrier = pltpu.get_barrier_semaphore()
    if square:

        @pl.when(row > 0)
        def _():
            pl.semaphore_signal(barrier, inc=1, device_id={"row": row - 1}, device_id_type=MESH)

        @pl.when(row < ROWS - 1)
        def _():
            pl.semaphore_signal(barrier, inc=1, device_id={"row": row + 1}, device_id_type=MESH)

        for step in range(1, SQUARE):
            pl.semaphore_signal(
                barrier, inc=1, device_id={"dp": partner(place, step)}, device_id_type=MESH
            )
        met = (
            SQUARE - 1 + (row > 0).astype(jnp.int32) + (row < ROWS - 1).astype(jnp.int32)
        )
    else:
        for step in range(1, ROWS):
            pl.semaphore_signal(
                barrier,
                inc=1,
                device_id={"row": lax.rem(row + step, ROWS)},
                device_id_type=MESH,
            )
        met = ROWS - 1
    pl.semaphore_signal(barrier, inc=1, device_id={"col": 1 - col}, device_id_type=MESH)
    pl.semaphore_wait(barrier, met + 1)


class Line:
    def __init__(self, row, buffer, sent, arrived):
        self.row, self.buffer, self.sent, self.arrived = row, buffer, sent, arrived

    def copy(self, block, way):
        to = self.row + 1 if way == 0 else self.row - 1
        here = self.buffer.at[block]
        return remote(here, here, self.sent.at[block, way], self.arrived.at[block], {"row": to})

    def each(self, block, act):
        @pl.when(jnp.logical_and(block <= self.row, self.row < ROWS - 1))
        def _():
            act(self.copy(block, 0))

        @pl.when(jnp.logical_and(block >= self.row, self.row > 0))
        def _():
            act(self.copy(block, 1))

    def wait(self, block):
        self.copy(block, 0).wait_recv()

    def pass_on(self, block):
        self.each(block, lambda copy: copy.start())

    def finish(self):
        def one(block, carried):
            self.each(block, lambda copy: copy.wait_send())
            return carried

        lax.fori_loop(0, ROWS, one, 0)


class SumLine:
    def __init__(self, row, part, leaving, coming, sent, arrived):
        self.row, self.part, self.leaving, self.coming = row, part, leaving, coming
        self.sent, self.arrived = sent, arrived
        self.lines = part.shape[1] // SPLIT

    def piece(self, index):
        return pl.ds(index * self.lines, self.lines)

    def copy(self, block, index, way):
        return remote(
            self.leaving.at[block, self.piece(index)],
            self.coming.at[way, block, self.piece(index)],
            self.sent.at[block, index],
            self.arrived.at[way, block, index],
            {"row": self.row + 1 - 2 * way},
        )

    def send(self, block, index):
        @pl.when(block > self.row)
        def _():
            self.copy(block, index, 0).start()

        @pl.when(block < self.row)
        def _():
            self.copy(block, index, 1).start()

    def chained(self, block):
        return jnp.logical_or(
            jnp.logical_and(block > self.row, self.row > 0),
            jnp.logical_and(block < self.row, self.row < ROWS - 1),
        )

    def begin(self, block):
        @pl.when(jnp.logical_and(block != self.row, jnp.logical_not(self.chained(block))))
        def _():
            self.leaving[block] = self.part[block].astype(bf16)
            for index in range(SPLIT):
                self.send(block, index)

    def pass_on(self, block):
        @pl.when(self.chained(block))
        def _():
            way = (block < self.row).astype(jnp.int32)
            for index in range(SPLIT):
                self.copy(block, index, way).wait_recv()
                piece = self.piece(index)
                self.leaving[block, piece] = (
                    self.part[block, piece] + self.coming[way, block, piece].astype(f32)
                ).astype(bf16)
                self.send(block, index)

    def total(self, target):
        target[...] = self.part[self.row]
        for way, there in ((0, self.row > 0), (1, self.row < ROWS - 1)):

            @pl.when(there)
            def _(way=way):
                for index in range(SPLIT):
                    self.copy(self.row, index, way).wait_recv()
                    target[self.piece(index)] += self.coming[
                        way, self.row, self.piece(index)
                    ].astype(f32)

    def finish(self):
        def one(block, carried):
            @pl.when(block != self.row)
            def _():
                for index in range(SPLIT):
                    self.copy(block, index, 0).wait_send()

            return carried

        lax.fori_loop(0, ROWS, one, 0)


def swap_halves(values):
    lanes = values.shape[1]
    lane = lax.broadcasted_iota(jnp.int32, values.shape, 1)
    return jnp.where(
        lane % ROPE < ROPE // 2,
        pltpu.roll(values, lanes - ROPE // 2, 1),
        pltpu.roll(values, ROPE // 2, 1),
    )


def attend_kernel(
    act_ref,
    scaling_ref,
    compress_ref,
    rescale_ref,
    premix_ref,
    cos_ref,
    sin_ref,
    key_cos_ref,
    key_sin_ref,
    mark_rows_ref,
    mark_ref,
    cot_ref,
    route_ref,
    queries_ref,
    expand_ref,
    combine_ref,
    one_ref,
    query_ref,
    key_ref,
    value_ref,
    probs_ref,
    latent_ref,
    normed_latent_ref,
    attended_ref,
    compress_all,
    residual_ref,
    two_ref,
    scale_one_ref,
    scale_two_ref,
    cot_all,
    pick_ref,
    back_ref,
    rows_ref,
    queries,
    expand,
    combine,
    stat_to,
    stat_from,
    query_own,
    query_to,
    query_from,
    latent_to,
    latent_from,
    part,
    leaving,
    coming,
    routes,
    staged,
    load_sem,
    stat_sent,
    stat_arrived,
    line_sent,
    line_arrived,
    comp_sent,
    comp_arrived,
    comp_out_sent,
    comp_out_arrived,
    query_sent,
    query_arrived,
    latent_sent,
    latent_arrived,
    att_sent,
    att_arrived,
    sum_sent,
    sum_arrived,
    cot_sent,
    cot_arrived,
    route_sent,
    route_arrived,
    out_sent,
    out_arrived,
    pair_sent,
    pair_arrived,
):
    place, row, col = lax.axis_index("dp"), lax.axis_index("row"), lax.axis_index("col")
    other = 1 - col
    sibling = {"col": other}
    tokens, width = act_ref.shape
    slots = pick_ref.shape[1] // SQUARE
    mine = query_own.shape[2]
    sliced = compress_ref.shape[0]
    quarter = width // SQUARE
    score_scale = (NOPE + ROPE) ** (-0.5)
    loads = [
        pltpu.make_async_copy(source, target, load_sem.at[i])
        for i, (source, target) in enumerate(
            [(queries_ref, queries), (expand_ref, expand), (combine_ref, combine)]
        )
    ]
    for load in loads:
        load.start()

    def stat_copy(index):
        return remote(
            stat_to.at[index],
            stat_from.at[index],
            stat_sent.at[index],
            stat_arrived.at[index],
            sibling,
        )

    def scale_of(values, index):
        own = jnp.sum(values * values, axis=1, keepdims=True)
        stat_to[index] = jnp.broadcast_to(own, (tokens, 128))
        stat_copy(index).start()
        stat_copy(index).wait_recv()
        return lax.rsqrt((own + stat_from[index][:, 0:1]) / D + epsilon)

    def comp_piece(block, member):
        return compress_all.at[
            pl.ds(pl.multiple_of(block * sliced, 16), sliced),
            pl.ds(pl.multiple_of(member * quarter, 128), quarter),
        ]

    def comp_copy(block, way):
        here = comp_piece(block, place)
        return remote(
            here,
            here,
            comp_sent.at[block, way],
            comp_arrived.at[block],
            {"row": row + 1 - 2 * way},
        )

    def comp_each(block, act):
        @pl.when(jnp.logical_and(block <= row, row < ROWS - 1))
        def _():
            act(comp_copy(block, 0))

        @pl.when(jnp.logical_and(block >= row, row > 0))
        def _():
            act(comp_copy(block, 1))

    def comp_out(block, step, member):
        here = comp_piece(block, member)
        return remote(
            here,
            here,
            comp_out_sent.at[block, step],
            comp_out_arrived.at[block, step],
            {"dp": partner(place, step)},
        )

    line = Line(row, one_ref, line_sent, line_arrived)
    cot_line = Line(row, cot_all, cot_sent, cot_arrived)
    route_line = Line(row, routes, route_sent, route_arrived)
    sums = SumLine(row, part, leaving, coming, sum_sent, sum_arrived)

    greet(row, place, col)
    compress_all[pl.ds(pl.multiple_of(row * sliced, 16), sliced)] = compress_ref[...]
    compress_all[ROWS * sliced :] = jnp.zeros(
        (compress_all.shape[0] - ROWS * sliced, width), bf16
    )
    comp_each(row, lambda copy: copy.start())
    inputs = act_ref[...].astype(f32)
    scale_one = scale_of(inputs, 0)
    scale_one_ref[...] = scale_one
    one_ref[pl.ds(row, 1)] = (
        (inputs * scale_one * scaling_ref[...]).astype(bf16).reshape(1, tokens, width)
    )
    cot_all[pl.ds(row, 1)] = cot_ref[...].reshape(1, tokens, width)
    routes[pl.ds(row, 1)] = route_ref[...].reshape((1,) + route_ref.shape)
    line.pass_on(row)
    loads[0].wait()

    def query_copy(block):
        return remote(
            query_to.at[block],
            query_from.at[block],
            query_sent.at[block],
            query_arrived.at[block],
            sibling,
        )

    def latent_copy(block):
        return remote(
            latent_to.at[block],
            latent_from.at[block],
            latent_sent.at[block],
            latent_arrived.at[block],
            sibling,
        )

    def att_copy(block, half):
        here = attended_ref.at[block, :, pl.ds(pl.multiple_of(half * 2 * HEADV, 128), 2 * HEADV)]
        return remote(here, here, att_sent.at[block], att_arrived.at[block], sibling)

    def gather(step, carried):
        block = block_at(row, step)

        @pl.when(step > 0)
        def _():
            comp_copy(block, 0).wait_recv()
            comp_each(block, lambda copy: copy.start())
            for shift in (3, 2, 1):
                comp_out(block, shift, place).start()
            line.wait(block)
            line.pass_on(block)

        tokens_here = one_ref[block]
        query_to[block] = nn(
            tokens_here, queries[:, pl.ds(pl.multiple_of(other * mine, 128), mine)]
        ).astype(bf16)
        query_copy(block).start()
        query_own[block] = nn(tokens_here, queries[:, pl.ds(pl.multiple_of(col * mine, 128), mine)])
        return carried

    lax.fori_loop(0, ROWS, gather, 0)

    cot_line.pass_on(row)
    route_line.pass_on(row)

    def out_copy(block, step):
        piece = pl.ds(step * slots, slots)
        return remote(
            staged.at[block, piece],
            rows_ref.at[col, block, piece],
            out_sent.at[block, step],
            out_arrived.at[block, step],
            {"dp": partner(place, step)},
        )

    def pair_copy(block, half):
        here = rows_ref.at[half, block]
        return remote(here, here, pair_sent.at[block], pair_arrived.at[block], sibling)

    def take(step):
        block = block_at(row, step)

        @pl.when(step > 0)
        def _():
            route_line.wait(block)
            cot_line.wait(block)
            route_line.pass_on(block)
            cot_line.pass_on(block)

        before = (
            lax.broadcasted_iota(jnp.int32, (tokens, tokens), 0)
            < lax.broadcasted_iota(jnp.int32, (tokens, tokens), 1)
        ).astype(bf16)
        routing = routes[block]
        chosen = []
        for shift in range(SQUARE):
            expert = partner(place, shift) * ROWS + row
            hit = (routing[:TOP] == expert).astype(f32)
            chosen.append(jnp.max(hit, axis=0, keepdims=True))
        goes = jnp.concatenate(chosen + chosen, axis=0)
        rank = nn(goes.astype(bf16), before)
        for shift in range(SQUARE):
            slot = lax.broadcasted_iota(jnp.int32, (slots, tokens), 0).astype(f32)
            here = jnp.logical_and(slot == rank[shift : shift + 1], goes[shift : shift + 1] > 0.5)
            pick = here.astype(f32)
            pick_ref[block, shift * slots : (shift + 1) * slots] = pick.astype(bf16)
            back_ref[block, :, shift * slots : (shift + 1) * slots] = pick.T.astype(bf16)
        staged[block] = nn(pick_ref[block], cot_all[block]).astype(bf16)
        for shift in (3, 2, 1):
            out_copy(block, shift).start()
        rows_ref[col, block, 0:slots] = staged[block, 0:slots]

    def forward(step):
        block = block_at(row, step)
        for shift in range(1, SQUARE):
            out_copy(block, shift).wait_recv()
        pair_copy(block, col).start()

    def comp_arrive(block, carried):
        @pl.when(block != row)
        def _():
            for shift in range(1, SQUARE):
                comp_out(block, shift, partner(place, shift)).wait_recv()

        return carried

    lax.fori_loop(0, ROWS, comp_arrive, 0)

    def latents(block, carried):
        value = nt(one_ref[block], compress_all[...])
        latent_to[block] = value
        latent_copy(block).start()
        latent_ref[block] = value
        return carried

    lax.fori_loop(0, ROWS, latents, 0)
    take(0)
    loads[1].wait()

    def keys(block, carried):
        latent_copy(block).wait_recv()
        latent = latent_ref[block] + latent_from[block]
        latent_ref[block] = latent
        plain = latent[:, :RANK]
        scale = lax.rsqrt(jnp.mean(plain * plain, axis=1, keepdims=True) + epsilon)
        normed = (plain * scale * rescale_ref[...]).astype(bf16)
        normed_latent_ref[block] = normed
        own = 2 * (NOPE + HEADV)
        expanded = nn(normed, expand[:, pl.ds(pl.multiple_of(col * own, 128), own)])
        rope = latent[:, RANK:]
        rope = rope * key_cos_ref[block] + swap_halves(rope) * key_sin_ref[block]
        first = jnp.concatenate([expanded[:, :NOPE], rope], axis=1)
        second = jnp.concatenate([expanded[:, 2 * NOPE : 3 * NOPE], rope], axis=1)
        key_ref[0, block] = first.astype(bf16)
        key_ref[1, block] = pltpu.roll(second, ROPE, 1).astype(bf16)
        value_ref[0, block] = expanded[:, NOPE : 2 * NOPE].astype(bf16)
        value_ref[1, block] = expanded[:, 3 * NOPE :].astype(bf16)
        query_copy(block).wait_recv()
        query = query_own[block] + query_from[block].astype(f32)
        query_ref[block] = (
            query * cos_ref[block] + swap_halves(query) * sin_ref[block]
        ).astype(bf16)
        return carried

    lax.fori_loop(0, ROWS, keys, 0)
    seq = ROWS * tokens
    lanes = NOPE + 2 * ROPE

    def attend(turn, carried):
        block = block_at(row, ROWS - 1 - turn)
        visible = mark_ref[...] <= mark_rows_ref[block]
        for head in range(2):
            query = query_ref[block, :, head * NOPE : head * NOPE + lanes]
            scores = nt(query, key_ref[head].reshape(seq, lanes)) * score_scale
            scores = jnp.where(visible, scores, masked_score)
            weight = jnp.exp(scores - jnp.max(scores, axis=1, keepdims=True))
            probs = (weight / jnp.sum(weight, axis=1, keepdims=True)).astype(bf16)
            probs_ref[head, block] = probs
            result = nn(probs, value_ref[head].reshape(seq, HEADV)).astype(bf16)
            at = pl.multiple_of((col * 2 + head) * HEADV, 128)
            attended_ref[block, :, pl.ds(at, HEADV)] = result
        att_copy(block, col).start()

        @pl.when(jnp.logical_or(turn == 1, turn == 2))
        def _():
            take(turn)

        return carried

    lax.fori_loop(0, ROWS, attend, 0)
    loads[2].wait()

    def mix(turn, carried):
        block = block_at(row, ROWS - 1 - turn)
        att_copy(block, other).wait_recv()
        part[block] = nn(attended_ref[block], combine[...])
        sums.begin(block)
        return carried

    lax.fori_loop(0, ROWS, mix, 0)

    def hand_on(turn, carried):
        sums.pass_on(block_at(row, jnp.where(turn == 0, 3, turn)))

        @pl.when(turn == 0)
        def _():
            take(3)

        forward(turn)
        return carried

    lax.fori_loop(0, 3, hand_on, 0)
    sums.total(residual_ref)
    residual = residual_ref[...] + inputs
    residual_ref[...] = residual
    scale_two = scale_of(residual, 1)
    scale_two_ref[...] = scale_two
    two_ref[...] = (residual * scale_two * premix_ref[...]).astype(bf16)
    forward(3)

    def ended(block, carried):
        pair_copy(block, other).wait_recv()
        pair_copy(block, col).wait_send()
        for shift in range(1, SQUARE):
            out_copy(block, shift).wait_send()

            @pl.when(block != row)
            def _(shift=shift):
                comp_out(block, shift, place).wait_send()

        comp_each(block, lambda copy: copy.wait_send())
        query_copy(block).wait_send()
        latent_copy(block).wait_send()
        att_copy(block, col).wait_send()
        return carried

    lax.fori_loop(0, ROWS, ended, 0)
    stat_copy(0).wait_send()
    stat_copy(1).wait_send()
    sums.finish()
    line.finish()
    cot_line.finish()
    route_line.finish()


def turning_tables(length):
    half = ROPE // 2
    frequency = 10000.0 ** (-np.arange(half, dtype=np.float32) * 2.0 / ROPE)
    angles = np.arange(length, dtype=np.float32)[:, None] * frequency[None, :].astype(np.float32)
    cosine, sine = np.cos(angles), np.sin(angles)
    cosine, sine = np.concatenate([cosine, cosine], 1), np.concatenate([-sine, sine], 1)
    ones, zeros = np.ones((length, NOPE)), np.zeros((length, NOPE))
    gap = np.zeros((length, 128 - ROPE))
    tables = (
        np.concatenate([ones, cosine, ones, cosine], 1),
        np.concatenate([zeros, sine, zeros, sine], 1),
        np.concatenate([cosine, gap], 1),
        np.concatenate([sine, gap], 1),
    )
    return [
        jnp.asarray(table.reshape(ROWS, length // ROWS, -1).astype(np.float32))
        for table in tables
    ]


def pair_sems():
    return [DMA((ROWS,)), DMA((ROWS,))]


def line_sems():
    return [DMA((ROWS, 2)), DMA((ROWS,))]


def square_sems():
    return [DMA((ROWS, SQUARE)), DMA((ROWS, SQUARE))]


def sum_sems():
    return [DMA((ROWS, SPLIT)), DMA((2, ROWS, SPLIT))]


def run_attention(
    activations,
    scaling,
    queries,
    compress,
    rescale,
    expand,
    combine,
    premix,
    segments,
    cotangent,
    routing,
    tables,
    slots,
):
    tokens, width = activations.shape
    seq = ROWS * tokens
    mine = queries.shape[1] // COLS
    sliced = compress.shape[1]
    latent_width = RANK + 128
    picked = SQUARE * slots
    lanes = NOPE + 2 * ROPE
    routes = jnp.pad(routing.T, ((0, 8 - routing.shape[1]), (0, 0)), constant_values=-1)
    whole = pl.BlockSpec(memory_space=VMEM)
    far = pl.BlockSpec(memory_space=pl.ANY)

    def shape(*dims, dtype=bf16):
        return jax.ShapeDtypeStruct(dims, dtype)

    return pl.pallas_call(
        attend_kernel,
        name="attend",
        out_shape=(
            shape(ROWS, tokens, width),
            shape(ROWS, tokens, mine),
            shape(2, ROWS, tokens, lanes),
            shape(2, ROWS, tokens, HEADV),
            shape(2, ROWS, tokens, seq),
            shape(ROWS, tokens, latent_width, dtype=f32),
            shape(ROWS, tokens, RANK),
            shape(ROWS, tokens, COLS * 2 * HEADV),
            shape(latent_width, width),
            shape(tokens, width, dtype=f32),
            shape(tokens, width),
            shape(tokens, 1, dtype=f32),
            shape(tokens, 1, dtype=f32),
            shape(ROWS, tokens, width),
            shape(ROWS, picked, tokens),
            shape(ROWS, tokens, picked),
            shape(COLS, ROWS, picked, width),
        ),
        in_specs=[whole] * 13 + [far] * 3,
        out_specs=(whole,) * 17,
        scratch_shapes=[
            VMEM(queries.shape, bf16),
            VMEM(expand.shape, bf16),
            VMEM(combine.shape, bf16),
            VMEM((2, tokens, 128), f32),
            VMEM((2, tokens, 128), f32),
            VMEM((ROWS, tokens, mine), f32),
            VMEM((ROWS, tokens, mine), bf16),
            VMEM((ROWS, tokens, mine), bf16),
            VMEM((ROWS, tokens, latent_width), f32),
            VMEM((ROWS, tokens, latent_width), f32),
            VMEM((ROWS, tokens, width), f32),
            VMEM((ROWS, tokens, width), bf16),
            VMEM((2, ROWS, tokens, width), bf16),
            VMEM((ROWS,) + routes.shape, jnp.int32),
            VMEM((ROWS, picked, width), bf16),
            DMA((3,)),
            DMA((2,)),
            DMA((2,)),
            *line_sems(),
            *line_sems(),
            *square_sems(),
            *pair_sems(),
            *pair_sems(),
            *pair_sems(),
            *sum_sems(),
            *line_sems(),
            *line_sems(),
            *square_sems(),
            *pair_sems(),
        ],
        compiler_params=pltpu.CompilerParams(
            collective_id=1, has_side_effects=True, vmem_limit_bytes=56 * MIB
        ),
        cost_estimate=pl.CostEstimate(
            flops=40 * 1024**3, bytes_accessed=32 * MIB, transcendentals=0
        ),
    )(
        activations,
        scaling.reshape(1, width),
        compress.T,
        rescale.reshape(1, RANK),
        premix.reshape(1, width),
        *tables,
        segments.reshape(ROWS, tokens, 1),
        segments.reshape(1, seq),
        cotangent,
        routes,
        queries,
        expand,
        combine,
    )


def attend_back_kernel(
    normed_grad_ref,
    residual_ref,
    scale_two_ref,
    premix_ref,
    cot_ref,
    act_ref,
    scale_one_ref,
    scaling_ref,
    one_ref,
    query_ref,
    key_ref,
    value_ref,
    probs_ref,
    latent_ref,
    rescale_ref,
    cos_ref,
    sin_ref,
    key_cos_ref,
    key_sin_ref,
    compress_all,
    queries_ref,
    expand_ref,
    combine_ref,
    input_grad_ref,
    branch_ref,
    query_grad_ref,
    expanded_ref,
    own_latent_ref,
    scaling_rows,
    rescale_rows,
    queries,
    expand,
    combine,
    stat_to,
    stat_from,
    grad_own,
    grad_to,
    grad_from,
    key_grad,
    value_grad,
    latent_own,
    latent_to,
    latent_from,
    turned,
    turned_from,
    part,
    leaving,
    coming,
    total,
    load_sem,
    stat_sent,
    stat_arrived,
    line_sent,
    line_arrived,
    grad_sent,
    grad_arrived,
    query_sent,
    query_arrived,
    latent_sent,
    latent_arrived,
    turned_sent,
    turned_arrived,
    own_sent,
    own_arrived,
    sum_sent,
    sum_arrived,
):
    place, row, col = lax.axis_index("dp"), lax.axis_index("row"), lax.axis_index("col")
    other = 1 - col
    sibling = {"col": other}
    tokens, width = act_ref.shape
    seq = ROWS * tokens
    mine = query_ref.shape[2]
    lanes = key_ref.shape[3]
    both = 2 * HEADV
    sliced = own_latent_ref.shape[0]
    score_scale = (NOPE + ROPE) ** (-0.5)
    loads = [
        pltpu.make_async_copy(source, target, load_sem.at[i])
        for i, (source, target) in enumerate(
            [(combine_ref, combine), (queries_ref, queries), (expand_ref, expand)]
        )
    ]
    for load in loads:
        load.start()
    line = Line(row, branch_ref, line_sent, line_arrived)
    sums = SumLine(row, part, leaving, coming, sum_sent, sum_arrived)
    greet(row, place, col, square=False)

    def stat_copy(index):
        return remote(
            stat_to.at[index],
            stat_from.at[index],
            stat_sent.at[index],
            stat_arrived.at[index],
            sibling,
        )

    def norm_grad(values, scale, gain, upstream, index):
        weighted = upstream * gain
        own = jnp.sum(weighted * values, axis=1, keepdims=True)
        stat_to[index] = jnp.broadcast_to(own, (tokens, 128))
        stat_copy(index).start()
        stat_copy(index).wait_recv()
        inner = (own + stat_from[index][:, 0:1]) / D
        return weighted * scale - values * (scale * scale * scale * inner)

    residual_grad = cot_ref[...].astype(f32) + norm_grad(
        residual_ref[...], scale_two_ref[...], premix_ref[...], normed_grad_ref[...], 0
    )
    input_grad_ref[...] = residual_grad
    branch_ref[pl.ds(row, 1)] = residual_grad.astype(bf16).reshape(1, tokens, width)
    key_grad[...] = jnp.zeros_like(key_grad)
    value_grad[...] = jnp.zeros_like(value_grad)
    scaling_rows[...] = jnp.zeros_like(scaling_rows)
    rescale_rows[...] = jnp.zeros_like(rescale_rows)

    def grad_copy(block):
        return remote(
            grad_to.at[block],
            grad_from.at[block],
            grad_sent.at[block],
            grad_arrived.at[block],
            sibling,
        )

    def query_copy(block, half):
        here = query_grad_ref.at[block, :, pl.ds(pl.multiple_of(half * mine, 128), mine)]
        return remote(here, here, query_sent.at[block], query_arrived.at[block], sibling)

    def latent_copy(block):
        return remote(
            latent_to.at[block],
            latent_from.at[block],
            latent_sent.at[block],
            latent_arrived.at[block],
            sibling,
        )

    def arrive(step):
        block = block_at(row, step)

        @pl.when(step > 0)
        def _():
            line.wait(block)

        line.pass_on(block)

        @pl.when(step == 0)
        def _():
            loads[0].wait()

        grads = branch_ref[block]
        grad_to[block] = nt(
            grads, combine[pl.ds(pl.multiple_of(other * both, 16), both)]
        ).astype(bf16)
        grad_copy(block).start()
        grad_own[block] = nt(grads, combine[pl.ds(pl.multiple_of(col * both, 16), both)])

    def heads(step):
        block = block_at(row, step)
        grad_copy(block).wait_recv()
        grads = (grad_own[block] + grad_from[block].astype(f32)).astype(bf16)
        pieces = []
        for head in range(2):
            upstream = grads[:, head * HEADV : (head + 1) * HEADV]
            query = query_ref[block, :, head * NOPE : head * NOPE + lanes]
            probs = probs_ref[head, block]
            weight = probs.astype(f32)
            probs_back = nt(upstream, value_ref[head].reshape(seq, HEADV))
            inner = jnp.sum(weight * probs_back, axis=1, keepdims=True)
            score_grad = (weight * (probs_back - inner)).astype(bf16)
            pieces.append(nn(score_grad, key_ref[head].reshape(seq, lanes)) * score_scale)
            key_grad[head] += tn(score_grad, query)
            value_grad[head] += tn(probs, upstream)
        first, second = pieces
        grad = jnp.concatenate(
            [first[:, :NOPE], first[:, NOPE:] + second[:, :NOPE], second[:, NOPE:]], axis=1
        )
        grad = grad * cos_ref[block] - swap_halves(grad) * sin_ref[block]
        query_grad_ref[block, :, pl.ds(pl.multiple_of(col * mine, 128), mine)] = grad.astype(bf16)
        query_copy(block, col).start()

    def project(step):
        block = block_at(row, step)

        @pl.when(step == 0)
        def _():
            loads[1].wait()

        query_copy(block, other).wait_recv()
        part[block] = nt(query_grad_ref[block], queries[...])

    def turn(step, carried):
        for delay, stage in ((0, arrive), (1, heads), (2, project)):

            @pl.when(jnp.logical_and(step >= delay, step < delay + ROWS))
            def _(delay=delay, stage=stage):
                stage(step - delay)

        return carried

    lax.fori_loop(0, ROWS + 1, turn, 0)
    loads[2].wait()

    def latents(turn, carried):
        block = block_at(row, ROWS - 1 - turn)
        here = pl.ds(pl.multiple_of(block * tokens, 128), tokens)
        first = key_grad[0, here] * score_scale
        second = pltpu.roll(key_grad[1, here] * score_scale, lanes - ROPE, 1)
        grad = jnp.concatenate(
            [first[:, :NOPE], value_grad[0, here], second[:, :NOPE], value_grad[1, here]], axis=1
        ).astype(bf16)
        expanded_ref[block] = grad
        own = 2 * (NOPE + HEADV)
        upstream = nt(grad, expand[:, pl.ds(pl.multiple_of(col * own, 128), own)])
        plain = latent_ref[block][:, :RANK]
        scale = lax.rsqrt(jnp.mean(plain * plain, axis=1, keepdims=True) + epsilon)
        rescale_rows[...] += jnp.sum(
            (upstream * plain * scale).reshape(tokens // 8, 8, RANK), axis=0
        )
        weighted = upstream * rescale_ref[...]
        inner = jnp.mean(weighted * plain, axis=1, keepdims=True)
        plain_grad = weighted * scale - plain * (scale * scale * scale * inner)
        rope = first[:, NOPE:] + second[:, NOPE:]
        lane = lax.broadcasted_iota(jnp.int32, rope.shape, 1)
        rope = jnp.where(lane < ROPE, rope, 0.0)
        rope = rope * key_cos_ref[block] - swap_halves(rope) * key_sin_ref[block]
        value = jnp.concatenate([plain_grad, rope], axis=1)
        latent_own[block] = value
        latent_to[block] = value.astype(bf16)
        latent_copy(block).start()
        return carried

    lax.fori_loop(0, ROWS, latents, 0)
    project(ROWS - 1)

    def turned_piece(member):
        return turned.at[
            pl.ds(pl.multiple_of(member * sliced, 16), sliced),
            pl.ds(pl.multiple_of(col * (seq // COLS), 128), seq // COLS),
        ]

    def turned_copy(step):
        to = lax.rem(row + step, ROWS)
        return remote(
            turned_piece(to),
            turned_from.at[step],
            turned_sent.at[step],
            turned_arrived.at[step],
            {"row": to},
        )

    def mix(turn, carried):
        block = block_at(row, ROWS - 1 - turn)
        latent_copy(block).wait_recv()
        latent = latent_own[block] + latent_from[block].astype(f32)
        here = pl.ds(pl.multiple_of(block * tokens, 128), tokens)
        total_here = part[block] + nn(latent.astype(bf16), compress_all[...])
        part[block] = total_here
        sums.begin(block)
        turned[:, here] = latent.T.astype(bf16)
        scaling_rows[...] += jnp.sum(
            (total_here * one_ref[block].astype(f32)).reshape(tokens // 8, 8, width), axis=0
        )
        return carried

    lax.fori_loop(0, ROWS, mix, 0)
    for step in range(1, ROWS):
        turned_copy(step).start()

    def hand_on(turn, carried):
        sums.pass_on(block_at(row, jnp.where(turn == 0, 3, turn)))
        return carried

    lax.fori_loop(0, 3, hand_on, 0)
    for step in range(1, ROWS):
        turned_copy(step).wait_recv()
    half = pl.ds(pl.multiple_of(col * (seq // COLS), 128), seq // COLS)
    own_sum = turned[pl.ds(pl.multiple_of(row * sliced, 16), sliced), half].astype(f32)
    for step in range(1, ROWS):
        own_sum = own_sum + turned_from[step].astype(f32)
    own_latent_ref[:, half] = own_sum.astype(bf16)

    def own_copy(part_of):
        here = own_latent_ref.at[
            :, pl.ds(pl.multiple_of(part_of * (seq // COLS), 128), seq // COLS)
        ]
        return remote(here, here, own_sent.at[0], own_arrived.at[0], sibling)

    own_copy(col).start()
    sums.total(total)
    input_grad_ref[...] += norm_grad(
        act_ref[...].astype(f32), scale_one_ref[...], scaling_ref[...], total[...], 1
    )
    own_copy(other).wait_recv()
    own_copy(col).wait_send()

    def ended(block, carried):
        grad_copy(block).wait_send()
        query_copy(block, col).wait_send()
        latent_copy(block).wait_send()
        return carried

    lax.fori_loop(0, ROWS, ended, 0)
    for step in range(1, ROWS):
        turned_copy(step).wait_send()
    stat_copy(0).wait_send()
    stat_copy(1).wait_send()
    sums.finish()
    line.finish()


def run_attention_back(
    normed_grad,
    residual,
    scale_two,
    premix,
    cotangent,
    activations,
    scale_one,
    scaling,
    one,
    query,
    key,
    value,
    probs,
    latent,
    rescale,
    tables,
    compress_all,
    queries,
    expand,
    combine,
):
    tokens, width = activations.shape
    seq = ROWS * tokens
    mine = query.shape[2]
    lanes = key.shape[3]
    latent_width = latent.shape[2]
    sliced = (RANK + ROPE) // ROWS
    whole = pl.BlockSpec(memory_space=VMEM)
    far = pl.BlockSpec(memory_space=pl.ANY)

    def shape(*dims, dtype=bf16):
        return jax.ShapeDtypeStruct(dims, dtype)

    return pl.pallas_call(
        attend_back_kernel,
        name="attend_back",
        out_shape=(
            shape(tokens, width, dtype=f32),
            shape(ROWS, tokens, width),
            shape(ROWS, tokens, COLS * mine),
            shape(ROWS, tokens, 2 * (NOPE + HEADV)),
            shape(sliced, seq),
            shape(8, width, dtype=f32),
            shape(8, RANK, dtype=f32),
        ),
        in_specs=[whole] * 20 + [far] * 3,
        out_specs=(whole,) * 7,
        scratch_shapes=[
            VMEM(queries.shape, bf16),
            VMEM(expand.shape, bf16),
            VMEM(combine.shape, bf16),
            VMEM((2, tokens, 128), f32),
            VMEM((2, tokens, 128), f32),
            VMEM((ROWS, tokens, 2 * HEADV), f32),
            VMEM((ROWS, tokens, 2 * HEADV), bf16),
            VMEM((ROWS, tokens, 2 * HEADV), bf16),
            VMEM((2, seq, lanes), f32),
            VMEM((2, seq, HEADV), f32),
            VMEM((ROWS, tokens, latent_width), f32),
            VMEM((ROWS, tokens, latent_width), bf16),
            VMEM((ROWS, tokens, latent_width), bf16),
            VMEM((latent_width, seq), bf16),
            VMEM((ROWS, sliced, seq // COLS), bf16),
            VMEM((ROWS, tokens, width), f32),
            VMEM((ROWS, tokens, width), bf16),
            VMEM((2, ROWS, tokens, width), bf16),
            VMEM((tokens, width), f32),
            DMA((3,)),
            DMA((2,)),
            DMA((2,)),
            *line_sems(),
            *pair_sems(),
            *pair_sems(),
            *pair_sems(),
            *pair_sems(),
            *pair_sems(),
            *sum_sems(),
        ],
        compiler_params=pltpu.CompilerParams(
            collective_id=3, has_side_effects=True, vmem_limit_bytes=56 * MIB
        ),
        cost_estimate=pl.CostEstimate(
            flops=40 * 1024**3, bytes_accessed=32 * MIB, transcendentals=0
        ),
    )(
        normed_grad,
        residual,
        scale_two,
        premix.reshape(1, width),
        cotangent,
        activations,
        scale_one,
        scaling.reshape(1, width),
        one,
        query,
        key,
        value,
        probs,
        latent,
        rescale.reshape(1, RANK),
        *tables,
        compress_all,
        queries,
        expand,
        combine,
    )


def silu_pair(values):
    sigmoid = 1.0 / (1.0 + jnp.exp(-values))
    return values * sigmoid, sigmoid * (1.0 + values * (1.0 - sigmoid))


def expert_kernel(
    normed_ref,
    pick_ref,
    back_ref,
    cot_rows_ref,
    cot_ref,
    fan_ref,
    fun_ref,
    wide_ref,
    narrow_ref,
    router_ref,
    sum_ref,
    gathered_ref,
    rows_out,
    gu_out,
    hidden_out,
    logit_out,
    shared_out,
    shared_gu_out,
    premix_ref,
    fan,
    fun,
    wide,
    narrow,
    cot_rows,
    rows,
    staged,
    gu,
    hidden,
    pair_own,
    pair_to,
    pair_from,
    home,
    shared_own,
    shared_to,
    shared_from,
    part,
    passed_to,
    passed_from,
    load_sem,
    store_sem,
    line_sent,
    line_arrived,
    out_sent,
    out_arrived,
    fwd_sent,
    fwd_arrived,
    shared_sent,
    shared_arrived,
    half_sent,
    half_arrived,
    home_sent,
    home_arrived,
    sum_sent,
    sum_arrived,
):
    place, row, col = lax.axis_index("dp"), lax.axis_index("row"), lax.axis_index("col")
    other = 1 - col
    tokens, width = normed_ref.shape
    picked = pick_ref.shape[1]
    slots = picked // SQUARE
    hid = fun.shape[0]
    share = narrow.shape[0]
    experts = router_ref.shape[1]
    loads = [
        pltpu.make_async_copy(source, target, load_sem.at[i])
        for i, (source, target) in enumerate(
            [
                (wide_ref, wide),
                (narrow_ref, narrow),
                (fan_ref, fan),
                (cot_rows_ref, cot_rows),
                (fun_ref, fun),
            ]
        )
    ]
    for load in loads:
        load.start()
    greet(row, place, col)
    gathered_ref[pl.ds(row, 1)] = normed_ref[...].reshape(1, tokens, width)
    premix_ref[...] = jnp.zeros_like(premix_ref)
    line = Line(row, gathered_ref, line_sent, line_arrived)
    sums = SumLine(row, part, passed_to, passed_from, sum_sent, sum_arrived)
    sibling = {"col": other}

    def out_copy(block, step):
        piece = pl.ds(step * slots, slots)
        return remote(
            staged.at[block, piece],
            rows.at[col, block, piece],
            out_sent.at[block, step],
            out_arrived.at[block, step],
            {"dp": partner(place, step)},
        )

    def home_copy(block, step):
        piece = pl.ds(step * slots, slots)
        return remote(
            staged.at[block, piece],
            home.at[block, piece],
            home_sent.at[block, step],
            home_arrived.at[block, step],
            {"dp": partner(place, step)},
        )

    def fwd_copy(block, half):
        here = rows.at[half, block]
        return remote(here, here, fwd_sent.at[block], fwd_arrived.at[block], sibling)

    def shared_copy(block):
        return remote(
            shared_to.at[block],
            shared_from.at[block],
            shared_sent.at[block],
            shared_arrived.at[block],
            sibling,
        )

    def half_copy(block):
        return remote(
            pair_to.at[block],
            pair_from.at[block],
            half_sent.at[block],
            half_arrived.at[block],
            sibling,
        )

    def stores(block):
        return [
            pltpu.make_async_copy(source, target, store_sem.at[index, block])
            for index, (source, target) in enumerate(
                [
                    (rows.at[:, block], rows_out.at[:, block]),
                    (gu.at[:, block], gu_out.at[:, block]),
                    (hidden.at[block], hidden_out.at[block]),
                ]
            )
        ]

    def take(step):
        block = block_at(row, step)

        @pl.when(step > 0)
        def _():
            line.wait(block)

        line.pass_on(block)
        staged[block] = nn(pick_ref[block], gathered_ref[block]).astype(bf16)
        for shift in (3, 2, 1):
            out_copy(block, shift).start()
        rows[col, block, 0:slots] = staged[block, 0:slots]

        @pl.when(step == 0)
        def _():
            loads[0].wait()
            loads[1].wait()

        slot = lax.rem(step, 2)
        for index, value in enumerate(
            (
                nn(gathered_ref[block], wide[0]),
                nn(gathered_ref[block], wide[1]),
                nt(cot_ref[block], narrow[...]),
            )
        ):
            shared_own[slot, index] = value
            shared_to[block, index] = value.astype(bf16)
        shared_copy(block).start()

    def forward(step):
        block = block_at(row, step)
        for shift in range(1, SQUARE):
            out_copy(block, shift).wait_recv()
        fwd_copy(block, col).start()

    def shared(step):
        block = block_at(row, step)
        slot = lax.rem(step, 2)
        shared_copy(block).wait_recv()
        gate, up, grad = [
            shared_own[slot, index] + shared_from[block, index].astype(f32) for index in range(3)
        ]
        act, slope = silu_pair(gate)
        shared_out[block] = (act * up).astype(bf16)
        gate_grad = (grad * up * slope).astype(bf16)
        up_grad = (grad * act).astype(bf16)
        shared_gu_out[0, block] = gate_grad
        shared_gu_out[1, block] = up_grad
        part[block] = nt(gate_grad, wide[0]) + nt(up_grad, wide[1])

    def experts_of(step):
        block = block_at(row, step)
        fwd_copy(block, other).wait_recv()

        @pl.when(step == 0)
        def _():
            for load in loads[2:]:
                load.wait()

        left, right = rows[0, block], rows[1, block]
        logits = nn(left, router_ref[0:width]) + nn(right, router_ref[width:])
        logits = logits - jnp.max(logits, axis=1, keepdims=True)
        weight = jnp.exp(logits)
        probs = weight / jnp.sum(weight, axis=1, keepdims=True)
        own = (
            lax.broadcasted_iota(jnp.int32, (picked, experts), 1) == place * ROWS + row
        ).astype(f32)
        gates = jnp.sum(probs * own, axis=1, keepdims=True)
        raw = nt(cot_rows[0, block], fun[:, 0:width]) + nt(cot_rows[1, block], fun[:, width:])
        gate = nn(left, fan[0, 0:width]) + nn(right, fan[0, width:])
        up = nn(left, fan[1, 0:width]) + nn(right, fan[1, width:])
        act, slope = silu_pair(gate)
        value = act * up
        hidden[block] = value.astype(bf16)
        gate_sum = gates * jnp.sum(value * raw, axis=1, keepdims=True)
        logit_grad = gate_sum * (own - probs)
        logit_out[block, :, 0:experts] = logit_grad
        logit_out[block, :, experts : experts + 1] = gates
        raw = raw * gates
        gu[0, block] = (raw * up * slope).astype(bf16)
        gu[1, block] = (raw * act).astype(bf16)
        logit_grad = logit_grad.astype(bf16)

        def half_of(half):
            lines = pl.ds(pl.multiple_of(half * width, width), width)
            return (
                nt(gu[0, block], fan[0, lines])
                + nt(gu[1, block], fan[1, lines])
                + nt(logit_grad, router_ref[lines])
            )

        pair_to[block] = half_of(other).astype(bf16)
        half_copy(block).start()
        pair_own[...] = half_of(col)
        for copy in stores(block):
            copy.start()

    def send_home(step):
        block = block_at(row, step)
        for shift in range(1, SQUARE):
            out_copy(block, shift).wait_send()
        half_copy(block).wait_recv()
        staged[block] = (pair_own[...] + pair_from[block].astype(f32)).astype(bf16)
        for shift in (3, 2, 1):
            home_copy(block, shift).start()
        home[block, 0:slots] = staged[block, 0:slots]

    def add_up(step):
        block = block_at(row, step)
        for shift in range(1, SQUARE):
            home_copy(block, shift).wait_recv()
        total = part[block] + nn(back_ref[block], home[block])
        part[block] = total
        premix_ref[...] += jnp.sum(
            (total * gathered_ref[block].astype(f32)).reshape(tokens // 8, 8, width), axis=0
        )

        sums.begin(block)

    stages = (
        (0, take),
        (1, forward),
        (1, shared),
        (3, send_home),
        (2, experts_of),
        (4, add_up),
    )

    def turn(step, carried):
        for delay, stage in stages:

            @pl.when(jnp.logical_and(step >= delay, step < delay + ROWS))
            def _(delay=delay, stage=stage):
                stage(step - delay)

        @pl.when(step >= ROWS + 3)
        def _():
            sums.pass_on(block_at(row, jnp.where(step == ROWS + 5, 1, step - 5)))

        return carried

    lax.fori_loop(0, ROWS + 6, turn, 0)
    sums.total(sum_ref)

    def ended(block, carried):
        shared_copy(block).wait_send()
        fwd_copy(block, col).wait_send()
        half_copy(block).wait_send()
        for shift in range(1, SQUARE):
            home_copy(block, shift).wait_send()
        for copy in stores(block):
            copy.wait()
        return carried

    lax.fori_loop(0, ROWS, ended, 0)
    sums.finish()
    line.finish()


def run_experts(
    normed, pick, back, cot_rows, cot_all, fan, fun, wide, narrow, router_all
):
    tokens, width = normed.shape
    picked = pick.shape[1]
    hid = fun.shape[0]
    share = narrow.shape[0]
    experts = router_all.shape[1]
    whole = pl.BlockSpec(memory_space=VMEM)
    far = pl.BlockSpec(memory_space=pl.ANY)

    def shape(*dims, dtype=bf16):
        return jax.ShapeDtypeStruct(dims, dtype)

    return pl.pallas_call(
        expert_kernel,
        name="experts",
        out_shape=(
            shape(tokens, width, dtype=f32),
            shape(ROWS, tokens, width),
            shape(COLS, ROWS, picked, width),
            shape(2, ROWS, picked, hid),
            shape(ROWS, picked, hid),
            shape(ROWS, picked, experts + 1, dtype=f32),
            shape(ROWS, tokens, share),
            shape(2, ROWS, tokens, share),
            shape(8, width, dtype=f32),
        ),
        in_specs=[whole, whole, whole, far, whole, far, far, far, far, whole],
        out_specs=(whole, whole, far, far, far, whole, whole, whole, whole),
        scratch_shapes=[
            VMEM(fan.shape, bf16),
            VMEM(fun.shape, bf16),
            VMEM(wide.shape, bf16),
            VMEM(narrow.shape, bf16),
            VMEM(cot_rows.shape, bf16),
            VMEM((COLS, ROWS, picked, width), bf16),
            VMEM((ROWS, picked, width), bf16),
            VMEM((2, ROWS, picked, hid), bf16),
            VMEM((ROWS, picked, hid), bf16),
            VMEM((picked, width), f32),
            VMEM((ROWS, picked, width), bf16),
            VMEM((ROWS, picked, width), bf16),
            VMEM((ROWS, picked, width), bf16),
            VMEM((2, 3, tokens, share), f32),
            VMEM((ROWS, 3, tokens, share), bf16),
            VMEM((ROWS, 3, tokens, share), bf16),
            VMEM((ROWS, tokens, width), f32),
            VMEM((ROWS, tokens, width), bf16),
            VMEM((2, ROWS, tokens, width), bf16),
            DMA((5,)),
            DMA((3, ROWS)),
            DMA((ROWS, 2)),
            DMA((ROWS,)),
            DMA((ROWS, SQUARE)),
            DMA((ROWS, SQUARE)),
            DMA((ROWS,)),
            DMA((ROWS,)),
            DMA((ROWS,)),
            DMA((ROWS,)),
            DMA((ROWS,)),
            DMA((ROWS,)),
            DMA((ROWS, SQUARE)),
            DMA((ROWS, SQUARE)),
            DMA((ROWS, SPLIT)),
            DMA((2, ROWS, SPLIT)),
        ],
        compiler_params=pltpu.CompilerParams(
            collective_id=2, has_side_effects=True, vmem_limit_bytes=62 * MIB
        ),
        cost_estimate=pl.CostEstimate(
            flops=60 * 1024**3, bytes_accessed=64 * MIB, transcendentals=0
        ),
    )(normed, pick, back, cot_rows, cot_all, fan, fun, wide, narrow, router_all)


def swap_back(parts):
    moves = [[(i, i ^ step) for i in range(SQUARE)] for step in range(SQUARE)]
    return [parts[0]] + [
        lax.ppermute(parts[step], "dp", moves[step]) for step in range(1, SQUARE)
    ]


def local_square(
    activations,
    cotangent,
    routing,
    segments,
    scaling,
    queries,
    compress,
    rescale,
    expand,
    combine,
    premix,
    router,
    widening,
    narrowing,
    fanout,
    funnel,
):
    dp_count = lax.axis_size("dp")
    row_count = lax.axis_size("row")
    col_count = lax.axis_size("col")
    col_index = lax.axis_index("col")
    local_rows, col_width = activations.shape
    seq_length = local_rows * row_count
    expert_total = router.shape[1]
    capacity = local_rows * TOP * 4 // (3 * expert_total)
    slot_total = capacity * row_count * dp_count
    tables = turning_tables(seq_length)
    router_all = col_gather(router)
    (
        one,
        query,
        key,
        value,
        probs,
        latent,
        latent_normed,
        attended,
        compress_all,
        residual,
        normed_two,
        scale_one,
        scale_two,
        cot_blocks,
        pick,
        back,
        cot_rows,
    ) = run_attention(
        activations,
        scaling,
        queries,
        compress,
        rescale,
        expand,
        combine,
        premix,
        segments,
        cotangent,
        routing,
        tables,
        capacity,
    )
    (
        normed_grad,
        two_blocks,
        expert_rows,
        expert_gu_grad,
        expert_hidden,
        slot_values,
        hidden_blocks,
        gu_blocks,
        premix_rows,
    ) = run_experts(
        normed_two,
        pick,
        back,
        cot_rows,
        cot_blocks,
        fanout[0],
        funnel[0],
        widening,
        narrowing,
        router_all,
    )
    cotangent_all = cot_blocks.reshape(seq_length, col_width)
    gathered_two = two_blocks.reshape(seq_length, col_width)
    hidden_all = hidden_blocks.reshape(seq_length, -1)
    gu_grad_all = gu_blocks.reshape(2, seq_length, -1)
    slot_rows = expert_rows.reshape(col_count, slot_total, col_width)
    reply_grad_rows = cot_rows.reshape(col_count, slot_total, col_width)
    slot_hidden = expert_hidden.reshape(slot_total, -1)
    slot_gu_grad = expert_gu_grad.reshape(2, slot_total, -1)
    slot_values = slot_values.reshape(slot_total, -1)
    logit_grad = slot_values[:, :expert_total].astype(bf16)
    slot_gates = slot_values[:, expert_total]

    narrowing_grad = dot_tn(hidden_all, cotangent_all)
    widening_grad = jnp.stack([dot_tn(gathered_two, gu_grad_all[i]) for i in range(2)])
    shared_sums = lax.psum((narrowing_grad.astype(bf16), widening_grad.astype(bf16)), "dp")
    (
        input_grad,
        branch_blocks,
        query_grad,
        expanded_grad,
        own_latent_grad,
        scaling_rows,
        rescale_rows,
    ) = run_attention_back(
        normed_grad,
        residual,
        scale_two,
        premix,
        cotangent,
        activations,
        scale_one,
        scaling,
        one,
        query,
        key,
        value,
        probs,
        latent,
        rescale,
        tables,
        compress_all,
        queries,
        expand,
        combine,
    )
    gathered_one = one.reshape(seq_length, col_width)
    attended_all = attended.reshape(seq_length, -1)
    late_parts = (
        dot_tn(gathered_one, query_grad.reshape(seq_length, -1)).astype(bf16),
        dot_tn(
            latent_normed.reshape(seq_length, -1), expanded_grad.reshape(seq_length, -1)
        ).astype(bf16),
        dot(own_latent_grad, gathered_one).astype(bf16),
        dot_tn(attended_all, branch_blocks.reshape(seq_length, col_width)).astype(bf16),
    )
    late_parts = (after(late_parts[0], *shared_sums),) + late_parts[1:]
    queries_sum, expand_sum, compress_sum, combine_sum = lax.psum(late_parts, "dp")

    scaled_hidden = (slot_hidden.astype(f32) * slot_gates[:, None]).astype(bf16)
    reply_part = dot(scaled_hidden, funnel[0])
    summed = col_scatter(reply_part.astype(bf16), axis=1)
    summed = summed.reshape(row_count, dp_count, capacity, col_width)
    returned = jnp.stack(swap_back([summed[:, k] for k in range(dp_count)]), axis=1)
    routed = jnp.einsum(
        "bts,bsd->btd",
        back,
        returned.reshape(row_count, dp_count * capacity, col_width),
        preferred_element_type=f32,
    ).reshape(seq_length, col_width)
    shared_out = row_scatter(routed + dot(hidden_all, narrowing))
    layer_output = (residual + shared_out).astype(bf16)

    funnel_grad = jnp.concatenate(
        [dot_tn(scaled_hidden, reply_grad_rows[i]) for i in range(col_count)], axis=1
    )[None]
    fanout_grad = jnp.stack(
        [
            jnp.concatenate([dot_tn(slot_rows[i], slot_gu_grad[j]) for i in range(col_count)])
            for j in range(2)
        ]
    )[None]

    router_part = jnp.concatenate([dot_tn(slot_rows[i], logit_grad) for i in range(col_count)])
    router_part = col_scatter(router_part)
    premix_part = jnp.sum(premix_rows, axis=0) / premix
    scaling_part = jnp.sum(scaling_rows, axis=0) / scaling
    rescale_part = col_totals(jnp.sum(rescale_rows, axis=0))
    small = jnp.concatenate(
        [premix_part, scaling_part, rescale_part, router_part.reshape(-1)]
    )
    small = lax.psum(small, ("dp", "row"))
    return (
        layer_output,
        input_grad,
        small[col_width : 2 * col_width],
        queries_sum.astype(f32),
        compress_sum.T.astype(f32),
        small[2 * col_width : 2 * col_width + RANK],
        col_gather(expand_sum, axis=1).astype(f32),
        combine_sum.astype(f32),
        small[:col_width],
        small[2 * col_width + RANK :].reshape(col_width, expert_total),
        shared_sums[1].astype(f32),
        shared_sums[0].astype(f32),
        fanout_grad,
        funnel_grad,
    )


def local(
    activations,
    cotangent,
    routing,
    segments,
    scaling,
    queries,
    compress,
    rescale,
    expand,
    combine,
    premix,
    router,
    widening,
    narrowing,
    fanout,
    funnel,
):
    dp_count = lax.axis_size("dp")
    row_count = lax.axis_size("row")
    col_count = lax.axis_size("col")
    dp_index = lax.axis_index("dp")
    row_index = lax.axis_index("row")
    col_index = lax.axis_index("col")
    local_rows = activations.shape[0]
    col_width = activations.shape[1]
    seq_length = local_rows * row_count
    half_length = seq_length // col_count
    head_width = NOPE + ROPE
    pair_width = NOPE + HEADV
    local_heads = queries.shape[1] // head_width
    slice_width = compress.shape[1]
    expert_total = router.shape[1]
    capacity = local_rows * TOP * 4 // (3 * expert_total)
    slots = capacity * row_count
    slot_total = slots * dp_count
    block_rows = min(512, half_length)
    block_count = half_length // block_rows
    score_scale = head_width ** (-0.5)

    inputs = activations.astype(f32)
    scale_one = norm_scale(inputs)
    normed_one = (inputs * scale_one[:, None] * scaling).astype(bf16)
    gathered_one = row_gather(normed_one)
    compress_all = lax.all_gather(compress, "row", axis=1, tiled=True)

    routing_all = row_gather(routing)
    cotangent_all = row_gather(after(cotangent, gathered_one))
    offsets = jnp.arange(dp_count, dtype=jnp.int32)
    my_experts = ((dp_index + offsets) % dp_count) * row_count + row_index
    goes = jnp.any(routing_all[None, :, :] == my_experts[:, None, None], axis=2)
    token_range = jnp.arange(seq_length, dtype=jnp.int32)
    earlier = (token_range[:, None] < token_range[None, :]).astype(bf16)
    rank = dot(goes.astype(bf16), earlier).astype(jnp.int32)
    slot_range = jnp.arange(slots, dtype=jnp.int32)
    pick = (
        ((rank[:, None, :] == slot_range[None, :, None]) & goes[:, None, :])
        .astype(bf16)
        .reshape(slot_total, seq_length)
    )

    def dispatch(tokens):
        rows = dot(pick, tokens).astype(bf16).reshape(dp_count, slots, col_width)
        arrived = send_out([rows[k] for k in range(dp_count)])
        return col_gather(jnp.concatenate(arrived, axis=0), axis=1)

    def bring_back(part):
        summed = col_scatter(part.astype(bf16), axis=1).reshape(dp_count, slots, col_width)
        arrived = send_back([summed[k] for k in range(dp_count)])
        return dot_tn(pick, jnp.concatenate(arrived, axis=0))

    query_part = dot(gathered_one, queries)
    latent_part = dot(gathered_one, compress_all)
    query_raw, latent_raw = col_scatter((query_part, latent_part))
    latent_plain = latent_raw[:, :RANK]
    latent_scale = lax.rsqrt(jnp.mean(latent_plain * latent_plain, axis=1) + epsilon)
    latent_normed = (latent_plain * latent_scale[:, None] * rescale).astype(bf16)
    expanded = dot(latent_normed, expand).reshape(half_length, local_heads, pair_width)
    positions = col_index * half_length + jnp.arange(half_length, dtype=jnp.int32)
    cosine, sine_table = rotation(positions, ROPE)
    key_shared = rotate(latent_raw[:, RANK:], cosine, sine_table, 1.0)
    query_heads = query_raw.reshape(half_length, local_heads, head_width)
    query_local = jnp.concatenate(
        [
            query_heads[..., :NOPE],
            rotate(query_heads[..., NOPE:], cosine[:, None, :], sine_table[:, None, :], 1.0),
        ],
        axis=2,
    ).astype(bf16)
    key_local = jnp.concatenate(
        [
            expanded[..., :NOPE],
            jnp.broadcast_to(key_shared[:, None, :], (half_length, local_heads, ROPE)),
        ],
        axis=2,
    ).astype(bf16)
    value_local = expanded[..., NOPE:].astype(bf16)
    key_flat, value_flat = (
        col_gather(key_local.reshape(half_length, local_heads * head_width)),
        col_gather(value_local.reshape(half_length, local_heads * HEADV)),
    )
    key_heads = key_flat.reshape(seq_length, local_heads, head_width)
    value_heads = value_flat.reshape(seq_length, local_heads, HEADV)
    own_segments = lax.dynamic_slice_in_dim(
        segments, col_index * half_length, half_length, 0
    ).reshape(block_count, block_rows)
    query_blocks = query_local.reshape(block_count, block_rows, local_heads, head_width)

    def attend_block(inputs_block):
        query_block, segment_block = inputs_block
        scores = (
            jnp.einsum("qhd,khd->hqk", query_block, key_heads, preferred_element_type=f32)
            * score_scale
        )
        visible = segments[None, None, :] <= segment_block[None, :, None]
        scores = jnp.where(visible, scores, masked_score)
        largest = jnp.max(scores, axis=2, keepdims=True)
        weight = jnp.exp(scores - largest)
        totals = jnp.sum(weight, axis=2, keepdims=True)
        probability = (weight / totals).astype(bf16)
        result = jnp.einsum("hqk,khd->qhd", probability, value_heads, preferred_element_type=f32)
        return (result.astype(bf16), (largest + jnp.log(totals))[..., 0])

    attended_blocks, log_totals = lax.map(attend_block, (query_blocks, own_segments))
    attended = attended_blocks.reshape(half_length, local_heads * HEADV)
    attended_all = col_gather(attended)
    branch = row_scatter(dot(attended_all, combine))

    reply_grad_rows = dispatch(cotangent_all)
    inner_weight = fanout[0]
    outer_weight = funnel[0]
    hidden_raw = dot_nt(reply_grad_rows, outer_weight)
    shared_hidden_grad = col_scatter(dot_nt(cotangent_all, narrowing))

    residual = inputs + branch
    scale_two = norm_scale(residual)
    normed_two = (residual * scale_two[:, None] * premix).astype(bf16)
    gathered_two = row_gather(normed_two)

    expert_rows = dispatch(gathered_two)
    expert_range = jnp.arange(expert_total, dtype=jnp.int32)
    router_all = lax.all_gather(router, "col", axis=0, tiled=True)
    own_expert = dp_index * row_count + row_index
    slot_probs = jax.nn.softmax(dot(expert_rows, router_all), axis=1)
    slot_gates = jnp.sum(jnp.where(expert_range == own_expert, slot_probs, 0.0), axis=1)
    gate_up = jnp.einsum("rd,gdf->grf", expert_rows, inner_weight, preferred_element_type=f32)
    gate_input, up_input = gate_up[0], gate_up[1]
    hidden = jax.nn.silu(gate_input) * up_input
    expert_hidden = hidden.astype(bf16)
    slot_gate_grad = col_totals(jnp.sum(hidden * hidden_raw, axis=1))
    hidden_grad = hidden_raw * slot_gates[:, None]
    expert_gu_grad = jnp.stack(
        [hidden_grad * up_input * silu_slope(gate_input), hidden_grad * jax.nn.silu(gate_input)]
    ).astype(bf16)
    input_part = jnp.einsum(
        "grf,gdf->rd", expert_gu_grad, inner_weight, preferred_element_type=f32
    )
    routed_grad = bring_back(input_part)
    gate_grad_parts = send_back(
        [slot_gate_grad.reshape(dp_count, slots)[k] for k in range(dp_count)]
    )

    logits = col_totals(dot(gathered_two, router))
    router_probs = jax.nn.softmax(logits, axis=1)
    gate_grad = jnp.sum(
        pick.reshape(dp_count, slots, seq_length).astype(f32)
        * jnp.stack(gate_grad_parts)[:, :, None],
        axis=1,
    )
    mine = (my_experts[:, None] == expert_range[None, :]).astype(f32)
    probs_grad = jnp.sum(gate_grad[:, :, None] * mine[:, None, :], axis=0)
    logit_grad = router_probs * (
        probs_grad - jnp.sum(router_probs * probs_grad, axis=1, keepdims=True)
    )
    router_part = dot_tn(gathered_two, logit_grad)

    shared_gate_up = col_scatter(
        jnp.einsum("td,gdf->tgf", gathered_two, widening, preferred_element_type=f32)
    )
    shared_hidden = (jax.nn.silu(shared_gate_up[:, 0]) * shared_gate_up[:, 1]).astype(bf16)
    hidden_all = col_gather(shared_hidden)
    narrowing_grad = dot_tn(hidden_all, cotangent_all)
    shared_gu_grad = jnp.stack(
        [
            shared_hidden_grad * shared_gate_up[:, 1] * silu_slope(shared_gate_up[:, 0]),
            shared_hidden_grad * jax.nn.silu(shared_gate_up[:, 0]),
        ],
        axis=1,
    ).astype(bf16)
    gu_grad_all = col_gather(shared_gu_grad)
    widening_grad = jnp.einsum(
        "td,tgf->gdf", gathered_two, gu_grad_all, preferred_element_type=f32
    )
    shared_input_part = jnp.einsum(
        "tgf,gdf->td", gu_grad_all, widening, preferred_element_type=f32
    )
    shared_sums = lax.psum((narrowing_grad.astype(bf16), widening_grad.astype(bf16)), "dp")

    grad_part = routed_grad + shared_input_part + dot_nt(logit_grad, router)
    premix_part = jnp.sum(grad_part * gathered_two.astype(f32), axis=0) / premix
    normed_grad = row_scatter(grad_part)

    upstream = cotangent.astype(f32)
    residual_grad = upstream + norm_back(residual, scale_two, premix, normed_grad)
    branch_all = row_gather(residual_grad.astype(bf16))

    funnel_grad = dot_tn((hidden * slot_gates[:, None]).astype(bf16), reply_grad_rows)[None]
    fanout_grad = jnp.einsum(
        "rd,grf->gdf", expert_rows, expert_gu_grad, preferred_element_type=f32
    )[None]
    reply_part = dot(expert_hidden, outer_weight) * slot_gates[:, None]
    routed = bring_back(reply_part)
    shared_out = row_scatter(routed + dot(hidden_all, narrowing))
    layer_output = (residual + shared_out).astype(bf16)

    combine_grad = dot_tn(attended_all, branch_all)
    combine_sum = lax.psum(after(combine_grad.astype(bf16), *shared_sums), "dp")
    attended_grad = col_scatter(dot_nt(branch_all, combine))
    attended_grad_blocks = attended_grad.astype(bf16).reshape(
        block_count, block_rows, local_heads, HEADV
    )

    def attend_back(carried, inputs_block):
        key_sum, value_sum = carried
        query_block, grad_block, log_block, segment_block = inputs_block
        scores = (
            jnp.einsum("qhd,khd->hqk", query_block, key_heads, preferred_element_type=f32)
            * score_scale
        )
        visible = segments[None, None, :] <= segment_block[None, :, None]
        probability = jnp.where(visible, jnp.exp(scores - log_block[..., None]), 0.0)
        weight_grad = jnp.einsum(
            "qhd,khd->hqk", grad_block, value_heads, preferred_element_type=f32
        )
        inner_sum = jnp.sum(probability * weight_grad, axis=2, keepdims=True)
        score_grad = (probability * (weight_grad - inner_sum)).astype(bf16)
        query_grad_block = (
            jnp.einsum("hqk,khd->qhd", score_grad, key_heads, preferred_element_type=f32)
            * score_scale
        )
        key_sum = (
            key_sum
            + jnp.einsum("hqk,qhd->khd", score_grad, query_block, preferred_element_type=f32)
            * score_scale
        )
        value_sum = value_sum + jnp.einsum(
            "hqk,qhd->khd", probability.astype(bf16), grad_block, preferred_element_type=f32
        )
        return ((key_sum, value_sum), query_grad_block)

    key_start = jnp.zeros((seq_length, local_heads, head_width), f32)
    value_start = jnp.zeros((seq_length, local_heads, HEADV), f32)
    (key_grad_all, value_grad_all), query_grad_blocks = lax.scan(
        attend_back,
        (key_start, value_start),
        (query_blocks, attended_grad_blocks, log_totals, own_segments),
    )
    key_grad, value_grad = col_scatter(
        (
            key_grad_all.reshape(seq_length, local_heads * head_width),
            value_grad_all.reshape(seq_length, local_heads * HEADV),
        )
    )
    key_grad = key_grad.reshape(half_length, local_heads, head_width)
    value_grad = value_grad.reshape(half_length, local_heads, HEADV)
    query_grad = query_grad_blocks.reshape(half_length, local_heads, head_width)
    query_raw_grad = (
        jnp.concatenate(
            [
                query_grad[..., :NOPE],
                rotate(query_grad[..., NOPE:], cosine[:, None, :], sine_table[:, None, :], -1.0),
            ],
            axis=2,
        )
        .astype(bf16)
        .reshape(half_length, local_heads * head_width)
    )
    expanded_grad = (
        jnp.concatenate([key_grad[..., :NOPE], value_grad], axis=2)
        .astype(bf16)
        .reshape(half_length, local_heads * pair_width)
    )
    shared_rope_grad = rotate(jnp.sum(key_grad[..., NOPE:], axis=1), cosine, sine_table, -1.0)

    latent_grad = dot_nt(expanded_grad, expand)
    latent_weighted = latent_grad * rescale
    latent_inner = jnp.mean(latent_weighted * latent_plain, axis=1)
    rescale_part = jnp.sum(latent_grad * latent_plain * latent_scale[:, None], axis=0)
    plain_grad = (
        latent_weighted * latent_scale[:, None]
        - latent_plain * (latent_scale**3 * latent_inner)[:, None]
    )
    latent_raw_grad = jnp.concatenate([plain_grad, shared_rope_grad], axis=1).astype(bf16)
    query_grad_all = col_gather(query_raw_grad)
    latent_grad_all = col_gather(latent_raw_grad)
    first_part = dot_nt(query_grad_all, queries) + dot_nt(latent_grad_all, compress_all)
    first_grad = row_scatter(first_part)
    input_grad = residual_grad + norm_back(inputs, scale_one, scaling, first_grad)

    queries_part = dot_tn(gathered_one, query_grad_all)
    own_latent_grad = lax.psum_scatter(
        latent_raw_grad, "row", scatter_dimension=1, tiled=True
    )
    compress_part = dot_tn(gathered_one, col_gather(own_latent_grad))
    half_rank = RANK // col_count
    latent_normed_all = col_gather(latent_normed)
    expanded_grad_all = col_gather(expanded_grad)
    expand_half = dot_tn(
        lax.dynamic_slice_in_dim(latent_normed_all, col_index * half_rank, half_rank, 1),
        expanded_grad_all,
    )
    scaling_part = jnp.sum(first_part * gathered_one.astype(f32), axis=0) / scaling
    queries_sum, expand_sum, compress_sum = lax.psum(
        (
            after(queries_part.astype(bf16), combine_sum),
            expand_half.astype(bf16),
            compress_part.astype(bf16),
        ),
        "dp",
    )
    premix_sum, router_sum = lax.psum((premix_part, router_part), ("dp", "row"))
    rescale_sum = lax.psum(rescale_part, ("dp", "row", "col"))
    scaling_sum = lax.psum(scaling_part, ("dp", "row"))
    return (
        layer_output,
        input_grad,
        scaling_sum,
        queries_sum.astype(f32),
        compress_sum.astype(f32),
        rescale_sum,
        col_gather(expand_sum).astype(f32),
        combine_sum.astype(f32),
        premix_sum,
        router_sum,
        shared_sums[1].astype(f32),
        shared_sums[0].astype(f32),
        fanout_grad,
        funnel_grad,
    )


def solution(mesh):
    placed = (
        P(("dp", "row"), "col"),
        P(("dp", "row"), "col"),
        P(("dp", "row"), None),
        P("dp"),
        P("col"),
        P("col", "row"),
        P("col", "row"),
        P(),
        P(None, "row"),
        P("row", "col"),
        P("col"),
        P("col", None),
        P(None, "col", "row"),
        P("row", "col"),
        P(("dp", "row"), None, None, "col"),
        P(("dp", "row"), "col", None),
    )
    squared = mesh.shape["dp"] == SQUARE and mesh.shape["row"] == ROWS
    return jax.shard_map(
        local_square if squared else local,
        mesh=mesh,
        in_specs=placed,
        out_specs=(
            P(("dp", "row"), "col"),
            P(("dp", "row"), "col"),
            P("col"),
            P("col", "row"),
            P("col", "row"),
            P(),
            P(None, "row"),
            P("row", "col"),
            P("col"),
            P("col", None),
            P(None, "col", "row"),
            P("row", "col"),
            P(("dp", "row"), None, None, "col"),
            P(("dp", "row"), "col", None),
        ),
        check_vma=False,
    )
```

time: 884 us -> 565 us (0.64)
  waiting for transfers between devices: 435 us -> 182 us
  Pallas kernels: 0 us -> 228 us
  blocking collectives: 141 us -> 5.45 us
  matrix products: 114 us -> 44.5 us
  other arithmetic: 68.9 us -> 34.9 us
  local copies, waits for them, and re-layouts: 74.7 us -> 41.4 us
  starting transfers between devices: 22.6 us -> 3.41 us
    pallas_call x0 -> x3, Pallas kernels: none -> 228 us  [the longest x1 86.2 us: run_experts(): pl.pallas_call(expert_kernel, name='experts', out_shape=(shape(tokens, wi...]
    all_to_all x3 -> x0, waiting for transfers between devices: 104 us -> none  [expert_exchange(): lax.all_to_all(values, ('dp', 'row'), split_axis=0, concat_axis=0, tiled=...]
    reduce_scatter x13 -> x3, waiting for transfers between devices: 78.1 us -> 0.03 us  [the longest x2 0.03 us: col_scatter(): return lax.psum_scatter(values, 'col', scatter_dimension=axis, tiled=True)]
    all_gather x7 -> x1, waiting for transfers between devices: 74.5 us -> 0.01 us  [col_gather(): return lax.all_gather(values, 'col', axis=axis, tiled=True)]
    dot_general x33 -> x18, matrix products: 114 us -> 44.5 us  [the longest x14 35 us: dot_tn(): lax.dot_general(left, right, (((0,), (0,)), ((), ())), preferred_element_...]
    all_to_all x1 -> x0, blocking collectives: 52.6 us -> none  [expert_exchange(): lax.all_to_all(values, ('dp', 'row'), split_axis=0, concat_axis=0, tiled=...]
    all_gather x7 -> x1, blocking collectives: 34 us -> 2.62 us  [col_gather(): return lax.all_gather(values, 'col', axis=axis, tiled=True)]
    psum x2 -> x0, blocking collectives: 27.7 us -> none  [the longest x1 14.5 us: local(): lax.psum(scaling_sum.astype(jnp.bfloat16), 'dp').astype(jnp.float32)]
  transfers between devices with their start and end apart: 25 -> 10, of which waited for: 17 -> 3; matrix products, arithmetic and copies ran while one was open for 20% -> 15% of each run, Pallas kernels for 0% -> 12%
where the time goes in v1:
time: 565 us; the launch traced here: 556 us
  Pallas kernels  228 us (40%)
  waiting for transfers between devices  182 us (32%)
  matrix products  44.5 us (8%)
  local copies, waits for them, and re-layouts  41.4 us (7%)
  other arithmetic  34.9 us (6%)
  between operations  16.3 us (3%)
    pallas_call x1, Pallas kernels, run_experts(): pl.pallas_call(expert_kernel, name='experts', out_shape=(shape(tokens, wi...  86.2 us
    psum x1, waiting for transfers between devices, local_square(): lax.psum(late_parts, 'dp')  85.2 us
    psum x1, waiting for transfers between devices, local_square(): small = lax.psum(small, ('dp', 'row'))  77.9 us
    pallas_call x1, Pallas kernels, run_attention(): pl.pallas_call(attend_kernel, name='attend', out_shape=(shape(ROWS, token...  75.4 us
    pallas_call x1, Pallas kernels, run_attention_back(): pl.pallas_call(attend_back_kernel, name='attend_back', out_shape=(shape(t...  66.1 us
    dot_general x14, matrix products, dot_tn(): lax.dot_general(left, right, (((0,), (0,)), ((), ())), preferred_element_...  35 us
    unnamed x76, local copies, waits for them, and re-layouts  28.5 us
    psum x1, waiting for transfers between devices, local_square(): lax.psum((narrowing_grad.astype(bf16), widening_grad.astype(bf16)), 'dp')  19.1 us
  transfers between devices with their start and end apart: 10, of which 3 were waited for; matrix products, arithmetic and copies ran while one was open for 15% of the time, Pallas kernels for 12%

profile of v1, /device:TPU:9, one launch (start us, length us, event | category | flops | bytes accessed | tf_op | source)
XLA Modules:
  0.0 555.9 jit_solution(1181543302501757956)
XLA Ops:
  9.0 2.6 all_gather.6.router_ref
  11.6 1.5 copy.49.mark_rows_ref
  13.1 4.6 copy.52.wide_ref
  17.7 8.5 %copy.50 = bf16[1,2,2048,704]{3,2,1,0:T(8,128)(2,1)} copy(bf16[1,2,2048,704]{2,3,1,0:T(8,128)(2,1)} %param.34) | data formatting | bytes 11534336 | tf_op args[14]
  26.8 75.4 %attend.1 = (bf16[4,128,1024]{2,1,0:T(8,128)(2,1)}, bf16[4,128,384]{2,1,0:T(8,128)(2,1)}, bf16[2,4,128,256]{3,2,1,0:T(8,128)(2,1)}, bf16[2,4,128,128]{3,2,1,0:T(...) custom-call(bf16[128,1024]{1,0:T(8,128)(2,1)} %act_ref.3, ...), custom_call_target="tpu_custom_call" | custom-call | flops 42949672960 | bytes 33554432 | tf_op jit(solution)/shard_map/attend/pallas_call | solution.py:768
  102.3 86.2 %experts.1 = (f32[128,1024]{1,0:T(8,128)}, bf16[4,128,1024]{2,1,0:T(8,128)(2,1)}, bf16[2,4,256,1024]{3,2,1,0:T(8,128)(2,1)}, bf16[2,4,256,704]{3,2,1,0:T(8,128)(...) custom-call(bf16[128,1024]{1,0:T(8,128)(2,1)} %get-tuple-element.50., ...), custom_call_target="tpu_custom_call" | custom-call | flops 64424509440 | bytes 67108864 | tf_op jit(solution)/shard_map/experts/pallas_call | solution.py:1587
  188.4 3.6 bitcast_convert_fusion.1
  192.2 1.1 copy-done.27
  194.3 1.0 fusion.25
  195.2 1.8 pad_maximum_fusion
  197.1 2.7 fusion.41
  202.5 2.2 copy-done.25
  204.6 4.9 convolution_convert_fusion
  209.6 66.1 %attend_back.1 = (f32[128,1024]{1,0:T(8,128)}, bf16[4,128,1024]{2,1,0:T(8,128)(2,1)}, bf16[4,128,768]{2,1,0:T(8,128)(2,1)}, bf16[4,128,512]{2,1,0:T(8,128)(2,1)}...) custom-call(f32[128,1024]{1,0:T(8,128)} %get-tuple-element.57.normed_grad_ref, ...), custom_call_target="tpu_custom_call" | custom-call | flops 42949672960 | bytes 33554432 | tf_op jit(solution)/shard_map/attend_back/pallas_call | solution.py:1194
  275.7 2.1 fusion.32
  277.8 2.5 fusion.31
  280.3 1.7 bitcast_convert_fusion.2
  282.0 2.2 bitcast_convert_fusion
  284.2 19.1 %all-reduce.11.cloned.1.call-done = (bf16[704,1024]{1,0:T(8,128)(2,1)}, bf16[2,1024,704]{1,2,0:T(8,128)(2,1)}) async-done(((bf16[704,1024]{1,0:T(8,128)(2,1)}, bf16[2,1024,704]{1,2,0:T(8,128)(2,1)}), (bf16[704,1024]{1,0:T(8,128)(2,1)}, bf16[2,1024,704]{1,2,0:T(8,128)(2,1)})) %all-reduce.11.cloned.1.call-update) | async-done | bytes 4325392 | tf_op jit(solution)/shard_map/psum | solution.py:1754
  303.6 2.8 psum.56
  306.4 5.5 fusion.15
  311.9 3.4 fusion.18
  315.3 3.3 fusion.12
  318.6 1.0 copy.58
  320.6 3.0 slice_bitcast_fusion.3
  323.6 1.2 collective-permute-start
  324.8 1.2 collective-permute-start.2
  326.3 2.5 fusion.40
  328.7 85.2 %all-reduce.9.cloned.1.call-done = (bf16[1024,768]{1,0:T(8,128)(2,1)}, bf16[1024,144]{0,1:T(8,128)(2,1)}, bf16[512,512]{1,0:T(8,128)(2,1)}, bf16[512,1024]{1,0:T(8,128)(2,1)}) async-done(((bf16[1024,768]{1,0:T(8,128)(2,1)}, bf16[1024,144]{0,1:T(8,128)(2,1)}, bf16[512,512]{1,0:T(8,128)(2,1)}, bf16[512,1024]{1,0:T(8,128)(2,1)}), (bf16[1024,768]{1,0:T(8,128)(2,1)}, bf16[1024,144]{0,1:T(8,128)(2,1)}, ...) | async-done | bytes 3440656 | tf_op jit(solution)/shard_map/psum | solution.py:1796
  414.2 4.9 fusion.46
  419.1 1.5 pad_maximum_fusion.1
  422.0 1.0 copy-done.26
  423.3 2.1 fusion.8
  425.4 3.4 fusion.45
  428.8 3.7 maximum_bitcast_fusion.3
  432.5 1.7 copy-done.33
  434.2 1.7 fusion.9
  437.8 3.2 maximum_bitcast_fusion.1
  441.0 8.9 %maximum_bitcast_fusion = f32[1,2,2048,704]{2,3,1,0:T(8,128)} fusion(f32[1,2048,704]{1,2,0:T(8,128)} %get-tuple-element.115, f32[1,2048,704]{1,2,0:T(8,128)S(1)} %get-tuple-element.114), kind=kLoop, calls=%fused_computation | loop fusion | flops 2883584 | bytes 23068672 | tf_op jit(solution)/shard_map/broadcast_in_dim | solution.py:1815
  449.9 77.9 %all-reduce.7.cloned.1.call-done = f32[18944]{0:T(1024)} async-done(((f32[18944]{0:T(1024)}), f32[18944]{0:T(1024)}) %all-reduce.7.cloned.1.call-update) | async-done | bytes 75792 | tf_op jit(solution)/shard_map/psum | solution.py:1830
  529.7 1.3 slice.102
  530.9 1.3 fusion.43
  532.2 1.9 convert_element_type.82
  535.1 3.3 convert_element_type.81
  539.2 1.9 convert_element_type.73
  541.1 1.6 convert_element_type.80
  542.7 2.9 convert_element_type.78
  545.6 1.7 add_convert_fusion
  (112 shorter events, 15.0 us)
Async XLA Ops:
  8.0 295.4 %all-reduce.11.cloned.1.call-start = ((), (), s32[]{:S(2)}) async-start(), calls=%async_computation.9 | async-start | bytes 8650752 | tf_op jit(solution)/shard_map/psum | solution.py:1754
  17.7 8.5 %copy-start.24 = (s32[128,6]{0,1:T(8,128)S(1)}, s32[128,6]{0,1:T(8,128)}, u32[]{:S(2)}) copy-start(s32[128,6]{0,1:T(8,128)} %param.22) | copy-start | bytes 9220
  188.4 3.6 copy-start.10
  192.1 1.2 copy-start.27
  197.1 121.5 %reduce-scatter.8.cloned.1.call-start = ((), (), s32[]{:S(2)}) async-start(), calls=%async_computation.5 | async-start | bytes 196608 | tf_op jit(solution)/shard_map/reduce_scatter | solution.py:77
  197.1 2.8 copy-start.1
  200.3 1.8 copy-start.9
  201.5 119.1 %reduce-scatter.4.cloned.1.call-start = ((), (), s32[]{:S(2)}) async-start(), calls=%async_computation.3 | async-start | bytes 6291456 | tf_op jit(solution)/shard_map/reduce_scatter | solution.py:77
  202.1 2.5 copy-start.25
  209.6 204.3 %all-reduce.9.cloned.1.call-start = ((), (), s32[]{:S(2)}) async-start(), calls=%async_computation.8 | async-start | bytes 6881280 | tf_op jit(solution)/shard_map/psum | solution.py:1796
  209.6 66.1 %copy-start.14 = (bf16[4,128,1024]{2,1,0:T(8,128)(2,1)S(1)}, bf16[4,128,1024]{2,1,0:T(8,128)(2,1)}, u32[]{:S(2)}) copy-start(bf16[4,128,1024]{2,1,0:T(8,128)(2,1)} %get-tuple-element.60.one_ref) | copy-start | bytes 3145732
  209.6 68.2 %copy-start.29 = (bf16[4,128,512]{2,1,0:T(8,128)(2,1)S(1)}, bf16[4,128,512]{2,1,0:T(8,128)(2,1)}, u32[]{:S(2)}) copy-start(bf16[4,128,512]{2,1,0:T(8,128)(2,1)} %get-tuple-element.77) | copy-start | bytes 1572868
  275.7 4.6 copy-start.30
  275.7 4.6 copy-start.31
  277.8 4.2 copy-start.34
  284.2 19.2 %copy-start.21 = (f32[8,512]{1,0:T(8,128)S(1)}, f32[8,512]{1,0:T(8,128)}, u32[]{:S(2)}) copy-start(f32[8,512]{1,0:T(8,128)} %get-tuple-element.70) | copy-start | bytes 49156
  284.2 19.3 %copy-start.20 = (f32[8,1024]{1,0:T(8,128)S(1)}, f32[8,1024]{1,0:T(8,128)}, u32[]{:S(2)}) copy-start(f32[8,1024]{1,0:T(8,128)} %get-tuple-element.69) | copy-start | bytes 98308
  284.2 19.3 %copy-start.19 = (f32[8,1024]{1,0:T(8,128)S(1)}, f32[8,1024]{1,0:T(8,128)}, u32[]{:S(2)}) copy-start(f32[8,1024]{1,0:T(8,128)} %get-tuple-element.68) | copy-start | bytes 98308
  284.2 19.3 %copy-start.22 = (f32[1024]{0:T(1024)S(1)}, f32[1024]{0:T(1024)}, u32[]{:S(2)}) copy-start(f32[1024]{0:T(1024)} %param.30) | copy-start | bytes 12292
  284.2 19.3 %copy-start.23 = (f32[1024]{0:T(1024)S(1)}, f32[1024]{0:T(1024)}, u32[]{:S(2)}) copy-start(f32[1024]{0:T(1024)} %param.24) | copy-start | bytes 12292
  303.4 224.4 %all-reduce.7.cloned.1.call-start = ((), (), s32[]{:S(2)}) async-start(), calls=%async_computation.6 | async-start | bytes 155648 | tf_op jit(solution)/shard_map/psum | solution.py:1830
  306.4 5.5 copy-start.2
  306.4 5.5 copy-start.32
  320.5 222.2 %all-gather.2.cloned.1.call-start = ((), (), s32[]{:S(2)}) async-start(), calls=%async_computation.7 | async-start | bytes 1572864 | tf_op jit(solution)/shard_map/all_gather | solution.py:73
  320.6 5.7 %copy-start.4 = (bf16[2,4,256,1024]{3,2,1,0:T(8,128)(2,1)S(1)}, bf16[2,4,256,1024]{3,2,1,0:T(8,128)(2,1)}, u32[]{:S(2)}) copy-start(bf16[2,4,256,1024]{3,2,1,0:T(8,128)(2,1)} %get-tuple-element.52.cot_rows_ref) | copy-start | bytes 12582916
  323.6 95.4 %collective-permute-start = (bf16[4,64,1024]{2,1,0:T(8,128)(2,1)}, bf16[4,64,1024]{2,1,0:T(8,128)(2,1)S(1)}, u32[]{:S(2)}, u32[]{:S(2)}) collective-permute-start(bf16[4,64,1024]{2,1,0:T(8,128)(2,1)} %get-tuple-element.107), channel_id=1, source_target_pairs={{0,8},{8,0},{16,24},{24,16},{1,9},{9,1},{17,25},{25,17},{2,10},{10... | collective-permute-start | bytes 1572872 | tf_op jit(solution)/shard_map/ppermute | solution.py:1652
  324.8 94.3 %collective-permute-start.2 = (bf16[4,64,1024]{2,1,0:T(8,128)(2,1)}, bf16[4,64,1024]{2,1,0:T(8,128)(2,1)}, u32[]{:S(2)}, u32[]{:S(2)}) collective-permute-start(bf16[4,64,1024]{2,1,0:T(8,128)(2,1)} %get-tuple-element.108), channel_id=1, source_target_pairs={{0,24},{8,16},{16,8},{24,0},{1,25},{9,17},{17,9},{25,1},{2,26},{10... | collective-permute-start | bytes 1572872 | tf_op jit(solution)/shard_map/ppermute | solution.py:1652
  326.0 93.1 %collective-permute-start.1 = (bf16[4,64,1024]{2,1,0:T(8,128)(2,1)S(1)}, bf16[4,64,1024]{2,1,0:T(8,128)(2,1)}, u32[]{:S(2)}, u32[]{:S(2)}) collective-permute-start(bf16[4,64,1024]{2,1,0:T(8,128)(2,1)S(1)} %get-tuple-element.109), channel_id=1, source_target_pairs={{0,16},{8,24},{16,0},{24,8},{1,17},{9,25},{17,1},{25,9},{2,18},{10... | collective-permute-start | bytes 1572872 | tf_op jit(solution)/shard_map/ppermute | solution.py:1652
  413.9 131.7 %reduce-scatter.6.cloned.1.call-start = ((), (), s32[]{:S(2)}) async-start(), calls=%async_computation.4 | async-start | bytes 1310720 | tf_op jit(solution)/shard_map/reduce_scatter | solution.py:81
  420.6 1.0 copy-start.18
  421.5 1.5 copy-start.26
  421.5 1.7 copy-start.28
  425.4 3.5 copy-start
  428.8 3.7 copy-start.3
  428.8 5.4 copy-start.33
  434.2 1.8 copy-start.6
  434.2 2.7 copy-start.7
  434.2 3.6 copy-start.8
  441.0 91.2 %copy-start.12 = (bf16[704,1024]{1,0:T(8,128)(2,1)S(1)}, bf16[704,1024]{1,0:T(8,128)(2,1)}, u32[]{:S(2)}) copy-start(bf16[704,1024]{1,0:T(8,128)(2,1)} %get-tuple-element.100) | copy-start | bytes 4325380
  532.2 2.9 copy-start.5
  535.1 3.3 copy-start.17
  535.1 4.1 copy-start.11
  539.2 1.9 copy-start.13
  542.7 2.9 copy-start.15
  542.7 4.6 copy-start.16
Sparse Core Ops, SparseCore 0:
  197.2 106.1 all-reduce.10
  307.8 106.0 all-reduce.8
  420.0 107.8 all-reduce.6
Sparse Core Ops, SparseCore 1:
  201.6 7.9 reduce-scatter.7
  212.3 13.1 reduce-scatter.3
  414.0 9.6 all-gather.1
  426.1 25.3 reduce-scatter.5

commit v2 on v1

--- a/solution.py
+++ b/solution.py
@@ -157,26 +157,10 @@
     )
 
 
-def greet(row, place, col, square=True):
+def greet(row, place, col, line=False, square=True):
     barrier = pltpu.get_barrier_semaphore()
-    if square:
-
-        @pl.when(row > 0)
-        def _():
-            pl.semaphore_signal(barrier, inc=1, device_id={"row": row - 1}, device_id_type=MESH)
-
-        @pl.when(row < ROWS - 1)
-        def _():
-            pl.semaphore_signal(barrier, inc=1, device_id={"row": row + 1}, device_id_type=MESH)
-
-        for step in range(1, SQUARE):
-            pl.semaphore_signal(
-                barrier, inc=1, device_id={"dp": partner(place, step)}, device_id_type=MESH
-            )
-        met = (
-            SQUARE - 1 + (row > 0).astype(jnp.int32) + (row < ROWS - 1).astype(jnp.int32)
-        )
-    else:
+    met = 1
+    if line:
         for step in range(1, ROWS):
             pl.semaphore_signal(
                 barrier,
@@ -184,9 +168,26 @@
                 device_id={"row": lax.rem(row + step, ROWS)},
                 device_id_type=MESH,
             )
-        met = ROWS - 1
+        met = met + ROWS - 1
+    else:
+
+        @pl.when(row > 0)
+        def _():
+            pl.semaphore_signal(barrier, inc=1, device_id={"row": row - 1}, device_id_type=MESH)
+
+        @pl.when(row < ROWS - 1)
+        def _():
+            pl.semaphore_signal(barrier, inc=1, device_id={"row": row + 1}, device_id_type=MESH)
+
+        met = met + (row > 0).astype(jnp.int32) + (row < ROWS - 1).astype(jnp.int32)
+    if square:
+        for step in range(1, SQUARE):
+            pl.semaphore_signal(
+                barrier, inc=1, device_id={"dp": partner(place, step)}, device_id_type=MESH
+            )
+        met = met + SQUARE - 1
     pl.semaphore_signal(barrier, inc=1, device_id={"col": 1 - col}, device_id_type=MESH)
-    pl.semaphore_wait(barrier, met + 1)
+    pl.semaphore_wait(barrier, met)
 
 
 class Line:
@@ -317,10 +318,10 @@
     sin_ref,
     key_cos_ref,
     key_sin_ref,
-    mark_rows_ref,
     mark_ref,
     cot_ref,
     route_ref,
+    router_ref,
     queries_ref,
     expand_ref,
     combine_ref,
@@ -341,6 +342,7 @@
     pick_ref,
     back_ref,
     rows_ref,
+    router_all,
     queries,
     expand,
     combine,
@@ -356,6 +358,7 @@
     coming,
     routes,
     staged,
+    marks,
     load_sem,
     stat_sent,
     stat_arrived,
@@ -381,6 +384,8 @@
     out_arrived,
     pair_sent,
     pair_arrived,
+    router_sent,
+    router_arrived,
 ):
     place, row, col = lax.axis_index("dp"), lax.axis_index("row"), lax.axis_index("col")
     other = 1 - col
@@ -462,6 +467,12 @@
         (compress_all.shape[0] - ROWS * sliced, width), bf16
     )
     comp_each(row, lambda copy: copy.start())
+
+    def router_copy(half):
+        here = router_all.at[:, pl.ds(pl.multiple_of(half * width, width), width)]
+        return remote(here, here, router_sent.at[0], router_arrived.at[0], sibling)
+
+    router_all[:, pl.ds(pl.multiple_of(col * width, width), width)] = router_ref[...]
     inputs = act_ref[...].astype(f32)
     scale_one = scale_of(inputs, 0)
     scale_one_ref[...] = scale_one
@@ -471,6 +482,10 @@
     cot_all[pl.ds(row, 1)] = cot_ref[...].reshape(1, tokens, width)
     routes[pl.ds(row, 1)] = route_ref[...].reshape((1,) + route_ref.shape)
     line.pass_on(row)
+    router_copy(col).start()
+    for block in range(ROWS):
+        mark = mark_ref[:, block * tokens : (block + 1) * tokens].astype(f32)
+        marks[block] = jnp.broadcast_to(mark, (8, tokens)).T
     loads[0].wait()
 
     def query_copy(block):
@@ -552,7 +567,7 @@
         chosen = []
         for shift in range(SQUARE):
             expert = partner(place, shift) * ROWS + row
-            hit = (routing[:TOP] == expert).astype(f32)
+            hit = (routing == expert).astype(f32)
             chosen.append(jnp.max(hit, axis=0, keepdims=True))
         goes = jnp.concatenate(chosen + chosen, axis=0)
         rank = nn(goes.astype(bf16), before)
@@ -625,7 +640,7 @@
 
     def attend(turn, carried):
         block = block_at(row, ROWS - 1 - turn)
-        visible = mark_ref[...] <= mark_rows_ref[block]
+        visible = mark_ref[...].astype(f32) <= marks[block][:, 0:1]
         for head in range(2):
             query = query_ref[block, :, head * NOPE : head * NOPE + lanes]
             scores = nt(query, key_ref[head].reshape(seq, lanes)) * score_scale
@@ -692,6 +707,8 @@
         return carried
 
     lax.fori_loop(0, ROWS, ended, 0)
+    router_copy(other).wait_recv()
+    router_copy(col).wait_send()
     stat_copy(0).wait_send()
     stat_copy(1).wait_send()
     sums.finish()
@@ -748,6 +765,7 @@
     segments,
     cotangent,
     routing,
+    router,
     tables,
     slots,
 ):
@@ -758,7 +776,7 @@
     latent_width = RANK + 128
     picked = SQUARE * slots
     lanes = NOPE + 2 * ROPE
-    routes = jnp.pad(routing.T, ((0, 8 - routing.shape[1]), (0, 0)), constant_values=-1)
+    routes = routing.T
     whole = pl.BlockSpec(memory_space=VMEM)
     far = pl.BlockSpec(memory_space=pl.ANY)
 
@@ -786,9 +804,10 @@
             shape(ROWS, picked, tokens),
             shape(ROWS, tokens, picked),
             shape(COLS, ROWS, picked, width),
+            shape(router.shape[1], COLS * width),
         ),
         in_specs=[whole] * 13 + [far] * 3,
-        out_specs=(whole,) * 17,
+        out_specs=(whole,) * 18,
         scratch_shapes=[
             VMEM(queries.shape, bf16),
             VMEM(expand.shape, bf16),
@@ -805,6 +824,7 @@
             VMEM((2, ROWS, tokens, width), bf16),
             VMEM((ROWS,) + routes.shape, jnp.int32),
             VMEM((ROWS, picked, width), bf16),
+            VMEM((ROWS, tokens, 8), f32),
             DMA((3,)),
             DMA((2,)),
             DMA((2,)),
@@ -819,6 +839,8 @@
             *line_sems(),
             *square_sems(),
             *pair_sems(),
+            DMA((1,)),
+            DMA((1,)),
         ],
         compiler_params=pltpu.CompilerParams(
             collective_id=1, has_side_effects=True, vmem_limit_bytes=56 * MIB
@@ -833,10 +855,10 @@
         rescale.reshape(1, RANK),
         premix.reshape(1, width),
         *tables,
-        segments.reshape(ROWS, tokens, 1),
         segments.reshape(1, seq),
         cotangent,
         routes,
+        router.T,
         queries,
         expand,
         combine,
@@ -931,7 +953,7 @@
         load.start()
     line = Line(row, branch_ref, line_sent, line_arrived)
     sums = SumLine(row, part, leaving, coming, sum_sent, sum_arrived)
-    greet(row, place, col, square=False)
+    greet(row, place, col, line=True, square=False)
 
     def stat_copy(index):
         return remote(
@@ -1287,10 +1309,10 @@
     rows_out,
     gu_out,
     hidden_out,
-    logit_out,
     shared_out,
     shared_gu_out,
     premix_ref,
+    router_rows,
     fan,
     fun,
     wide,
@@ -1334,7 +1356,7 @@
     slots = picked // SQUARE
     hid = fun.shape[0]
     share = narrow.shape[0]
-    experts = router_ref.shape[1]
+    experts = router_ref.shape[0]
     loads = [
         pltpu.make_async_copy(source, target, load_sem.at[i])
         for i, (source, target) in enumerate(
@@ -1352,6 +1374,7 @@
     greet(row, place, col)
     gathered_ref[pl.ds(row, 1)] = normed_ref[...].reshape(1, tokens, width)
     premix_ref[...] = jnp.zeros_like(premix_ref)
+    router_rows[...] = jnp.zeros_like(router_rows)
     line = Line(row, gathered_ref, line_sent, line_arrived)
     sums = SumLine(row, part, passed_to, passed_from, sum_sent, sum_arrived)
     sibling = {"col": other}
@@ -1431,8 +1454,8 @@
         slot = lax.rem(step, 2)
         for index, value in enumerate(
             (
-                nn(gathered_ref[block], wide[0]),
-                nn(gathered_ref[block], wide[1]),
+                nt(gathered_ref[block], wide[0]),
+                nt(gathered_ref[block], wide[1]),
                 nt(cot_ref[block], narrow[...]),
             )
         ):
@@ -1459,7 +1482,7 @@
         up_grad = (grad * act).astype(bf16)
         shared_gu_out[0, block] = gate_grad
         shared_gu_out[1, block] = up_grad
-        part[block] = nt(gate_grad, wide[0]) + nt(up_grad, wide[1])
+        part[block] = nn(gate_grad, wide[0]) + nn(up_grad, wide[1])
 
     def experts_of(step):
         block = block_at(row, step)
@@ -1471,7 +1494,7 @@
                 load.wait()
 
         left, right = rows[0, block], rows[1, block]
-        logits = nn(left, router_ref[0:width]) + nn(right, router_ref[width:])
+        logits = nt(left, router_ref[:, 0:width]) + nt(right, router_ref[:, width:])
         logits = logits - jnp.max(logits, axis=1, keepdims=True)
         weight = jnp.exp(logits)
         probs = weight / jnp.sum(weight, axis=1, keepdims=True)
@@ -1480,26 +1503,26 @@
         ).astype(f32)
         gates = jnp.sum(probs * own, axis=1, keepdims=True)
         raw = nt(cot_rows[0, block], fun[:, 0:width]) + nt(cot_rows[1, block], fun[:, width:])
-        gate = nn(left, fan[0, 0:width]) + nn(right, fan[0, width:])
-        up = nn(left, fan[1, 0:width]) + nn(right, fan[1, width:])
+        gate = nt(left, fan[0, :, 0:width]) + nt(right, fan[0, :, width:])
+        up = nt(left, fan[1, :, 0:width]) + nt(right, fan[1, :, width:])
         act, slope = silu_pair(gate)
         value = act * up
-        hidden[block] = value.astype(bf16)
+        hidden[block] = (value * gates).astype(bf16)
         gate_sum = gates * jnp.sum(value * raw, axis=1, keepdims=True)
         logit_grad = gate_sum * (own - probs)
-        logit_out[block, :, 0:experts] = logit_grad
-        logit_out[block, :, experts : experts + 1] = gates
         raw = raw * gates
         gu[0, block] = (raw * up * slope).astype(bf16)
         gu[1, block] = (raw * act).astype(bf16)
         logit_grad = logit_grad.astype(bf16)
+        router_rows[:, 0:width] += tn(logit_grad, left)
+        router_rows[:, width:] += tn(logit_grad, right)
 
         def half_of(half):
             lines = pl.ds(pl.multiple_of(half * width, width), width)
             return (
-                nt(gu[0, block], fan[0, lines])
-                + nt(gu[1, block], fan[1, lines])
-                + nt(logit_grad, router_ref[lines])
+                nn(gu[0, block], fan[0, :, lines])
+                + nn(gu[1, block], fan[1, :, lines])
+                + nn(logit_grad, router_ref[:, lines])
             )
 
         pair_to[block] = half_of(other).astype(bf16)
@@ -1577,7 +1600,7 @@
     picked = pick.shape[1]
     hid = fun.shape[0]
     share = narrow.shape[0]
-    experts = router_all.shape[1]
+    experts = router_all.shape[0]
     whole = pl.BlockSpec(memory_space=VMEM)
     far = pl.BlockSpec(memory_space=pl.ANY)
 
@@ -1593,10 +1616,10 @@
             shape(COLS, ROWS, picked, width),
             shape(2, ROWS, picked, hid),
             shape(ROWS, picked, hid),
-            shape(ROWS, picked, experts + 1, dtype=f32),
             shape(ROWS, tokens, share),
             shape(2, ROWS, tokens, share),
             shape(8, width, dtype=f32),
+            shape(experts, COLS * width, dtype=f32),
         ),
         in_specs=[whole, whole, whole, far, whole, far, far, far, far, whole],
         out_specs=(whole, whole, far, far, far, whole, whole, whole, whole),
@@ -1646,11 +1669,550 @@
     )(normed, pick, back, cot_rows, cot_all, fan, fun, wide, narrow, router_all)
 
 
-def swap_back(parts):
-    moves = [[(i, i ^ step) for i in range(SQUARE)] for step in range(SQUARE)]
-    return [parts[0]] + [
-        lax.ppermute(parts[step], "dp", moves[step]) for step in range(1, SQUARE)
+class SquareSum:
+    def __init__(self, place, part, first, second, middle, result, sent, arrived):
+        self.x, self.y = lax.rem(place, 2), lax.div(place, 2)
+        self.to_x, self.to_y = {"dp": partner(place, 1)}, {"dp": partner(place, 2)}
+        self.part, self.first, self.second = part, first, second
+        self.middle, self.result = middle, result
+        self.sent, self.arrived = sent, arrived
+
+    def copies(self, phase):
+        x, y = self.x, self.y
+        if phase == 0:
+            plan = (
+                (self.part.at[pl.ds(2 - 2 * x, 2)], self.first.at[0:2], self.to_x),
+                (self.part.at[pl.ds(6 - 2 * y, 2)], self.first.at[2:4], self.to_y),
+            )
+        elif phase == 1:
+            plan = (
+                (self.middle.at[0], self.second.at[0], self.to_y),
+                (self.middle.at[1], self.second.at[1], self.to_x),
+            )
+        elif phase == 2:
+            one, two = self.result.at[2 * x + y], self.result.at[4 + 2 * y + x]
+            plan = ((one, one, self.to_y), (two, two, self.to_x))
+        else:
+            one, two = self.result.at[pl.ds(2 * x, 2)], self.result.at[pl.ds(4 + 2 * y, 2)]
+            plan = ((one, one, self.to_x), (two, two, self.to_y))
+        return [
+            remote(source, target, self.sent.at[2 * phase + i], self.arrived.at[2 * phase + i], to)
+            for i, (source, target, to) in enumerate(plan)
+        ]
+
+    def start(self, phase):
+        for copy in self.copies(phase):
+            copy.start()
+
+    def arrive(self, phase):
+        for copy in self.copies(phase):
+            copy.wait_recv()
+
+    def run(self, phase):
+        x, y = self.x, self.y
+        if phase > 0:
+            self.arrive(phase - 1)
+        if phase == 1:
+            for slot, piece, came in (
+                (0, 2 * x + 1 - y, 1 - y),
+                (1, 4 + 2 * y + 1 - x, 3 - x),
+            ):
+                self.middle[slot] = (
+                    self.part[piece].astype(f32) + self.first[came].astype(f32)
+                ).astype(bf16)
+        if phase == 2:
+            for slot, piece, came in ((0, 2 * x + y, y), (1, 4 + 2 * y + x, 2 + x)):
+                self.result[piece] = (
+                    self.part[piece].astype(f32)
+                    + self.first[came].astype(f32)
+                    + self.second[slot].astype(f32)
+                ).astype(bf16)
+        if phase < 4:
+            self.start(phase)
+
+    def finish(self):
+        for phase in range(4):
+            for copy in self.copies(phase):
+                copy.wait_send()
+
+
+def square_scratch(dims):
+    count, rows, lanes = dims
+    return [
+        VMEM((count, 8, rows, lanes), bf16),
+        VMEM((count, 4, rows, lanes), bf16),
+        VMEM((count, 2, rows, lanes), bf16),
+        VMEM((count, 2, rows, lanes), bf16),
+        VMEM((count, 8, rows, lanes), bf16),
+        DMA((count, 8)),
+        DMA((count, 8)),
     ]
+
+
+def finish_kernel(
+    own_latent_ref,
+    back_ref,
+    shared_ref,
+    residual_ref,
+    premix_rows,
+    scaling_rows,
+    rescale_rows,
+    router_rows,
+    premix_ref,
+    scaling_ref,
+    hidden_ref,
+    funnel_ref,
+    one_ref,
+    query_grad_ref,
+    attended_ref,
+    branch_ref,
+    latent_ref,
+    expanded_ref,
+    narrow_ref,
+    output_ref,
+    queries_out,
+    combine_out,
+    expand_out,
+    compress_out,
+    small_ref,
+    hidden,
+    funnel,
+    one,
+    query_grad,
+    attended,
+    branch,
+    latent,
+    expanded,
+    narrow,
+    reply_own,
+    reply_to,
+    reply_from,
+    staged,
+    home,
+    part,
+    leaving,
+    coming,
+    total,
+    queries_wide,
+    combine_wide,
+    expand_wide,
+    compress_wide,
+    small_to,
+    small_from,
+    small_line,
+    small_square,
+    small_own,
+    load_sem,
+    store_sem,
+    reply_sent,
+    reply_arrived,
+    home_sent,
+    home_arrived,
+    sum_sent,
+    sum_arrived,
+    pair_sent,
+    pair_arrived,
+    small_sent,
+    small_arrived,
+    *sums_scratch,
+):
+    place, row, col = lax.axis_index("dp"), lax.axis_index("row"), lax.axis_index("col")
+    other = 1 - col
+    sibling = {"col": other}
+    tokens, width = output_ref.shape
+    seq = ROWS * tokens
+    picked = back_ref.shape[2]
+    slots = picked // SQUARE
+    experts = router_rows.shape[0]
+    loads = [
+        pltpu.make_async_copy(source, target, load_sem.at[i])
+        for i, (source, target) in enumerate(
+            [
+                (funnel_ref, funnel),
+                (hidden_ref, hidden),
+                (one_ref, one),
+                (query_grad_ref, query_grad),
+                (attended_ref, attended),
+                (branch_ref, branch),
+                (latent_ref, latent),
+                (expanded_ref, expanded),
+                (narrow_ref, narrow),
+            ]
+        )
+    ]
+    for load in loads:
+        load.start()
+    greet(row, place, col, line=True, square=True)
+    line_sums = SumLine(row, part, leaving, coming, sum_sent, sum_arrived)
+
+    def reply_copy(block):
+        return remote(
+            reply_to.at[block],
+            reply_from.at[block],
+            reply_sent.at[block],
+            reply_arrived.at[block],
+            sibling,
+        )
+
+    def home_copy(block, step):
+        piece = pl.ds(step * slots, slots)
+        return remote(
+            staged.at[block, piece],
+            home.at[block, piece],
+            home_sent.at[block, step],
+            home_arrived.at[block, step],
+            {"dp": partner(place, step)},
+        )
+
+    def reply(turn):
+        block = block_at(row, ROWS - 1 - turn)
+        value = hidden[block]
+        reply_to[block] = nn(
+            value, funnel[:, pl.ds(pl.multiple_of(other * width, width), width)]
+        ).astype(bf16)
+        reply_copy(block).start()
+        reply_own[lax.rem(turn, 2)] = nn(
+            value, funnel[:, pl.ds(pl.multiple_of(col * width, width), width)]
+        )
+
+    def reply_home(turn):
+        block = block_at(row, ROWS - 1 - turn)
+        reply_copy(block).wait_recv()
+        staged[block] = (
+            reply_own[lax.rem(turn, 2)] + reply_from[block].astype(f32)
+        ).astype(bf16)
+        for shift in (3, 2, 1):
+            home_copy(block, shift).start()
+        home[block, 0:slots] = staged[block, 0:slots]
+
+    def reply_add(turn, carried):
+        block = block_at(row, ROWS - 1 - turn)
+        for shift in range(1, SQUARE):
+            home_copy(block, shift).wait_recv()
+        part[block] = nn(back_ref[block], home[block]) + nn(shared_ref[block], narrow[...])
+        line_sums.begin(block)
+        return carried
+
+    loads[0].wait()
+    loads[1].wait()
+
+    def replies(turn, carried):
+        @pl.when(turn < ROWS)
+        def _():
+            reply(turn)
+
+        @pl.when(turn > 0)
+        def _():
+            reply_home(turn - 1)
+
+        return carried
+
+    lax.fori_loop(0, ROWS + 1, replies, 0)
+
+    kinds = [sums_scratch[7 * i : 7 * i + 7] for i in range(4)]
+    sums = []
+    for scratch in kinds:
+        for index in range(scratch[0].shape[0]):
+            sums.append(SquareSum(place, *[ref.at[index] for ref in scratch]))
+    parts = [scratch[0] for scratch in kinds]
+    counts = [ref.shape[0] for ref in parts]
+    for load in loads[2:4]:
+        load.wait()
+    index = 0
+    for chunk in range(counts[0]):
+        height = 8 * parts[0].shape[2]
+        tokens_here = one[:, :, chunk * height : (chunk + 1) * height].reshape(seq, height)
+        grad = tn(tokens_here, query_grad[...].reshape(seq, query_grad.shape[2]))
+        parts[0][chunk] = grad.astype(bf16).reshape(parts[0].shape[1:])
+        sums[index].run(0)
+        index += 1
+    loads[4].wait()
+    loads[5].wait()
+    for chunk in range(counts[1]):
+        height = 8 * parts[1].shape[2]
+        tokens_here = attended[:, :, chunk * height : (chunk + 1) * height].reshape(seq, height)
+        grad = tn(tokens_here, branch[...].reshape(seq, width))
+        parts[1][chunk] = grad.astype(bf16).reshape(parts[1].shape[1:])
+        sums[index].run(0)
+        index += 1
+    loads[6].wait()
+    loads[7].wait()
+    grad = tn(latent[...].reshape(seq, RANK), expanded[...].reshape(seq, expanded.shape[2]))
+    parts[2][0] = grad.astype(bf16).reshape(parts[2].shape[1:])
+    sums[index].run(0)
+    index += 1
+    grad = nn(own_latent_ref[...], one[...].reshape(seq, width)).astype(bf16)
+    for piece in range(8):
+        parts[3][0, piece] = grad[:, piece * (width // 8) : (piece + 1) * (width // 8)]
+    sums[index].run(0)
+
+    def small_copy(step):
+        if step == 0:
+            return remote(small_to, small_from, small_sent.at[0], small_arrived.at[0], sibling)
+        if step < ROWS:
+            return remote(
+                small_own,
+                small_line.at[step],
+                small_sent.at[step],
+                small_arrived.at[step],
+                {"row": lax.rem(row + step, ROWS)},
+            )
+        shift = step - ROWS + 1
+        return remote(
+            small_ref,
+            small_square.at[shift],
+            small_sent.at[step],
+            small_arrived.at[step],
+            {"dp": partner(place, shift)},
+        )
+
+    rescale_row = jnp.sum(rescale_rows[...], axis=0, keepdims=True)
+    empty = jnp.zeros((small_own.shape[0] - experts, width), f32)
+    small_to[0:experts] = router_rows[:, pl.ds(pl.multiple_of(other * width, width), width)]
+    small_to[experts:] = empty
+    small_to[experts + 2 : experts + 3, 0:RANK] = rescale_row
+    small_copy(0).start()
+    small_own[0:experts] = router_rows[:, pl.ds(pl.multiple_of(col * width, width), width)]
+    small_own[experts:] = empty
+    small_own[experts : experts + 1] = (
+        jnp.sum(premix_rows[...], axis=0, keepdims=True) / premix_ref[...]
+    )
+    small_own[experts + 1 : experts + 2] = (
+        jnp.sum(scaling_rows[...], axis=0, keepdims=True) / scaling_ref[...]
+    )
+    small_own[experts + 2 : experts + 3, 0:RANK] = rescale_row
+    small_copy(0).wait_recv()
+    small_own[...] += small_from[...]
+    for step in range(1, ROWS):
+        small_copy(step).start()
+
+    loads[8].wait()
+    lax.fori_loop(0, ROWS, reply_add, 0)
+
+    def line_pass(turn, carried):
+        line_sums.pass_on(block_at(row, jnp.where(turn == 0, 3, turn)))
+        return carried
+
+    stores = []
+
+    def store(source, target):
+        copy = pltpu.make_async_copy(source, target, store_sem.at[len(stores)])
+        copy.start()
+        stores.append(copy)
+
+    def pair_copy(half):
+        here = expand_wide.at[half]
+        return remote(here, here, pair_sent.at[0], pair_arrived.at[0], sibling)
+
+    def put(index):
+        kind, chunk = 0, index
+        while chunk >= counts[kind]:
+            chunk -= counts[kind]
+            kind += 1
+        result = kinds[kind][4][chunk]
+        pieces, rows, lanes = result.shape
+        if kind < 2:
+            wide, out = ((queries_wide, queries_out), (combine_wide, combine_out))[kind]
+            here = pl.ds(chunk * pieces * rows, pieces * rows)
+            wide[here] = result.astype(f32).reshape(pieces * rows, lanes)
+            store(wide.at[here], out.at[here])
+        elif kind == 2:
+            expand_wide[col] = result.astype(f32).reshape(pieces * rows, lanes)
+            pair_copy(col).start()
+        else:
+            for piece in range(pieces):
+                compress_wide[:, piece * lanes : (piece + 1) * lanes] = result[piece].astype(f32)
+            store(compress_wide, compress_out)
+
+    count = len(sums)
+    small_steps = {
+        2: "line",
+        count + 2: "square",
+    }
+    for turn in range(count + 6):
+        if turn < count:
+            sums[turn].run(1)
+        if turn == 1:
+            lax.fori_loop(0, 3, line_pass, 0)
+        if 0 <= turn - 2 < count:
+            sums[turn - 2].run(2)
+        if 0 <= turn - 4 < count:
+            sums[turn - 4].run(3)
+        if 0 <= turn - 6 < count:
+            sums[turn - 6].run(4)
+            put(turn - 6)
+        if small_steps.get(turn) == "line":
+            for step in range(1, ROWS):
+                small_copy(step).wait_recv()
+            small_ref[...] = (
+                small_own[...] + small_line[1] + small_line[2] + small_line[3]
+            )
+            for step in range(ROWS, ROWS + SQUARE - 1):
+                small_copy(step).start()
+            line_sums.total(total)
+            output_ref[...] = (total[...] + residual_ref[...]).astype(bf16)
+        if small_steps.get(turn) == "square":
+            for step in range(ROWS, ROWS + SQUARE - 1):
+                small_copy(step).wait_recv()
+            for step in range(ROWS, ROWS + SQUARE - 1):
+                small_copy(step).wait_send()
+            small_ref[...] += small_square[1] + small_square[2] + small_square[3]
+
+    pair_copy(other).wait_recv()
+    store(expand_wide.at[0], expand_out.at[:, 0 : expand_wide.shape[2]])
+    store(expand_wide.at[1], expand_out.at[:, expand_wide.shape[2] :])
+    for copy in stores:
+        copy.wait()
+    pair_copy(col).wait_send()
+    for step in range(ROWS):
+        small_copy(step).wait_send()
+    for one_sum in sums:
+        one_sum.finish()
+    line_sums.finish()
+
+    def ended(block, carried):
+        reply_copy(block).wait_send()
+        for shift in range(1, SQUARE):
+            home_copy(block, shift).wait_send()
+        return carried
+
+    lax.fori_loop(0, ROWS, ended, 0)
+
+
+def run_finish(
+    own_latent,
+    back,
+    shared,
+    residual,
+    premix_rows,
+    scaling_rows,
+    rescale_rows,
+    router_rows,
+    premix,
+    scaling,
+    hidden,
+    funnel,
+    one,
+    query_grad,
+    attended,
+    branch,
+    latent,
+    expanded,
+    narrow,
+):
+    tokens, width = residual.shape
+    picked = back.shape[2]
+    sliced = own_latent.shape[0]
+    wide = query_grad.shape[2]
+    heads = attended.shape[2]
+    own_heads = expanded.shape[2]
+    small = (24, width)
+    whole = pl.BlockSpec(memory_space=VMEM)
+    far = pl.BlockSpec(memory_space=pl.ANY)
+
+    def shape(*dims, dtype=f32):
+        return jax.ShapeDtypeStruct(dims, dtype)
+
+    loaded = (hidden, funnel, one, query_grad, attended, branch, latent, expanded, narrow)
+    return pl.pallas_call(
+        finish_kernel,
+        name="finish",
+        out_shape=(
+            shape(tokens, width, dtype=bf16),
+            shape(width, wide),
+            shape(heads, width),
+            shape(RANK, COLS * own_heads),
+            shape(sliced, width),
+            shape(*small),
+        ),
+        in_specs=[whole] * 10 + [far] * 9,
+        out_specs=(whole, far, far, far, far, whole),
+        scratch_shapes=[
+            *[VMEM(value.shape, bf16) for value in loaded],
+            VMEM((2, picked, width), f32),
+            VMEM((ROWS, picked, width), bf16),
+            VMEM((ROWS, picked, width), bf16),
+            VMEM((ROWS, picked, width), bf16),
+            VMEM((ROWS, picked, width), bf16),
+            VMEM((ROWS, tokens, width), f32),
+            VMEM((ROWS, tokens, width), bf16),
+            VMEM((2, ROWS, tokens, width), bf16),
+            VMEM((tokens, width), f32),
+            VMEM((width, wide), f32),
+            VMEM((heads, width), f32),
+            VMEM((COLS, RANK, own_heads), f32),
+            VMEM((sliced, width), f32),
+            VMEM(small, f32),
+            VMEM(small, f32),
+            VMEM((ROWS,) + small, f32),
+            VMEM((SQUARE,) + small, f32),
+            VMEM(small, f32),
+            DMA((len(loaded),)),
+            DMA((10,)),
+            *pair_sems(),
+            *square_sems(),
+            *sum_sems(),
+            DMA((1,)),
+            DMA((1,)),
+            DMA((ROWS + SQUARE - 1,)),
+            DMA((ROWS + SQUARE - 1,)),
+            *square_scratch((4, width // 32, wide)),
+            *square_scratch((2, heads // 16, width)),
+            *square_scratch((1, RANK // 8, own_heads)),
+            *square_scratch((1, sliced, width // 8)),
+        ],
+        compiler_params=pltpu.CompilerParams(
+            collective_id=4, has_side_effects=True, vmem_limit_bytes=60 * MIB
+        ),
+        cost_estimate=pl.CostEstimate(
+            flops=40 * 1024**3, bytes_accessed=64 * MIB, transcendentals=0
+        ),
+    )(
+        own_latent,
+        back,
+        shared,
+        residual,
+        premix_rows,
+        scaling_rows,
+        rescale_rows,
+        router_rows,
+        premix.reshape(1, width),
+        scaling.reshape(1, width),
+        *loaded,
+    )
+
+
+def product_kernel(left_ref, right_ref, out_ref):
+    wide = 256
+
+    def one(index, carried):
+        lanes = pl.ds(pl.multiple_of(index * wide, 128), wide)
+        out_ref[0, :, lanes] = tn(left_ref[0], right_ref[0, :, lanes])
+        return carried
+
+    lax.fori_loop(0, right_ref.shape[2] // wide, one, 0)
+
+
+def slot_products(left, right):
+    kinds, slots, tall = left.shape
+    halves, _, wide = right.shape
+    return pl.pallas_call(
+        product_kernel,
+        name="slot_products",
+        grid=(kinds, halves),
+        out_shape=jax.ShapeDtypeStruct((kinds, tall, halves * wide), f32),
+        in_specs=[
+            pl.BlockSpec((1, slots, tall), lambda kind, half: (kind, 0, 0)),
+            pl.BlockSpec((1, slots, wide), lambda kind, half: (half, 0, 0)),
+        ],
+        out_specs=pl.BlockSpec((1, tall, wide), lambda kind, half: (kind, 0, half)),
+        compiler_params=pltpu.CompilerParams(vmem_limit_bytes=40 * MIB),
+        cost_estimate=pl.CostEstimate(
+            flops=2 * kinds * halves * slots * tall * wide,
+            bytes_accessed=4 * kinds * halves * tall * wide,
+            transcendentals=0,
+        ),
+    )(left, right)
 
 
 def local_square(
@@ -1681,7 +2243,6 @@
     capacity = local_rows * TOP * 4 // (3 * expert_total)
     slot_total = capacity * row_count * dp_count
     tables = turning_tables(seq_length)
-    router_all = col_gather(router)
     (
         one,
         query,
@@ -1700,6 +2261,7 @@
         pick,
         back,
         cot_rows,
+        router_all,
     ) = run_attention(
         activations,
         scaling,
@@ -1712,6 +2274,7 @@
         segments,
         cotangent,
         routing,
+        router,
         tables,
         capacity,
     )
@@ -1721,19 +2284,19 @@
         expert_rows,
         expert_gu_grad,
         expert_hidden,
-        slot_values,
         hidden_blocks,
         gu_blocks,
         premix_rows,
+        router_rows,
     ) = run_experts(
         normed_two,
         pick,
         back,
         cot_rows,
         cot_blocks,
-        fanout[0],
+        fanout[0].transpose(0, 2, 1),
         funnel[0],
-        widening,
+        widening.transpose(0, 2, 1),
         narrowing,
         router_all,
     )
@@ -1745,12 +2308,10 @@
     reply_grad_rows = cot_rows.reshape(col_count, slot_total, col_width)
     slot_hidden = expert_hidden.reshape(slot_total, -1)
     slot_gu_grad = expert_gu_grad.reshape(2, slot_total, -1)
-    slot_values = slot_values.reshape(slot_total, -1)
-    logit_grad = slot_values[:, :expert_total].astype(bf16)
-    slot_gates = slot_values[:, expert_total]
-
     narrowing_grad = dot_tn(hidden_all, cotangent_all)
-    widening_grad = jnp.stack([dot_tn(gathered_two, gu_grad_all[i]) for i in range(2)])
+    widening_grad = jnp.einsum(
+        "gtf,td->gfd", gu_grad_all, gathered_two, preferred_element_type=f32
+    )
     shared_sums = lax.psum((narrowing_grad.astype(bf16), widening_grad.astype(bf16)), "dp")
     (
         input_grad,
@@ -1782,66 +2343,46 @@
         expand,
         combine,
     )
-    gathered_one = one.reshape(seq_length, col_width)
-    attended_all = attended.reshape(seq_length, -1)
-    late_parts = (
-        dot_tn(gathered_one, query_grad.reshape(seq_length, -1)).astype(bf16),
-        dot_tn(
-            latent_normed.reshape(seq_length, -1), expanded_grad.reshape(seq_length, -1)
-        ).astype(bf16),
-        dot(own_latent_grad, gathered_one).astype(bf16),
-        dot_tn(attended_all, branch_blocks.reshape(seq_length, col_width)).astype(bf16),
-    )
-    late_parts = (after(late_parts[0], *shared_sums),) + late_parts[1:]
-    queries_sum, expand_sum, compress_sum, combine_sum = lax.psum(late_parts, "dp")
-
-    scaled_hidden = (slot_hidden.astype(f32) * slot_gates[:, None]).astype(bf16)
-    reply_part = dot(scaled_hidden, funnel[0])
-    summed = col_scatter(reply_part.astype(bf16), axis=1)
-    summed = summed.reshape(row_count, dp_count, capacity, col_width)
-    returned = jnp.stack(swap_back([summed[:, k] for k in range(dp_count)]), axis=1)
-    routed = jnp.einsum(
-        "bts,bsd->btd",
+    fanout_grad = slot_products(slot_gu_grad, slot_rows)
+    funnel_grad = slot_products(slot_hidden[None], reply_grad_rows)
+    own_latent_grad, fanout_grad, funnel_grad = lax.optimization_barrier(
+        (own_latent_grad, fanout_grad, funnel_grad)
+    )
+    layer_output, queries_sum, combine_sum, expand_sum, compress_sum, small = run_finish(
+        own_latent_grad,
         back,
-        returned.reshape(row_count, dp_count * capacity, col_width),
-        preferred_element_type=f32,
-    ).reshape(seq_length, col_width)
-    shared_out = row_scatter(routed + dot(hidden_all, narrowing))
-    layer_output = (residual + shared_out).astype(bf16)
-
-    funnel_grad = jnp.concatenate(
-        [dot_tn(scaled_hidden, reply_grad_rows[i]) for i in range(col_count)], axis=1
-    )[None]
-    fanout_grad = jnp.stack(
-        [
-            jnp.concatenate([dot_tn(slot_rows[i], slot_gu_grad[j]) for i in range(col_count)])
-            for j in range(2)
-        ]
-    )[None]
-
-    router_part = jnp.concatenate([dot_tn(slot_rows[i], logit_grad) for i in range(col_count)])
-    router_part = col_scatter(router_part)
-    premix_part = jnp.sum(premix_rows, axis=0) / premix
-    scaling_part = jnp.sum(scaling_rows, axis=0) / scaling
-    rescale_part = col_totals(jnp.sum(rescale_rows, axis=0))
-    small = jnp.concatenate(
-        [premix_part, scaling_part, rescale_part, router_part.reshape(-1)]
-    )
-    small = lax.psum(small, ("dp", "row"))
+        hidden_blocks,
+        residual,
+        premix_rows,
+        scaling_rows,
+        rescale_rows,
+        router_rows,
+        premix,
+        scaling,
+        expert_hidden,
+        funnel[0],
+        one,
+        query_grad,
+        attended,
+        branch_blocks,
+        latent_normed,
+        expanded_grad,
+        narrowing,
+    )
     return (
         layer_output,
         input_grad,
-        small[col_width : 2 * col_width],
-        queries_sum.astype(f32),
-        compress_sum.T.astype(f32),
-        small[2 * col_width : 2 * col_width + RANK],
-        col_gather(expand_sum, axis=1).astype(f32),
-        combine_sum.astype(f32),
-        small[:col_width],
-        small[2 * col_width + RANK :].reshape(col_width, expert_total),
-        shared_sums[1].astype(f32),
+        small[expert_total + 1],
+        queries_sum,
+        compress_sum.T,
+        small[expert_total + 2, :RANK],
+        expand_sum,
+        combine_sum,
+        small[expert_total],
+        small[:expert_total].T,
+        shared_sums[1].astype(f32).transpose(0, 2, 1),
         shared_sums[0].astype(f32),
-        fanout_grad,
+        fanout_grad.transpose(0, 2, 1)[None],
         funnel_grad,
     )
 

time: 565 us -> 395 us (0.70); the launches traced: 556 us -> 394 us
  waiting for transfers between devices: 182 us -> 0.02 us
  Pallas kernels: 228 us -> 350 us
  matrix products: 44.5 us -> 6.61 us
  other arithmetic: 34.9 us -> 7.12 us
  local copies, waits for them, and re-layouts: 41.4 us -> 15.6 us
    psum x2 -> x0, waiting for transfers between devices: 163 us -> none  [the longest x1 85.2 us: local_square(): lax.psum(late_parts, 'dp')]
    pallas_call x0 -> x3, Pallas kernels: none -> 125 us  [the longest x1 106 us: run_finish(): pl.pallas_call(finish_kernel, name='finish', out_shape=(shape(tokens, wid...]
    dot_general x14 -> x1, matrix products: 35 us -> 3.33 us  [dot_tn(): lax.dot_general(left, right, (((0,), (0,)), ((), ())), preferred_element_...]
    psum x1, waiting for transfers between devices: 19.1 us -> 0.01 us  [local_square(): lax.psum((narrowing_grad.astype(bf16), widening_grad.astype(bf16)), 'dp')]
    unnamed x76 -> x34, local copies, waits for them, and re-layouts: 28.5 us -> 11.4 us
    broadcast_in_dim x2 -> x0, other arithmetic: 12.5 us -> none  [the longest x1 8.89 us: local_square(): jnp.stack([jnp.concatenate([dot_tn(slot_rows[i], slot_gu_grad[j]) for i i...]
    convert_element_type x7 -> x0, other arithmetic: 12.5 us -> none  [the longest x1 3.25 us: local_square(): shared_sums[1].astype(f32)]
    another operation x3 -> x0, other arithmetic: 6.5 us -> none  [the longest x1 3.21 us: local_square(): jnp.stack([jnp.concatenate([dot_tn(slot_rows[i], slot_gu_grad[j]) for i i...]
  transfers between devices with their start and end apart: 10 -> 1, of which waited for: 3 -> 0; matrix products, arithmetic and copies ran while one was open for 15% -> 1% of each run, Pallas kernels for 12% -> 49%
where the time goes in v2:
time: 395 us; the launch traced here: 394 us
  Pallas kernels  350 us (89%)
  local copies, waits for them, and re-layouts  15.6 us (4%)
  between operations  14.1 us (4%)
  other arithmetic  7.12 us (2%)
  matrix products  6.61 us (2%)
    pallas_call x1, Pallas kernels, run_finish(): pl.pallas_call(finish_kernel, name='finish', out_shape=(shape(tokens, wid...  106 us
    pallas_call x1, Pallas kernels, run_experts(): pl.pallas_call(expert_kernel, name='experts', out_shape=(shape(tokens, wi...  81.9 us
    pallas_call x1, Pallas kernels, run_attention(): pl.pallas_call(attend_kernel, name='attend', out_shape=(shape(ROWS, token...  76 us
    pallas_call x1, Pallas kernels, run_attention_back(): pl.pallas_call(attend_back_kernel, name='attend_back', out_shape=(shape(t...  67.2 us
    pallas_call x2, Pallas kernels, slot_products(): pl.pallas_call(product_kernel, name='slot_products', grid=(kinds, halves)...  18.5 us
    unnamed x34, local copies, waits for them, and re-layouts  11.4 us
  transfers between devices with their start and end apart: 1, of which 0 were waited for; matrix products, arithmetic and copies ran while one was open for 1% of the time, Pallas kernels for 49%

profile of v2, /device:TPU:9, one launch (start us, length us, event | category | flops | bytes accessed | tf_op | source)
XLA Modules:
  0.0 393.5 jit_solution(3519630689887831371)
XLA Ops:
  7.2 0.0 all-reduce.3.cloned.1.call-start
  7.2 76.0 %attend.1 = (bf16[4,128,1024]{2,1,0:T(8,128)(2,1)}, bf16[4,128,384]{2,1,0:T(8,128)(2,1)}, bf16[2,4,128,256]{3,2,1,0:T(8,128)(2,1)}, bf16[2,4,128,128]{3,2,1,0:T(...) custom-call(bf16[128,1024]{1,0:T(8,128)(2,1)} %act_ref.3, ...), custom_call_target="tpu_custom_call" | custom-call | flops 42949672960 | bytes 33554432 | tf_op jit(solution)/shard_map/attend/pallas_call | solution.py:786
  83.3 0.0 copy-start.12
  83.3 81.9 %experts.1 = (f32[128,1024]{1,0:T(8,128)}, bf16[4,128,1024]{2,1,0:T(8,128)(2,1)}, bf16[2,4,256,1024]{3,2,1,0:T(8,128)(2,1)}, bf16[2,4,256,704]{3,2,1,0:T(8,128)(...) custom-call(bf16[128,1024]{1,0:T(8,128)(2,1)} %get-tuple-element.57., ...), custom_call_target="tpu_custom_call" | custom-call | flops 64424509440 | bytes 67108864 | tf_op jit(solution)/shard_map/experts/pallas_call | solution.py:1610
  165.2 0.0 copy-done.12
  165.2 0.0 copy-start.11
  165.2 0.0 copy-start.13
  165.2 3.3 bitcast_convert_fusion.1
  168.5 0.0 copy-done.11
  168.5 0.0 copy-done.13
  168.5 3.3 fusion
  171.8 0.0 all-reduce.3.cloned.1.call-update
  171.8 0.0 copy-start.2
  171.8 2.2 copy-done.2
  174.0 0.0 copy-start.3
  174.0 1.9 copy-done.3
  175.9 0.0 copy-start
  175.9 0.0 copy-start.1
  175.9 11.8 %slot_products.2 = f32[2,704,2048]{2,1,0:T(8,128)} custom-call(bf16[2,1024,704]{2,1,0:T(8,128)(2,1)S(1)} %bitcast.43, bf16[2,1024,1024]{2,1,0:T(8,128)(2,1)S(1)} %bitcast.42), custom_call_target="tpu_custom_call" | custom-call | flops 5905580032 | bytes 11534336 | tf_op jit(solution)/shard_map/slot_products/pallas_call | solution.py:2199
  187.7 0.0 copy-done
  187.7 0.0 copy-done.1
  187.7 6.7 %slot_products.3 = f32[1,704,2048]{2,1,0:T(8,128)} custom-call(bf16[1,1024,704]{2,1,0:T(8,128)(2,1)S(1)} %bitcast.41, bf16[2,1024,1024]{2,1,0:T(8,128)(2,1)S(1)} %bitcast.40), custom_call_target="tpu_custom_call" | custom-call | flops 2952790016 | bytes 5767168 | tf_op jit(solution)/shard_map/slot_products/pallas_call | solution.py:2199
  194.4 67.2 %attend_back.1 = (f32[128,1024]{1,0:T(8,128)}, bf16[4,128,1024]{2,1,0:T(8,128)(2,1)}, bf16[4,128,768]{2,1,0:T(8,128)(2,1)}, bf16[4,128,512]{2,1,0:T(8,128)(2,1)}...) custom-call(f32[128,1024]{1,0:T(8,128)} %get-tuple-element.63.normed_grad_ref, ...), custom_call_target="tpu_custom_call" | custom-call | flops 42949672960 | bytes 33554432 | tf_op jit(solution)/shard_map/attend_back/pallas_call | solution.py:1216
  261.6 106.4 %finish.1 = (bf16[128,1024]{1,0:T(8,128)(2,1)}, f32[1024,768]{1,0:T(8,128)}, f32[512,1024]{1,0:T(8,128)}, f32[512,1024]{1,0:T(8,128)}, f32[144,1024]{1,0:T(8,128)}, /*index=5*/f32[24,1024]{1,0:T(8,128)}) custom-call(bf16[144,512]{1,0:T(8,128)(2,1)} %get-tuple-element.78.own_latent_ref, bf16[4,128,256]{2,1,0:T(8,128)(2,1)} %get-tuple-element.59.back_ref, ...), custom_call_target="tpu_custom_call" | custom-call | flops 42949672960 | bytes 67108864 | tf_op jit(solution)/shard_map/finish/pallas_call | solution.py:2117
  368.0 1.3 slice.13
  369.3 1.4 fusion.2
  370.8 1.5 slice_bitcast_fusion
  372.2 0.0 all-reduce.3.cloned.1.call-done
  372.3 0.0 copy-start.7
  372.3 5.2 %transpose.38 = f32[2,1024,704]{1,2,0:T(8,128)} convert(bf16[2,1024,704]{1,2,0:T(8,128)(2,1)} %get-tuple-element.100) | non-fusion elementwise | flops 1441792 | bytes 8650752 | tf_op jit(solution)/shard_map/transpose | solution.py:2383
  377.4 0.0 copy-start.10
  377.4 0.0 copy-start.9
  377.4 0.0 copy-done.7
  377.4 0.0 copy-start.4
  377.4 1.9 convert_element_type.12
  379.4 0.0 copy-done.10
  379.4 0.7 copy.47
  380.1 0.0 copy-done.9
  380.1 0.8 copy.48
  380.9 0.0 copy-done.4
  380.9 0.0 copy-start.8
  380.9 1.7 copy.49
  382.6 0.0 copy-done.8
  382.6 0.8 copy.50
  383.4 0.6 copy-done.6
  384.0 1.3 copy.51
  385.3 0.0 copy-done.5
  385.3 1.3 copy.52
  (2 shorter events, 0.0 us)
Async XLA Ops:
  7.2 365.1 %all-reduce.3.cloned.1.call-start = ((), (), s32[]{:S(2)}) async-start(), calls=%async_computation | async-start | bytes 8650752 | tf_op jit(solution)/shard_map/psum | solution.py:2315
  83.3 81.9 %copy-start.12 = (bf16[4,128,1024]{2,1,0:T(8,128)(2,1)S(1)}, bf16[4,128,1024]{2,1,0:T(8,128)(2,1)}, u32[]{:S(2)}) copy-start(bf16[4,128,1024]{2,1,0:T(8,128)(2,1)} %get-tuple-element.61.cot_ref) | copy-start | bytes 3145732
  165.2 3.3 copy-start.11
  165.2 3.3 copy-start.13
  171.8 2.2 copy-start.2
  174.0 1.9 copy-start.3
  175.9 11.8 %copy-start = (bf16[2,4,256,1024]{3,2,1,0:T(8,128)(2,1)S(1)}, bf16[2,4,256,1024]{3,2,1,0:T(8,128)(2,1)}, u32[]{:S(2)}) copy-start(bf16[2,4,256,1024]{3,2,1,0:T(8,128)(2,1)} %get-tuple-element.60.cot_rows_ref) | copy-start | bytes 12582916
  175.9 11.8 %copy-start.1 = (bf16[4,256,704]{2,1,0:T(8,128)(2,1)S(1)}, bf16[4,256,704]{2,1,0:T(8,128)(2,1)}, u32[]{:S(2)}) copy-start(bf16[4,256,704]{2,1,0:T(8,128)(2,1)} %get-tuple-element.77.hidden_ref) | copy-start | bytes 4325380
  372.3 5.2 %copy-start.7 = (bf16[704,1024]{1,0:T(8,128)(2,1)S(1)}, bf16[704,1024]{1,0:T(8,128)(2,1)}, u32[]{:S(2)}) copy-start(bf16[704,1024]{1,0:T(8,128)(2,1)} %get-tuple-element.101) | copy-start | bytes 4325380
  377.4 2.0 copy-start.10
  377.4 2.7 copy-start.9
  377.4 3.5 copy-start.4
  380.9 1.7 copy-start.8
  380.9 3.1 copy-start.6
  382.6 2.8 copy-start.5
Sparse Core Ops, SparseCore 0:
  171.9 125.5 all-reduce.2

commit v3 on v2

--- a/solution.py
+++ b/solution.py
@@ -220,6 +220,60 @@
             return carried
 
         lax.fori_loop(0, ROWS, one, 0)
+
+
+class SquareRest:
+    def __init__(self, place, kept, got, middle, second, result, sent, arrived):
+        self.x, self.y = lax.rem(place, 2), lax.div(place, 2)
+        self.to_x, self.to_y = {"dp": partner(place, 1)}, {"dp": partner(place, 2)}
+        self.kept, self.got = kept, got
+        self.middle, self.second, self.result = middle, second, result
+        self.sent, self.arrived = sent, arrived
+
+    def copies(self, phase):
+        x, y = self.x, self.y
+        if phase == 1:
+            plan = (
+                (self.middle.at[0], self.second.at[0], self.to_y),
+                (self.middle.at[1], self.second.at[1], self.to_x),
+            )
+        elif phase == 2:
+            one, two = self.result.at[2 * x + y], self.result.at[4 + 2 * y + x]
+            plan = ((one, one, self.to_y), (two, two, self.to_x))
+        else:
+            one, two = self.result.at[pl.ds(2 * x, 2)], self.result.at[pl.ds(4 + 2 * y, 2)]
+            plan = ((one, one, self.to_x), (two, two, self.to_y))
+        return [
+            remote(source, target, self.sent.at[2 * phase + i], self.arrived.at[2 * phase + i], to)
+            for i, (source, target, to) in enumerate(plan)
+        ]
+
+    def sum_of(self, half, side):
+        wide = self.middle.shape[3]
+        lanes = pl.ds(pl.multiple_of(side * wide, 128), wide)
+        return self.kept[half, :, :, lanes].astype(f32) + self.got[half, :, :, lanes].astype(f32)
+
+    def run(self, phase):
+        x, y = self.x, self.y
+        if phase > 1:
+            for copy in self.copies(phase - 1):
+                copy.wait_recv()
+        if phase == 1:
+            self.middle[0] = self.sum_of(0, 1 - y).astype(bf16)
+            self.middle[1] = self.sum_of(1, 1 - x).astype(bf16)
+        if phase == 2:
+            self.result[2 * x + y] = (self.sum_of(0, y) + self.second[0].astype(f32)).astype(bf16)
+            self.result[4 + 2 * y + x] = (
+                self.sum_of(1, x) + self.second[1].astype(f32)
+            ).astype(bf16)
+        if phase < 4:
+            for copy in self.copies(phase):
+                copy.start()
+
+    def finish(self):
+        for phase in (1, 2, 3):
+            for copy in self.copies(phase):
+                copy.wait_send()
 
 
 class SumLine:
@@ -325,6 +379,24 @@
     queries_ref,
     expand_ref,
     combine_ref,
+    one_out,
+    query_out,
+    key_out,
+    value_out,
+    probs_out,
+    latent_out,
+    normed_latent_out,
+    attended_out,
+    compress_out,
+    cot_out,
+    pick_out,
+    back_out,
+    rows_out,
+    residual_ref,
+    two_ref,
+    scale_one_ref,
+    scale_two_ref,
+    router_all,
     one_ref,
     query_ref,
     key_ref,
@@ -334,15 +406,10 @@
     normed_latent_ref,
     attended_ref,
     compress_all,
-    residual_ref,
-    two_ref,
-    scale_one_ref,
-    scale_two_ref,
     cot_all,
     pick_ref,
     back_ref,
     rows_ref,
-    router_all,
     queries,
     expand,
     combine,
@@ -360,6 +427,8 @@
     staged,
     marks,
     load_sem,
+    store_sem,
+    rows_sem,
     stat_sent,
     stat_arrived,
     line_sent,
@@ -389,6 +458,7 @@
 ):
     place, row, col = lax.axis_index("dp"), lax.axis_index("row"), lax.axis_index("col")
     other = 1 - col
+    inner = jnp.logical_and(row > 0, row < ROWS - 1)
     sibling = {"col": other}
     tokens, width = act_ref.shape
     slots = pick_ref.shape[1] // SQUARE
@@ -404,6 +474,30 @@
     ]
     for load in loads:
         load.start()
+    stores = [
+        pltpu.make_async_copy(source, target, store_sem.at[i])
+        for i, (source, target) in enumerate(
+            [
+                (one_ref, one_out),
+                (query_ref, query_out),
+                (key_ref, key_out),
+                (value_ref, value_out),
+                (latent_ref, latent_out),
+                (normed_latent_ref, normed_latent_out),
+                (compress_all, compress_out),
+                (probs_ref, probs_out),
+                (attended_ref, attended_out),
+                (cot_all, cot_out),
+                (pick_ref, pick_out),
+                (back_ref, back_out),
+            ]
+        )
+    ]
+
+    def rows_store(block):
+        return pltpu.make_async_copy(
+            rows_ref.at[:, block], rows_out.at[:, block], rows_sem.at[block]
+        )
 
     def stat_copy(index):
         return remote(
@@ -483,6 +577,12 @@
     routes[pl.ds(row, 1)] = route_ref[...].reshape((1,) + route_ref.shape)
     line.pass_on(row)
     router_copy(col).start()
+
+    @pl.when(jnp.logical_not(inner))
+    def _():
+        route_line.pass_on(row)
+        cot_line.pass_on(row)
+
     for block in range(ROWS):
         mark = mark_ref[:, block * tokens : (block + 1) * tokens].astype(f32)
         marks[block] = jnp.broadcast_to(mark, (8, tokens)).T
@@ -532,8 +632,17 @@
 
     lax.fori_loop(0, ROWS, gather, 0)
 
-    cot_line.pass_on(row)
-    route_line.pass_on(row)
+    @pl.when(inner)
+    def _():
+        route_line.pass_on(row)
+        cot_line.pass_on(row)
+
+    def relay(step):
+        block = block_at(row, step)
+        route_line.wait(block)
+        route_line.pass_on(block)
+        cot_line.wait(block)
+        cot_line.pass_on(block)
 
     def out_copy(block, step):
         piece = pl.ds(step * slots, slots)
@@ -552,12 +661,9 @@
     def take(step):
         block = block_at(row, step)
 
-        @pl.when(step > 0)
-        def _():
-            route_line.wait(block)
-            cot_line.wait(block)
-            route_line.pass_on(block)
-            cot_line.pass_on(block)
+        @pl.when(jnp.logical_and(step > 0, jnp.logical_not(inner)))
+        def _():
+            relay(step)
 
         before = (
             lax.broadcasted_iota(jnp.int32, (tokens, tokens), 0)
@@ -607,6 +713,12 @@
 
     lax.fori_loop(0, ROWS, latents, 0)
     take(0)
+
+    @pl.when(inner)
+    def _():
+        relay(1)
+        relay(2)
+
     loads[1].wait()
 
     def keys(block, carried):
@@ -635,6 +747,8 @@
         return carried
 
     lax.fori_loop(0, ROWS, keys, 0)
+    for index in range(7):
+        stores[index].start()
     seq = ROWS * tokens
     lanes = NOPE + 2 * ROPE
 
@@ -653,31 +767,31 @@
             attended_ref[block, :, pl.ds(at, HEADV)] = result
         att_copy(block, col).start()
 
-        @pl.when(jnp.logical_or(turn == 1, turn == 2))
-        def _():
+        @pl.when(jnp.logical_and(turn == 0, inner))
+        def _():
+            relay(3)
+
+        @pl.when(turn > 0)
+        def _():
+            mix(turn - 1)
             take(turn)
 
         return carried
 
-    lax.fori_loop(0, ROWS, attend, 0)
-    loads[2].wait()
-
-    def mix(turn, carried):
+    def mix(turn):
         block = block_at(row, ROWS - 1 - turn)
         att_copy(block, other).wait_recv()
         part[block] = nn(attended_ref[block], combine[...])
         sums.begin(block)
-        return carried
-
-    lax.fori_loop(0, ROWS, mix, 0)
+
+    loads[2].wait()
+    lax.fori_loop(0, ROWS, attend, 0)
+    mix(ROWS - 1)
+    for index in range(7, 12):
+        stores[index].start()
 
     def hand_on(turn, carried):
         sums.pass_on(block_at(row, jnp.where(turn == 0, 3, turn)))
-
-        @pl.when(turn == 0)
-        def _():
-            take(3)
-
         forward(turn)
         return carried
 
@@ -692,6 +806,7 @@
 
     def ended(block, carried):
         pair_copy(block, other).wait_recv()
+        rows_store(block).start()
         pair_copy(block, col).wait_send()
         for shift in range(1, SQUARE):
             out_copy(block, shift).wait_send()
@@ -707,6 +822,14 @@
         return carried
 
     lax.fori_loop(0, ROWS, ended, 0)
+    for store in stores:
+        store.wait()
+
+    def stored(block, carried):
+        rows_store(block).wait()
+        return carried
+
+    lax.fori_loop(0, ROWS, stored, 0)
     router_copy(other).wait_recv()
     router_copy(col).wait_send()
     stat_copy(0).wait_send()
@@ -783,32 +906,36 @@
     def shape(*dims, dtype=bf16):
         return jax.ShapeDtypeStruct(dims, dtype)
 
+    kept = [
+        shape(ROWS, tokens, width),
+        shape(ROWS, tokens, mine),
+        shape(2, ROWS, tokens, lanes),
+        shape(2, ROWS, tokens, HEADV),
+        shape(2, ROWS, tokens, seq),
+        shape(ROWS, tokens, latent_width, dtype=f32),
+        shape(ROWS, tokens, RANK),
+        shape(ROWS, tokens, COLS * 2 * HEADV),
+        shape(latent_width, width),
+        shape(ROWS, tokens, width),
+        shape(ROWS, picked, tokens),
+        shape(ROWS, tokens, picked),
+        shape(COLS, ROWS, picked, width),
+    ]
     return pl.pallas_call(
         attend_kernel,
         name="attend",
         out_shape=(
-            shape(ROWS, tokens, width),
-            shape(ROWS, tokens, mine),
-            shape(2, ROWS, tokens, lanes),
-            shape(2, ROWS, tokens, HEADV),
-            shape(2, ROWS, tokens, seq),
-            shape(ROWS, tokens, latent_width, dtype=f32),
-            shape(ROWS, tokens, RANK),
-            shape(ROWS, tokens, COLS * 2 * HEADV),
-            shape(latent_width, width),
+            *kept,
             shape(tokens, width, dtype=f32),
             shape(tokens, width),
             shape(tokens, 1, dtype=f32),
             shape(tokens, 1, dtype=f32),
-            shape(ROWS, tokens, width),
-            shape(ROWS, picked, tokens),
-            shape(ROWS, tokens, picked),
-            shape(COLS, ROWS, picked, width),
             shape(router.shape[1], COLS * width),
         ),
         in_specs=[whole] * 13 + [far] * 3,
-        out_specs=(whole,) * 18,
+        out_specs=(far,) * 13 + (whole,) * 5,
         scratch_shapes=[
+            *[VMEM(value.shape, value.dtype) for value in kept],
             VMEM(queries.shape, bf16),
             VMEM(expand.shape, bf16),
             VMEM(combine.shape, bf16),
@@ -826,6 +953,8 @@
             VMEM((ROWS, picked, width), bf16),
             VMEM((ROWS, tokens, 8), f32),
             DMA((3,)),
+            DMA((12,)),
+            DMA((ROWS,)),
             DMA((2,)),
             DMA((2,)),
             *line_sems(),
@@ -874,21 +1003,24 @@
     act_ref,
     scale_one_ref,
     scaling_ref,
-    one_ref,
-    query_ref,
-    key_ref,
-    value_ref,
-    probs_ref,
-    latent_ref,
     rescale_ref,
-    cos_ref,
-    sin_ref,
-    key_cos_ref,
-    key_sin_ref,
-    compress_all,
-    queries_ref,
-    expand_ref,
-    combine_ref,
+    combine_far,
+    query_far,
+    key_far,
+    value_far,
+    probs_far,
+    cos_far,
+    sin_far,
+    queries_far,
+    expand_far,
+    latent_far,
+    key_cos_far,
+    key_sin_far,
+    compress_far,
+    one_far,
+    kept_far,
+    got_x_far,
+    got_y_far,
     input_grad_ref,
     branch_ref,
     query_grad_ref,
@@ -896,9 +1028,26 @@
     own_latent_ref,
     scaling_rows,
     rescale_rows,
+    shared_sum,
+    combine,
+    query_ref,
+    key_ref,
+    value_ref,
+    probs_ref,
+    cos_ref,
+    sin_ref,
     queries,
     expand,
-    combine,
+    latent_ref,
+    key_cos_ref,
+    key_sin_ref,
+    compress_all,
+    one_ref,
+    kept,
+    got,
+    middle,
+    second,
+    result,
     stat_to,
     stat_from,
     grad_own,
@@ -932,6 +1081,9 @@
     own_arrived,
     sum_sent,
     sum_arrived,
+    rest_sent,
+    rest_arrived,
+    rest_sem,
 ):
     place, row, col = lax.axis_index("dp"), lax.axis_index("row"), lax.axis_index("col")
     other = 1 - col
@@ -946,14 +1098,32 @@
     loads = [
         pltpu.make_async_copy(source, target, load_sem.at[i])
         for i, (source, target) in enumerate(
-            [(combine_ref, combine), (queries_ref, queries), (expand_ref, expand)]
+            [
+                (combine_far, combine),
+                (query_far, query_ref),
+                (key_far, key_ref),
+                (value_far, value_ref),
+                (probs_far, probs_ref),
+                (cos_far, cos_ref),
+                (sin_far, sin_ref),
+                (queries_far, queries),
+                (expand_far, expand),
+                (latent_far, latent_ref),
+                (key_cos_far, key_cos_ref),
+                (key_sin_far, key_sin_ref),
+                (compress_far, compress_all),
+                (one_far, one_ref),
+                (kept_far, kept),
+                (got_x_far, got.at[0]),
+                (got_y_far, got.at[1]),
+            ]
         )
     ]
     for load in loads:
         load.start()
     line = Line(row, branch_ref, line_sent, line_arrived)
     sums = SumLine(row, part, leaving, coming, sum_sent, sum_arrived)
-    greet(row, place, col, line=True, square=False)
+    greet(row, place, col, line=True)
 
     def stat_copy(index):
         return remote(
@@ -978,10 +1148,13 @@
     )
     input_grad_ref[...] = residual_grad
     branch_ref[pl.ds(row, 1)] = residual_grad.astype(bf16).reshape(1, tokens, width)
+    line.pass_on(row)
     key_grad[...] = jnp.zeros_like(key_grad)
     value_grad[...] = jnp.zeros_like(value_grad)
     scaling_rows[...] = jnp.zeros_like(scaling_rows)
     rescale_rows[...] = jnp.zeros_like(rescale_rows)
+
+    rest = SquareRest(place, kept, got, middle, second, result, rest_sent, rest_arrived)
 
     def grad_copy(block):
         return remote(
@@ -1011,11 +1184,13 @@
         @pl.when(step > 0)
         def _():
             line.wait(block)
-
-        line.pass_on(block)
+            line.pass_on(block)
 
         @pl.when(step == 0)
         def _():
+            for load in loads[14:]:
+                load.wait()
+            rest.run(1)
             loads[0].wait()
 
         grads = branch_ref[block]
@@ -1027,6 +1202,12 @@
 
     def heads(step):
         block = block_at(row, step)
+
+        @pl.when(step == 0)
+        def _():
+            for load in loads[1:7]:
+                load.wait()
+
         grad_copy(block).wait_recv()
         grads = (grad_own[block] + grad_from[block].astype(f32)).astype(bf16)
         pieces = []
@@ -1054,7 +1235,7 @@
 
         @pl.when(step == 0)
         def _():
-            loads[1].wait()
+            loads[7].wait()
 
         query_copy(block, other).wait_recv()
         part[block] = nt(query_grad_ref[block], queries[...])
@@ -1066,10 +1247,15 @@
             def _(delay=delay, stage=stage):
                 stage(step - delay)
 
+        @pl.when(step == 2)
+        def _():
+            rest.run(2)
+
         return carried
 
     lax.fori_loop(0, ROWS + 1, turn, 0)
-    loads[2].wait()
+    for load in loads[8:14]:
+        load.wait()
 
     def latents(turn, carried):
         block = block_at(row, ROWS - 1 - turn)
@@ -1102,6 +1288,7 @@
 
     lax.fori_loop(0, ROWS, latents, 0)
     project(ROWS - 1)
+    rest.run(3)
 
     def turned_piece(member):
         return turned.at[
@@ -1158,6 +1345,15 @@
 
     own_copy(col).start()
     sums.total(total)
+    rest.run(4)
+    pieces = [
+        pltpu.make_async_copy(
+            result.at[i], shared_sum.at[:, :, i * 128 : (i + 1) * 128], rest_sem.at[i]
+        )
+        for i in range(8)
+    ]
+    for piece in pieces:
+        piece.start()
     input_grad_ref[...] += norm_grad(
         act_ref[...].astype(f32), scale_one_ref[...], scaling_ref[...], total[...], 1
     )
@@ -1175,6 +1371,9 @@
         turned_copy(step).wait_send()
     stat_copy(0).wait_send()
     stat_copy(1).wait_send()
+    for piece in pieces:
+        piece.wait()
+    rest.finish()
     sums.finish()
     line.finish()
 
@@ -1200,6 +1399,7 @@
     queries,
     expand,
     combine,
+    shared,
 ):
     tokens, width = activations.shape
     seq = ROWS * tokens
@@ -1213,6 +1413,24 @@
     def shape(*dims, dtype=bf16):
         return jax.ShapeDtypeStruct(dims, dtype)
 
+    kept, got_x, got_y = shared
+    piece = kept.shape[1:3] + (kept.shape[3] // 2,)
+    loaded = (
+        combine,
+        query,
+        key,
+        value,
+        probs,
+        tables[0],
+        tables[1],
+        queries,
+        expand,
+        latent,
+        tables[2],
+        tables[3],
+        compress_all,
+        one,
+    )
     return pl.pallas_call(
         attend_back_kernel,
         name="attend_back",
@@ -1224,13 +1442,17 @@
             shape(sliced, seq),
             shape(8, width, dtype=f32),
             shape(8, RANK, dtype=f32),
+            shape(*kept.shape[1:3], width),
         ),
-        in_specs=[whole] * 20 + [far] * 3,
-        out_specs=(whole,) * 7,
+        in_specs=[whole] * 9 + [far] * 17,
+        out_specs=(whole,) * 7 + (far,),
         scratch_shapes=[
-            VMEM(queries.shape, bf16),
-            VMEM(expand.shape, bf16),
-            VMEM(combine.shape, bf16),
+            *[VMEM(value.shape, value.dtype) for value in loaded],
+            VMEM(kept.shape, bf16),
+            VMEM(kept.shape, bf16),
+            VMEM((2,) + piece, bf16),
+            VMEM((2,) + piece, bf16),
+            VMEM((8,) + piece, bf16),
             VMEM((2, tokens, 128), f32),
             VMEM((2, tokens, 128), f32),
             VMEM((ROWS, tokens, 2 * HEADV), f32),
@@ -1247,7 +1469,7 @@
             VMEM((ROWS, tokens, width), bf16),
             VMEM((2, ROWS, tokens, width), bf16),
             VMEM((tokens, width), f32),
-            DMA((3,)),
+            DMA((17,)),
             DMA((2,)),
             DMA((2,)),
             *line_sems(),
@@ -1257,6 +1479,9 @@
             *pair_sems(),
             *pair_sems(),
             *sum_sems(),
+            DMA((8,)),
+            DMA((8,)),
+            DMA((8,)),
         ],
         compiler_params=pltpu.CompilerParams(
             collective_id=3, has_side_effects=True, vmem_limit_bytes=56 * MIB
@@ -1273,18 +1498,11 @@
         activations,
         scale_one,
         scaling.reshape(1, width),
-        one,
-        query,
-        key,
-        value,
-        probs,
-        latent,
         rescale.reshape(1, RANK),
-        *tables,
-        compress_all,
-        queries,
-        expand,
-        combine,
+        *loaded,
+        kept,
+        got_x,
+        got_y,
     )
 
 
@@ -1297,22 +1515,25 @@
     normed_ref,
     pick_ref,
     back_ref,
+    cot_ref,
+    router_ref,
     cot_rows_ref,
-    cot_ref,
     fan_ref,
     fun_ref,
     wide_ref,
     narrow_ref,
-    router_ref,
     sum_ref,
     gathered_ref,
     rows_out,
     gu_out,
     hidden_out,
+    shared_x,
+    shared_y,
+    shared_kept,
     shared_out,
-    shared_gu_out,
     premix_ref,
     router_rows,
+    reply_ref,
     fan,
     fun,
     wide,
@@ -1326,12 +1547,13 @@
     pair_to,
     pair_from,
     home,
-    shared_own,
     shared_to,
     shared_from,
     part,
     passed_to,
     passed_from,
+    shared_gu,
+    shared_grad,
     load_sem,
     store_sem,
     line_sent,
@@ -1348,15 +1570,20 @@
     home_arrived,
     sum_sent,
     sum_arrived,
+    other_sent,
+    other_arrived,
+    reply_sent,
+    reply_arrived,
+    grad_sem,
 ):
     place, row, col = lax.axis_index("dp"), lax.axis_index("row"), lax.axis_index("col")
     other = 1 - col
+    inner = jnp.logical_and(row > 0, row < ROWS - 1)
     tokens, width = normed_ref.shape
     picked = pick_ref.shape[1]
     slots = picked // SQUARE
-    hid = fun.shape[0]
+    experts = router_ref.shape[0]
     share = narrow.shape[0]
-    experts = router_ref.shape[0]
     loads = [
         pltpu.make_async_copy(source, target, load_sem.at[i])
         for i, (source, target) in enumerate(
@@ -1373,31 +1600,34 @@
         load.start()
     greet(row, place, col)
     gathered_ref[pl.ds(row, 1)] = normed_ref[...].reshape(1, tokens, width)
+    line = Line(row, gathered_ref, line_sent, line_arrived)
+    line.pass_on(row)
     premix_ref[...] = jnp.zeros_like(premix_ref)
     router_rows[...] = jnp.zeros_like(router_rows)
-    line = Line(row, gathered_ref, line_sent, line_arrived)
     sums = SumLine(row, part, passed_to, passed_from, sum_sent, sum_arrived)
     sibling = {"col": other}
 
-    def out_copy(block, step):
+    def half_lines(half):
+        return pl.ds(pl.multiple_of(half * width, width), width)
+
+    def square_copy(source, target, sent, arrived, block, step):
         piece = pl.ds(step * slots, slots)
         return remote(
-            staged.at[block, piece],
-            rows.at[col, block, piece],
-            out_sent.at[block, step],
-            out_arrived.at[block, step],
+            source.at[block, piece],
+            target.at[block, piece],
+            sent.at[block, step],
+            arrived.at[block, step],
             {"dp": partner(place, step)},
         )
 
+    def out_copy(block, step):
+        return square_copy(staged, rows.at[col], out_sent, out_arrived, block, step)
+
     def home_copy(block, step):
-        piece = pl.ds(step * slots, slots)
-        return remote(
-            staged.at[block, piece],
-            home.at[block, piece],
-            home_sent.at[block, step],
-            home_arrived.at[block, step],
-            {"dp": partner(place, step)},
-        )
+        return square_copy(staged, home, home_sent, home_arrived, block, step)
+
+    def reply_copy(block, step):
+        return square_copy(staged, reply_ref, reply_sent, reply_arrived, block, step)
 
     def fwd_copy(block, half):
         here = rows.at[half, block]
@@ -1412,35 +1642,49 @@
             sibling,
         )
 
-    def half_copy(block):
+    def half_copy(step):
         return remote(
-            pair_to.at[block],
-            pair_from.at[block],
-            half_sent.at[block],
-            half_arrived.at[block],
+            pair_to.at[lax.rem(step, 2)],
+            pair_from.at[step],
+            half_sent.at[step],
+            half_arrived.at[step],
             sibling,
         )
 
-    def stores(block):
+    def other_copy(step):
+        return remote(
+            pair_to.at[lax.rem(step, 2)],
+            pair_from.at[jnp.where(step == ROWS - 1, ROWS, step)],
+            other_sent.at[step],
+            other_arrived.at[step],
+            sibling,
+        )
+
+    def stores(step):
+        block = block_at(row, step)
         return [
-            pltpu.make_async_copy(source, target, store_sem.at[index, block])
+            pltpu.make_async_copy(source, target, store_sem.at[index, step])
             for index, (source, target) in enumerate(
                 [
                     (rows.at[:, block], rows_out.at[:, block]),
-                    (gu.at[:, block], gu_out.at[:, block]),
+                    (gu.at[:, lax.rem(step, 2)], gu_out.at[:, block]),
                     (hidden.at[block], hidden_out.at[block]),
                 ]
             )
         ]
 
+    def relay(step):
+        block = block_at(row, step)
+        line.wait(block)
+        line.pass_on(block)
+
     def take(step):
         block = block_at(row, step)
 
-        @pl.when(step > 0)
-        def _():
-            line.wait(block)
-
-        line.pass_on(block)
+        @pl.when(jnp.logical_and(step > 0, jnp.logical_not(inner)))
+        def _():
+            relay(step)
+
         staged[block] = nn(pick_ref[block], gathered_ref[block]).astype(bf16)
         for shift in (3, 2, 1):
             out_copy(block, shift).start()
@@ -1451,7 +1695,6 @@
             loads[0].wait()
             loads[1].wait()
 
-        slot = lax.rem(step, 2)
         for index, value in enumerate(
             (
                 nt(gathered_ref[block], wide[0]),
@@ -1459,7 +1702,6 @@
                 nt(cot_ref[block], narrow[...]),
             )
         ):
-            shared_own[slot, index] = value
             shared_to[block, index] = value.astype(bf16)
         shared_copy(block).start()
 
@@ -1471,28 +1713,33 @@
 
     def shared(step):
         block = block_at(row, step)
-        slot = lax.rem(step, 2)
         shared_copy(block).wait_recv()
         gate, up, grad = [
-            shared_own[slot, index] + shared_from[block, index].astype(f32) for index in range(3)
+            shared_to[block, index].astype(f32) + shared_from[block, index].astype(f32)
+            for index in range(3)
         ]
         act, slope = silu_pair(gate)
         shared_out[block] = (act * up).astype(bf16)
         gate_grad = (grad * up * slope).astype(bf16)
         up_grad = (grad * act).astype(bf16)
-        shared_gu_out[0, block] = gate_grad
-        shared_gu_out[1, block] = up_grad
+        shared_gu[0, block] = gate_grad
+        shared_gu[1, block] = up_grad
         part[block] = nn(gate_grad, wide[0]) + nn(up_grad, wide[1])
 
     def experts_of(step):
         block = block_at(row, step)
-        fwd_copy(block, other).wait_recv()
 
         @pl.when(step == 0)
         def _():
             for load in loads[2:]:
                 load.wait()
 
+        @pl.when(step > 1)
+        def _():
+            stores(step - 2)[1].wait()
+            half_copy(step - 2).wait_send()
+
+        fwd_copy(block, other).wait_recv()
         left, right = rows[0, block], rows[1, block]
         logits = nt(left, router_ref[:, 0:width]) + nt(right, router_ref[:, width:])
         logits = logits - jnp.max(logits, axis=1, keepdims=True)
@@ -1509,34 +1756,31 @@
         value = act * up
         hidden[block] = (value * gates).astype(bf16)
         gate_sum = gates * jnp.sum(value * raw, axis=1, keepdims=True)
-        logit_grad = gate_sum * (own - probs)
+        logit_grad = (gate_sum * (own - probs)).astype(bf16)
         raw = raw * gates
-        gu[0, block] = (raw * up * slope).astype(bf16)
-        gu[1, block] = (raw * act).astype(bf16)
-        logit_grad = logit_grad.astype(bf16)
+        slot = lax.rem(step, 2)
+        gu[0, slot] = (raw * up * slope).astype(bf16)
+        gu[1, slot] = (raw * act).astype(bf16)
+
+        def half_of(half):
+            lines = half_lines(half)
+            return (
+                nn(gu[0, slot], fan[0, :, lines])
+                + nn(gu[1, slot], fan[1, :, lines])
+                + nn(logit_grad, router_ref[:, lines])
+            )
+
+        pair_to[slot] = half_of(other).astype(bf16)
+        half_copy(step).start()
+        pair_own[...] = half_of(col)
         router_rows[:, 0:width] += tn(logit_grad, left)
         router_rows[:, width:] += tn(logit_grad, right)
-
-        def half_of(half):
-            lines = pl.ds(pl.multiple_of(half * width, width), width)
-            return (
-                nn(gu[0, block], fan[0, :, lines])
-                + nn(gu[1, block], fan[1, :, lines])
-                + nn(logit_grad, router_ref[:, lines])
-            )
-
-        pair_to[block] = half_of(other).astype(bf16)
-        half_copy(block).start()
-        pair_own[...] = half_of(col)
-        for copy in stores(block):
+        for copy in stores(step):
             copy.start()
-
-    def send_home(step):
-        block = block_at(row, step)
         for shift in range(1, SQUARE):
             out_copy(block, shift).wait_send()
-        half_copy(block).wait_recv()
-        staged[block] = (pair_own[...] + pair_from[block].astype(f32)).astype(bf16)
+        half_copy(step).wait_recv()
+        staged[block] = (pair_own[...] + pair_from[step].astype(f32)).astype(bf16)
         for shift in (3, 2, 1):
             home_copy(block, shift).start()
         home[block, 0:slots] = staged[block, 0:slots]
@@ -1550,45 +1794,142 @@
         premix_ref[...] += jnp.sum(
             (total * gathered_ref[block].astype(f32)).reshape(tokens // 8, 8, width), axis=0
         )
-
         sums.begin(block)
 
-    stages = (
-        (0, take),
-        (1, forward),
-        (1, shared),
-        (3, send_home),
-        (2, experts_of),
-        (4, add_up),
-    )
+    def reply(step):
+        block = block_at(row, step)
+        slot = lax.rem(step, 2)
+
+        @pl.when(step < 2)
+        def _():
+            half_copy(step + 2).wait_send()
+
+        @pl.when(step > 1)
+        def _():
+            other_copy(step - 2).wait_send()
+
+        pair_to[slot] = nn(hidden[block], fun[:, half_lines(other)]).astype(bf16)
+        other_copy(step).start()
+
+    def reply_home(step):
+        block = block_at(row, step)
+        own = nn(hidden[block], fun[:, half_lines(col)])
+        for shift in range(1, SQUARE):
+            home_copy(block, shift).wait_send()
+        came = jnp.where(step == ROWS - 1, ROWS, step)
+        other_copy(step).wait_recv()
+        staged[block] = (own + pair_from[came].astype(f32)).astype(bf16)
+        for shift in (3, 2, 1):
+            reply_copy(block, shift).start()
+        reply_ref[block, 0:slots] = staged[block, 0:slots]
 
     def turn(step, carried):
-        for delay, stage in stages:
-
-            @pl.when(jnp.logical_and(step >= delay, step < delay + ROWS))
-            def _(delay=delay, stage=stage):
-                stage(step - delay)
-
-        @pl.when(step >= ROWS + 3)
-        def _():
-            sums.pass_on(block_at(row, jnp.where(step == ROWS + 5, 1, step - 5)))
+        @pl.when(step < ROWS)
+        def _():
+            take(step)
+
+        @pl.when(jnp.logical_and(step == 0, inner))
+        def _():
+            relay(1)
+            relay(2)
+
+        @pl.when(jnp.logical_and(step >= 1, step < ROWS))
+        def _():
+            forward(step - 1)
+
+        @pl.when(jnp.logical_and(step >= 2, step < ROWS + 2))
+        def _():
+            experts_of(step - 2)
+
+        @pl.when(step == ROWS)
+        def _():
+            forward(ROWS - 1)
+
+        @pl.when(jnp.logical_or(step == 1, step >= 3))
+        def _():
+            shared(jnp.where(step == 1, 0, step - 2))
+
+        @pl.when(jnp.logical_and(step == 1, inner))
+        def _():
+            relay(3)
+
+        @pl.when(step >= 3)
+        def _():
+            add_up(step - 3)
 
         return carried
 
-    lax.fori_loop(0, ROWS + 6, turn, 0)
+    lax.fori_loop(0, ROWS + 2, turn, 0)
+
+    def replies(step, carried):
+        @pl.when(step < ROWS)
+        def _():
+            reply(step)
+
+        @pl.when(step > 0)
+        def _():
+            reply_home(step - 1)
+
+        return carried
+
+    lax.fori_loop(0, ROWS + 1, replies, 0)
+    add_up(ROWS - 1)
+
+    def hand_on(turn, carried):
+        sums.pass_on(block_at(row, jnp.where(turn == 2, 1, turn + 2)))
+        return carried
+
+    lax.fori_loop(0, ROWS - 1, hand_on, 0)
+
+    seq = ROWS * tokens
+    for index, (left, right) in enumerate(
+        (
+            (shared_out, cot_ref),
+            (shared_gu.at[0], gathered_ref),
+            (shared_gu.at[1], gathered_ref),
+        )
+    ):
+        grad = tn(left[...].reshape(seq, share), right[...].reshape(seq, width))
+        shared_grad[index] = grad.astype(bf16)
+    x, y = lax.rem(place, 2), lax.div(place, 2)
+    quarter = width // SQUARE
+    grad_copies = []
+    for index, (half, side, target) in enumerate(
+        (
+            (0, 1 - x, shared_x),
+            (1, 1 - y, shared_y),
+            (0, x, shared_kept.at[0]),
+            (1, y, shared_kept.at[1]),
+        )
+    ):
+        lanes = pl.ds(pl.multiple_of((2 * half + side) * quarter, 128), quarter)
+        grad_copies.append(
+            pltpu.make_async_copy(shared_grad.at[:, :, lanes], target, grad_sem.at[index])
+        )
+        grad_copies[index].start()
     sums.total(sum_ref)
 
-    def ended(block, carried):
+    def ended(step, carried):
+        block = block_at(row, step)
         shared_copy(block).wait_send()
         fwd_copy(block, col).wait_send()
-        half_copy(block).wait_send()
         for shift in range(1, SQUARE):
-            home_copy(block, shift).wait_send()
-        for copy in stores(block):
-            copy.wait()
+            reply_copy(block, shift).wait_recv()
+            reply_copy(block, shift).wait_send()
+        copies = stores(step)
+        copies[0].wait()
+        copies[2].wait()
+
+        @pl.when(step >= ROWS - 2)
+        def _():
+            copies[1].wait()
+            other_copy(step).wait_send()
+
         return carried
 
     lax.fori_loop(0, ROWS, ended, 0)
+    for copy in grad_copies:
+        copy.wait()
     sums.finish()
     line.finish()
 
@@ -1616,13 +1957,16 @@
             shape(COLS, ROWS, picked, width),
             shape(2, ROWS, picked, hid),
             shape(ROWS, picked, hid),
+            shape(3, share, width // SQUARE),
+            shape(3, share, width // SQUARE),
+            shape(2, 3, share, width // SQUARE),
             shape(ROWS, tokens, share),
-            shape(2, ROWS, tokens, share),
             shape(8, width, dtype=f32),
             shape(experts, COLS * width, dtype=f32),
+            shape(ROWS, picked, width),
         ),
-        in_specs=[whole, whole, whole, far, whole, far, far, far, far, whole],
-        out_specs=(whole, whole, far, far, far, whole, whole, whole, whole),
+        in_specs=[whole] * 5 + [far] * 5,
+        out_specs=(whole, whole) + (far,) * 6 + (whole,) * 4,
         scratch_shapes=[
             VMEM(fan.shape, bf16),
             VMEM(fun.shape, bf16),
@@ -1631,34 +1975,31 @@
             VMEM(cot_rows.shape, bf16),
             VMEM((COLS, ROWS, picked, width), bf16),
             VMEM((ROWS, picked, width), bf16),
-            VMEM((2, ROWS, picked, hid), bf16),
+            VMEM((2, 2, picked, hid), bf16),
             VMEM((ROWS, picked, hid), bf16),
             VMEM((picked, width), f32),
+            VMEM((2, picked, width), bf16),
+            VMEM((ROWS + 1, picked, width), bf16),
             VMEM((ROWS, picked, width), bf16),
-            VMEM((ROWS, picked, width), bf16),
-            VMEM((ROWS, picked, width), bf16),
-            VMEM((2, 3, tokens, share), f32),
             VMEM((ROWS, 3, tokens, share), bf16),
             VMEM((ROWS, 3, tokens, share), bf16),
             VMEM((ROWS, tokens, width), f32),
             VMEM((ROWS, tokens, width), bf16),
             VMEM((2, ROWS, tokens, width), bf16),
+            VMEM((2, ROWS, tokens, share), bf16),
+            VMEM((3, share, width), bf16),
             DMA((5,)),
             DMA((3, ROWS)),
-            DMA((ROWS, 2)),
-            DMA((ROWS,)),
-            DMA((ROWS, SQUARE)),
-            DMA((ROWS, SQUARE)),
-            DMA((ROWS,)),
-            DMA((ROWS,)),
-            DMA((ROWS,)),
-            DMA((ROWS,)),
-            DMA((ROWS,)),
-            DMA((ROWS,)),
-            DMA((ROWS, SQUARE)),
-            DMA((ROWS, SQUARE)),
-            DMA((ROWS, SPLIT)),
-            DMA((2, ROWS, SPLIT)),
+            *line_sems(),
+            *square_sems(),
+            *pair_sems(),
+            *pair_sems(),
+            *pair_sems(),
+            *square_sems(),
+            *sum_sems(),
+            *pair_sems(),
+            *square_sems(),
+            DMA((4,)),
         ],
         compiler_params=pltpu.CompilerParams(
             collective_id=2, has_side_effects=True, vmem_limit_bytes=62 * MIB
@@ -1666,7 +2007,7 @@
         cost_estimate=pl.CostEstimate(
             flops=60 * 1024**3, bytes_accessed=64 * MIB, transcendentals=0
         ),
-    )(normed, pick, back, cot_rows, cot_all, fan, fun, wide, narrow, router_all)
+    )(normed, pick, back, cot_all, router_all, cot_rows, fan, fun, wide, narrow)
 
 
 class SquareSum:
@@ -1760,8 +2101,7 @@
     router_rows,
     premix_ref,
     scaling_ref,
-    hidden_ref,
-    funnel_ref,
+    home_ref,
     one_ref,
     query_grad_ref,
     attended_ref,
@@ -1775,8 +2115,7 @@
     expand_out,
     compress_out,
     small_ref,
-    hidden,
-    funnel,
+    home,
     one,
     query_grad,
     attended,
@@ -1784,11 +2123,6 @@
     latent,
     expanded,
     narrow,
-    reply_own,
-    reply_to,
-    reply_from,
-    staged,
-    home,
     part,
     leaving,
     coming,
@@ -1804,10 +2138,6 @@
     small_own,
     load_sem,
     store_sem,
-    reply_sent,
-    reply_arrived,
-    home_sent,
-    home_arrived,
     sum_sent,
     sum_arrived,
     pair_sent,
@@ -1821,22 +2151,19 @@
     sibling = {"col": other}
     tokens, width = output_ref.shape
     seq = ROWS * tokens
-    picked = back_ref.shape[2]
-    slots = picked // SQUARE
     experts = router_rows.shape[0]
     loads = [
         pltpu.make_async_copy(source, target, load_sem.at[i])
         for i, (source, target) in enumerate(
             [
-                (funnel_ref, funnel),
-                (hidden_ref, hidden),
+                (narrow_ref, narrow),
+                (home_ref, home),
                 (one_ref, one),
                 (query_grad_ref, query_grad),
                 (attended_ref, attended),
                 (branch_ref, branch),
                 (latent_ref, latent),
                 (expanded_ref, expanded),
-                (narrow_ref, narrow),
             ]
         )
     ]
@@ -1845,69 +2172,11 @@
     greet(row, place, col, line=True, square=True)
     line_sums = SumLine(row, part, leaving, coming, sum_sent, sum_arrived)
 
-    def reply_copy(block):
-        return remote(
-            reply_to.at[block],
-            reply_from.at[block],
-            reply_sent.at[block],
-            reply_arrived.at[block],
-            sibling,
-        )
-
-    def home_copy(block, step):
-        piece = pl.ds(step * slots, slots)
-        return remote(
-            staged.at[block, piece],
-            home.at[block, piece],
-            home_sent.at[block, step],
-            home_arrived.at[block, step],
-            {"dp": partner(place, step)},
-        )
-
-    def reply(turn):
-        block = block_at(row, ROWS - 1 - turn)
-        value = hidden[block]
-        reply_to[block] = nn(
-            value, funnel[:, pl.ds(pl.multiple_of(other * width, width), width)]
-        ).astype(bf16)
-        reply_copy(block).start()
-        reply_own[lax.rem(turn, 2)] = nn(
-            value, funnel[:, pl.ds(pl.multiple_of(col * width, width), width)]
-        )
-
-    def reply_home(turn):
-        block = block_at(row, ROWS - 1 - turn)
-        reply_copy(block).wait_recv()
-        staged[block] = (
-            reply_own[lax.rem(turn, 2)] + reply_from[block].astype(f32)
-        ).astype(bf16)
-        for shift in (3, 2, 1):
-            home_copy(block, shift).start()
-        home[block, 0:slots] = staged[block, 0:slots]
-
     def reply_add(turn, carried):
         block = block_at(row, ROWS - 1 - turn)
-        for shift in range(1, SQUARE):
-            home_copy(block, shift).wait_recv()
         part[block] = nn(back_ref[block], home[block]) + nn(shared_ref[block], narrow[...])
         line_sums.begin(block)
         return carried
-
-    loads[0].wait()
-    loads[1].wait()
-
-    def replies(turn, carried):
-        @pl.when(turn < ROWS)
-        def _():
-            reply(turn)
-
-        @pl.when(turn > 0)
-        def _():
-            reply_home(turn - 1)
-
-        return carried
-
-    lax.fori_loop(0, ROWS + 1, replies, 0)
 
     kinds = [sums_scratch[7 * i : 7 * i + 7] for i in range(4)]
     sums = []
@@ -1916,35 +2185,32 @@
             sums.append(SquareSum(place, *[ref.at[index] for ref in scratch]))
     parts = [scratch[0] for scratch in kinds]
     counts = [ref.shape[0] for ref in parts]
-    for load in loads[2:4]:
-        load.wait()
-    index = 0
-    for chunk in range(counts[0]):
-        height = 8 * parts[0].shape[2]
-        tokens_here = one[:, :, chunk * height : (chunk + 1) * height].reshape(seq, height)
-        grad = tn(tokens_here, query_grad[...].reshape(seq, query_grad.shape[2]))
-        parts[0][chunk] = grad.astype(bf16).reshape(parts[0].shape[1:])
+    def begin(index):
+        kind, chunk = 0, index
+        while chunk >= counts[kind]:
+            chunk -= counts[kind]
+            kind += 1
+        if chunk == 0:
+            for load in loads[2 + 2 * min(kind, 3) :][: 2 if kind < 3 else 0]:
+                load.wait()
+        if kind < 2:
+            left, right = ((one, query_grad), (attended, branch))[kind]
+            height = 8 * parts[kind].shape[2]
+            piece = left[:, :, chunk * height : (chunk + 1) * height].reshape(seq, height)
+            grad = tn(piece, right[...].reshape(seq, right.shape[2]))
+        elif kind == 2:
+            grad = tn(latent[...].reshape(seq, RANK), expanded[...].reshape(seq, expanded.shape[2]))
+        else:
+            grad = nn(own_latent_ref[...], one[...].reshape(seq, width)).astype(bf16)
+            for piece in range(8):
+                parts[3][0, piece] = grad[:, piece * (width // 8) : (piece + 1) * (width // 8)]
+        if kind < 3:
+            parts[kind][chunk] = grad.astype(bf16).reshape(parts[kind].shape[1:])
         sums[index].run(0)
-        index += 1
-    loads[4].wait()
-    loads[5].wait()
-    for chunk in range(counts[1]):
-        height = 8 * parts[1].shape[2]
-        tokens_here = attended[:, :, chunk * height : (chunk + 1) * height].reshape(seq, height)
-        grad = tn(tokens_here, branch[...].reshape(seq, width))
-        parts[1][chunk] = grad.astype(bf16).reshape(parts[1].shape[1:])
-        sums[index].run(0)
-        index += 1
-    loads[6].wait()
-    loads[7].wait()
-    grad = tn(latent[...].reshape(seq, RANK), expanded[...].reshape(seq, expanded.shape[2]))
-    parts[2][0] = grad.astype(bf16).reshape(parts[2].shape[1:])
-    sums[index].run(0)
-    index += 1
-    grad = nn(own_latent_ref[...], one[...].reshape(seq, width)).astype(bf16)
-    for piece in range(8):
-        parts[3][0, piece] = grad[:, piece * (width // 8) : (piece + 1) * (width // 8)]
-    sums[index].run(0)
+
+    ahead = 3
+    for index in range(ahead):
+        begin(index)
 
     def small_copy(step):
         if step == 0:
@@ -1966,28 +2232,54 @@
             {"dp": partner(place, shift)},
         )
 
-    rescale_row = jnp.sum(rescale_rows[...], axis=0, keepdims=True)
-    empty = jnp.zeros((small_own.shape[0] - experts, width), f32)
-    small_to[0:experts] = router_rows[:, pl.ds(pl.multiple_of(other * width, width), width)]
-    small_to[experts:] = empty
-    small_to[experts + 2 : experts + 3, 0:RANK] = rescale_row
-    small_copy(0).start()
-    small_own[0:experts] = router_rows[:, pl.ds(pl.multiple_of(col * width, width), width)]
-    small_own[experts:] = empty
-    small_own[experts : experts + 1] = (
-        jnp.sum(premix_rows[...], axis=0, keepdims=True) / premix_ref[...]
-    )
-    small_own[experts + 1 : experts + 2] = (
-        jnp.sum(scaling_rows[...], axis=0, keepdims=True) / scaling_ref[...]
-    )
-    small_own[experts + 2 : experts + 3, 0:RANK] = rescale_row
-    small_copy(0).wait_recv()
-    small_own[...] += small_from[...]
-    for step in range(1, ROWS):
-        small_copy(step).start()
-
-    loads[8].wait()
-    lax.fori_loop(0, ROWS, reply_add, 0)
+    def small_begin():
+        rescale_row = jnp.sum(rescale_rows[...], axis=0, keepdims=True)
+        empty = jnp.zeros((small_own.shape[0] - experts, width), f32)
+        small_to[0:experts] = router_rows[:, pl.ds(pl.multiple_of(other * width, width), width)]
+        small_to[experts:] = empty
+        small_to[experts + 2 : experts + 3, 0:RANK] = rescale_row
+        small_copy(0).start()
+        small_own[0:experts] = router_rows[:, pl.ds(pl.multiple_of(col * width, width), width)]
+        small_own[experts:] = empty
+        small_own[experts : experts + 1] = (
+            jnp.sum(premix_rows[...], axis=0, keepdims=True) / premix_ref[...]
+        )
+        small_own[experts + 1 : experts + 2] = (
+            jnp.sum(scaling_rows[...], axis=0, keepdims=True) / scaling_ref[...]
+        )
+        small_own[experts + 2 : experts + 3, 0:RANK] = rescale_row
+
+    def small_line_begin():
+        small_copy(0).wait_recv()
+        small_own[...] += small_from[...]
+        for step in range(1, ROWS):
+            small_copy(step).start()
+
+    def small_square_begin():
+        for step in range(1, ROWS):
+            small_copy(step).wait_recv()
+        small_ref[...] = small_own[...] + small_line[1] + small_line[2] + small_line[3]
+        for step in range(ROWS, ROWS + SQUARE - 1):
+            small_copy(step).start()
+
+    def small_end():
+        for step in range(ROWS, ROWS + SQUARE - 1):
+            small_copy(step).wait_recv()
+        for step in range(ROWS, ROWS + SQUARE - 1):
+            small_copy(step).wait_send()
+        small_ref[...] += small_square[1] + small_square[2] + small_square[3]
+
+    def reply_begin():
+        loads[0].wait()
+        loads[1].wait()
+        lax.fori_loop(0, ROWS, reply_add, 0)
+
+    def reply_pass():
+        lax.fori_loop(0, 3, line_pass, 0)
+
+    def reply_end():
+        line_sums.total(total)
+        output_ref[...] = (total[...] + residual_ref[...]).astype(bf16)
 
     def line_pass(turn, carried):
         line_sums.pass_on(block_at(row, jnp.where(turn == 0, 3, turn)))
@@ -2025,38 +2317,27 @@
             store(compress_wide, compress_out)
 
     count = len(sums)
-    small_steps = {
-        2: "line",
-        count + 2: "square",
+    between = {
+        0: (reply_begin, small_begin),
+        1: (small_line_begin,),
+        4: (reply_pass,),
+        5: (small_square_begin,),
+        count - 1: (reply_end,),
+        count + 1: (small_end,),
     }
-    for turn in range(count + 6):
+    for turn in range(count + 3):
         if turn < count:
             sums[turn].run(1)
-        if turn == 1:
-            lax.fori_loop(0, 3, line_pass, 0)
-        if 0 <= turn - 2 < count:
-            sums[turn - 2].run(2)
-        if 0 <= turn - 4 < count:
-            sums[turn - 4].run(3)
-        if 0 <= turn - 6 < count:
-            sums[turn - 6].run(4)
-            put(turn - 6)
-        if small_steps.get(turn) == "line":
-            for step in range(1, ROWS):
-                small_copy(step).wait_recv()
-            small_ref[...] = (
-                small_own[...] + small_line[1] + small_line[2] + small_line[3]
-            )
-            for step in range(ROWS, ROWS + SQUARE - 1):
-                small_copy(step).start()
-            line_sums.total(total)
-            output_ref[...] = (total[...] + residual_ref[...]).astype(bf16)
-        if small_steps.get(turn) == "square":
-            for step in range(ROWS, ROWS + SQUARE - 1):
-                small_copy(step).wait_recv()
-            for step in range(ROWS, ROWS + SQUARE - 1):
-                small_copy(step).wait_send()
-            small_ref[...] += small_square[1] + small_square[2] + small_square[3]
+        if turn + ahead < count:
+            begin(turn + ahead)
+        for phase in (2, 3, 4):
+            index = turn + 1 - phase
+            if 0 <= index < count:
+                sums[index].run(phase)
+                if phase == 4:
+                    put(index)
+        for act in between.get(turn, ()):
+            act()
 
     pair_copy(other).wait_recv()
     store(expand_wide.at[0], expand_out.at[:, 0 : expand_wide.shape[2]])
@@ -2070,14 +2351,6 @@
         one_sum.finish()
     line_sums.finish()
 
-    def ended(block, carried):
-        reply_copy(block).wait_send()
-        for shift in range(1, SQUARE):
-            home_copy(block, shift).wait_send()
-        return carried
-
-    lax.fori_loop(0, ROWS, ended, 0)
-
 
 def run_finish(
     own_latent,
@@ -2090,8 +2363,7 @@
     router_rows,
     premix,
     scaling,
-    hidden,
-    funnel,
+    home,
     one,
     query_grad,
     attended,
@@ -2101,7 +2373,6 @@
     narrow,
 ):
     tokens, width = residual.shape
-    picked = back.shape[2]
     sliced = own_latent.shape[0]
     wide = query_grad.shape[2]
     heads = attended.shape[2]
@@ -2113,7 +2384,7 @@
     def shape(*dims, dtype=f32):
         return jax.ShapeDtypeStruct(dims, dtype)
 
-    loaded = (hidden, funnel, one, query_grad, attended, branch, latent, expanded, narrow)
+    loaded = (home, one, query_grad, attended, branch, latent, expanded, narrow)
     return pl.pallas_call(
         finish_kernel,
         name="finish",
@@ -2125,15 +2396,10 @@
             shape(sliced, width),
             shape(*small),
         ),
-        in_specs=[whole] * 10 + [far] * 9,
+        in_specs=[whole] * 10 + [far] * 8,
         out_specs=(whole, far, far, far, far, whole),
         scratch_shapes=[
             *[VMEM(value.shape, bf16) for value in loaded],
-            VMEM((2, picked, width), f32),
-            VMEM((ROWS, picked, width), bf16),
-            VMEM((ROWS, picked, width), bf16),
-            VMEM((ROWS, picked, width), bf16),
-            VMEM((ROWS, picked, width), bf16),
             VMEM((ROWS, tokens, width), f32),
             VMEM((ROWS, tokens, width), bf16),
             VMEM((2, ROWS, tokens, width), bf16),
@@ -2149,8 +2415,6 @@
             VMEM(small, f32),
             DMA((len(loaded),)),
             DMA((10,)),
-            *pair_sems(),
-            *square_sems(),
             *sum_sems(),
             DMA((1,)),
             DMA((1,)),
@@ -2182,12 +2446,16 @@
     )
 
 
-def product_kernel(left_ref, right_ref, out_ref):
+def product_kernel(left_ref, right_ref, out_ref, turned):
     wide = 256
+
+    @pl.when(pl.program_id(1) == 0)
+    def _():
+        turned[...] = left_ref[0].T
 
     def one(index, carried):
         lanes = pl.ds(pl.multiple_of(index * wide, 128), wide)
-        out_ref[0, :, lanes] = tn(left_ref[0], right_ref[0, :, lanes])
+        out_ref[0, :, lanes] = nn(turned[...], right_ref[0, :, lanes])
         return carried
 
     lax.fori_loop(0, right_ref.shape[2] // wide, one, 0)
@@ -2206,6 +2474,7 @@
             pl.BlockSpec((1, slots, wide), lambda kind, half: (half, 0, 0)),
         ],
         out_specs=pl.BlockSpec((1, tall, wide), lambda kind, half: (kind, 0, half)),
+        scratch_shapes=[VMEM((tall, slots), bf16)],
         compiler_params=pltpu.CompilerParams(vmem_limit_bytes=40 * MIB),
         cost_estimate=pl.CostEstimate(
             flops=2 * kinds * halves * slots * tall * wide,
@@ -2253,14 +2522,14 @@
         latent_normed,
         attended,
         compress_all,
+        cot_blocks,
+        pick,
+        back,
+        cot_rows,
         residual,
         normed_two,
         scale_one,
         scale_two,
-        cot_blocks,
-        pick,
-        back,
-        cot_rows,
         router_all,
     ) = run_attention(
         activations,
@@ -2284,10 +2553,13 @@
         expert_rows,
         expert_gu_grad,
         expert_hidden,
+        shared_x,
+        shared_y,
+        shared_kept,
         hidden_blocks,
-        gu_blocks,
         premix_rows,
         router_rows,
+        reply_blocks,
     ) = run_experts(
         normed_two,
         pick,
@@ -2300,19 +2572,17 @@
         narrowing,
         router_all,
     )
-    cotangent_all = cot_blocks.reshape(seq_length, col_width)
-    gathered_two = two_blocks.reshape(seq_length, col_width)
-    hidden_all = hidden_blocks.reshape(seq_length, -1)
-    gu_grad_all = gu_blocks.reshape(2, seq_length, -1)
     slot_rows = expert_rows.reshape(col_count, slot_total, col_width)
     reply_grad_rows = cot_rows.reshape(col_count, slot_total, col_width)
     slot_hidden = expert_hidden.reshape(slot_total, -1)
     slot_gu_grad = expert_gu_grad.reshape(2, slot_total, -1)
-    narrowing_grad = dot_tn(hidden_all, cotangent_all)
-    widening_grad = jnp.einsum(
-        "gtf,td->gfd", gu_grad_all, gathered_two, preferred_element_type=f32
-    )
-    shared_sums = lax.psum((narrowing_grad.astype(bf16), widening_grad.astype(bf16)), "dp")
+    got_x = lax.ppermute(shared_x, "dp", [(i, i ^ 1) for i in range(SQUARE)])
+    got_y = lax.ppermute(shared_y, "dp", [(i, i ^ 2) for i in range(SQUARE)])
+    fanout_grad = slot_products(slot_gu_grad, slot_rows)
+    funnel_grad = slot_products(slot_hidden[None], reply_grad_rows)
+    normed_grad, fanout_grad, funnel_grad = lax.optimization_barrier(
+        (normed_grad, fanout_grad, funnel_grad)
+    )
     (
         input_grad,
         branch_blocks,
@@ -2321,6 +2591,7 @@
         own_latent_grad,
         scaling_rows,
         rescale_rows,
+        shared_sum,
     ) = run_attention_back(
         normed_grad,
         residual,
@@ -2342,11 +2613,7 @@
         queries,
         expand,
         combine,
-    )
-    fanout_grad = slot_products(slot_gu_grad, slot_rows)
-    funnel_grad = slot_products(slot_hidden[None], reply_grad_rows)
-    own_latent_grad, fanout_grad, funnel_grad = lax.optimization_barrier(
-        (own_latent_grad, fanout_grad, funnel_grad)
+        (shared_kept, got_x, got_y),
     )
     layer_output, queries_sum, combine_sum, expand_sum, compress_sum, small = run_finish(
         own_latent_grad,
@@ -2359,8 +2626,7 @@
         router_rows,
         premix,
         scaling,
-        expert_hidden,
-        funnel[0],
+        reply_blocks,
         one,
         query_grad,
         attended,
@@ -2380,8 +2646,8 @@
         combine_sum,
         small[expert_total],
         small[:expert_total].T,
-        shared_sums[1].astype(f32).transpose(0, 2, 1),
-        shared_sums[0].astype(f32),
+        shared_sum[1:].astype(f32).transpose(0, 2, 1),
+        shared_sum[0].astype(f32),
         fanout_grad.transpose(0, 2, 1)[None],
         funnel_grad,
     )

time: 395 us -> 340 us (0.86)
  Pallas kernels: 350 us -> 308 us
  between operations: 14.1 us -> 0.7 us
  matrix products: 6.61 us -> 0 us
    pallas_call x1, Pallas kernels: 106 us -> 72.9 us  [run_finish(): pl.pallas_call(finish_kernel, name='finish', out_shape=(shape(tokens, wid...]
    pallas_call x1, Pallas kernels: 76 us -> 64.2 us  [run_attention(): pl.pallas_call(attend_kernel, name='attend', out_shape=(*kept, shape(toke...]
    dot_general x2 -> x0, matrix products: 6.61 us -> none  [the longest x1 3.33 us: dot_tn(): lax.dot_general(left, right, (((0,), (0,)), ((), ())), preferred_element_...]
    unnamed x34 -> x30, local copies, waits for them, and re-layouts: 11.4 us -> 11.9 us
  transfers between devices with their start and end apart: 1 -> 2, of which waited for: 0 -> 2; matrix products, arithmetic and copies ran while one was open for 1% -> 0% of each run, Pallas kernels for 49% -> 5%
where the time goes in v3:
time: 340 us; the launch traced here: 338 us
  Pallas kernels  308 us (91%)
  local copies, waits for them, and re-layouts  16.1 us (5%)
  other arithmetic  8.51 us (3%)
    pallas_call x1, Pallas kernels, run_experts(): pl.pallas_call(expert_kernel, name='experts', out_shape=(shape(tokens, wi...  85.7 us
    pallas_call x1, Pallas kernels, run_finish(): pl.pallas_call(finish_kernel, name='finish', out_shape=(shape(tokens, wid...  72.9 us
    pallas_call x1, Pallas kernels, run_attention_back(): pl.pallas_call(attend_back_kernel, name='attend_back', out_shape=(shape(t...  67.4 us
    pallas_call x1, Pallas kernels, run_attention(): pl.pallas_call(attend_kernel, name='attend', out_shape=(*kept, shape(toke...  64.2 us
    pallas_call x2, Pallas kernels, slot_products(): pl.pallas_call(product_kernel, name='slot_products', grid=(kinds, halves)...  18 us
    unnamed x30, local copies, waits for them, and re-layouts  11.9 us
  transfers between devices with their start and end apart: 2, of which 2 were waited for; matrix products, arithmetic and copies ran while one was open for 0% of the time, Pallas kernels for 5%

profile of v3, /device:TPU:9, one launch (start us, length us, event | category | flops | bytes accessed | tf_op | source)
XLA Modules:
  0.0 337.9 jit_solution(5317495173578936557)
XLA Ops:
  0.6 64.2 %attend.1 = (bf16[4,128,1024]{2,1,0:T(8,128)(2,1)}, bf16[4,128,384]{2,1,0:T(8,128)(2,1)}, bf16[2,4,128,256]{3,2,1,0:T(8,128)(2,1)}, bf16[2,4,128,128]{3,2,1,0:T(...) custom-call(bf16[128,1024]{1,0:T(8,128)(2,1)} %act_ref.3, ...), custom_call_target="tpu_custom_call" | custom-call | flops 42949672960 | bytes 33554432 | tf_op jit(solution)/shard_map/attend/pallas_call | solution.py:924
  64.9 85.7 %experts.1 = (f32[128,1024]{1,0:T(8,128)}, bf16[4,128,1024]{2,1,0:T(8,128)(2,1)}, bf16[2,4,256,1024]{3,2,1,0:T(8,128)(2,1)}, bf16[2,4,256,704]{3,2,1,0:T(8,128)(...) custom-call(bf16[128,1024]{1,0:T(8,128)(2,1)} %get-tuple-element.60., ...), custom_call_target="tpu_custom_call" | custom-call | flops 64424509440 | bytes 67108864 | tf_op jit(solution)/shard_map/experts/pallas_call | solution.py:1951
  150.5 1.3 collective-permute-start
  151.9 0.3 collective-permute-start.1
  152.2 0.0 copy-start
  152.2 2.2 copy-done
  154.4 0.0 copy-start.1
  154.4 1.4 copy-done.1
  155.8 0.0 copy-start.2
  155.8 0.0 copy-start.3
  155.8 6.5 %slot_products.3 = f32[1,704,2048]{2,1,0:T(8,128)} custom-call(bf16[1,1024,704]{2,1,0:T(8,128)(2,1)S(1)} %bitcast.31, bf16[2,1024,1024]{2,1,0:T(8,128)(2,1)S(1)} %bitcast.30), custom_call_target="tpu_custom_call" | custom-call | flops 2952790016 | bytes 5767168 | tf_op jit(solution)/shard_map/slot_products/pallas_call | solution.py:2467
  162.3 0.0 copy-done.2
  162.3 0.0 copy-done.3
  162.3 11.5 %slot_products.2 = f32[2,704,2048]{2,1,0:T(8,128)} custom-call(bf16[2,1024,704]{2,1,0:T(8,128)(2,1)S(1)} %bitcast.33, bf16[2,1024,1024]{2,1,0:T(8,128)(2,1)S(1)} %bitcast.32), custom_call_target="tpu_custom_call" | custom-call | flops 5905580032 | bytes 11534336 | tf_op jit(solution)/shard_map/slot_products/pallas_call | solution.py:2467
  173.8 1.8 collective-permute-done.got_x_far
  175.6 0.0 copy-start.10
  175.6 1.0 collective-permute-done.1.got_y_far
  176.6 0.0 copy-start.11
  176.6 0.0 copy-done.10
  176.6 1.0 copy-done.11
  177.6 67.4 %attend_back.1 = (f32[128,1024]{1,0:T(8,128)}, bf16[4,128,1024]{2,1,0:T(8,128)(2,1)}, bf16[4,128,768]{2,1,0:T(8,128)(2,1)}, bf16[4,128,512]{2,1,0:T(8,128)(2,1)}...) custom-call(f32[128,1024]{1,0:T(8,128)} %get-tuple-element.70.normed_grad_ref,, ...), custom_call_target="tpu_custom_call" | custom-call | flops 42949672960 | bytes 33554432 | tf_op jit(solution)/shard_map/attend_back/pallas_call | solution.py:1434
  245.0 72.9 %finish.1 = (bf16[128,1024]{1,0:T(8,128)(2,1)}, f32[1024,768]{1,0:T(8,128)}, f32[512,1024]{1,0:T(8,128)}, f32[512,1024]{1,0:T(8,128)}, f32[144,1024]{1,0:T(8,128)}, /*index=5*/f32[24,1024]{1,0:T(8,128)}) custom-call(bf16[144,512]{1,0:T(8,128)(2,1)} %get-tuple-element.84.own_latent_ref, bf16[4,128,256]{2,1,0:T(8,128)(2,1)} %get-tuple-element.62.back_ref, ...), custom_call_target="tpu_custom_call" | custom-call | flops 42949672960 | bytes 67108864 | tf_op jit(solution)/shard_map/finish/pallas_call | solution.py:2388
  317.9 1.3 slice.19
  319.2 1.4 fusion
  320.7 1.5 slice_bitcast_fusion
  322.1 3.3 bitcast_convert_fusion
  325.4 0.0 copy-start.9
  325.4 0.0 copy-start.8
  325.4 0.0 copy-start.4
  325.4 5.2 %convert_bitcast_fusion = f32[2,1024,704]{1,2,0:T(8,128)} fusion(bf16[3,704,1024]{2,1,0:T(8,128)(2,1)} %get-tuple-element.103), kind=kLoop, calls=%fused_computation | loop fusion | flops 1441792 | bytes 8650752 | tf_op jit(solution)/shard_map/transpose | solution.py:2649
  330.7 0.0 copy-done.9
  330.7 0.7 copy.40
  331.4 0.0 copy-done.8
  331.4 0.8 copy.41
  332.2 0.0 copy-done.4
  332.2 0.0 copy-start.7
  332.2 0.0 copy-start.6
  332.2 1.7 copy.42
  333.8 0.0 copy-done.7
  333.8 0.0 copy-start.5
  333.8 0.8 copy.43
  334.6 0.6 copy-done.6
  335.3 1.3 copy.44
  336.6 0.0 copy-done.5
  336.6 1.3 copy.45
Async XLA Ops:
  150.5 25.1 %collective-permute-start = (bf16[3,704,256]{2,1,0:T(8,128)(2,1)}, bf16[3,704,256]{2,1,0:T(8,128)(2,1)S(1)}, u32[]{:S(2)}, u32[]{:S(2)}) collective-permute-start(bf16[3,704,256]{2,1,0:T(8,128)(2,1)} %get-tuple-element.82), channel_id=1, source_target_pairs={{0,8},{8,0},{16,24},{24,16},{1,9},{9,1},{17,25},{25,17},{2,10},{10... | collective-permute-start | bytes 3244040 | tf_op jit(solution)/shard_map/ppermute | solution.py:2579
  151.9 24.7 %collective-permute-start.1 = (bf16[3,704,256]{2,1,0:T(8,128)(2,1)}, bf16[3,704,256]{2,1,0:T(8,128)(2,1)S(1)}, u32[]{:S(2)}, u32[]{:S(2)}) collective-permute-start(bf16[3,704,256]{2,1,0:T(8,128)(2,1)} %get-tuple-element.83), channel_id=1, source_target_pairs={{0,16},{8,24},{16,0},{24,8},{1,17},{9,25},{17,1},{25,9},{2,18},{10... | collective-permute-start | bytes 3244040 | tf_op jit(solution)/shard_map/ppermute | solution.py:2580
  152.2 2.2 copy-start
  154.4 1.4 copy-start.1
  155.8 6.5 %copy-start.2 = (bf16[2,4,256,1024]{3,2,1,0:T(8,128)(2,1)S(1)}, bf16[2,4,256,1024]{3,2,1,0:T(8,128)(2,1)}, u32[]{:S(2)}) copy-start(bf16[2,4,256,1024]{3,2,1,0:T(8,128)(2,1)} %get-tuple-element.68) | copy-start | bytes 12582916
  155.8 6.5 %copy-start.3 = (bf16[2,4,256,704]{3,2,1,0:T(8,128)(2,1)S(1)}, bf16[2,4,256,704]{3,2,1,0:T(8,128)(2,1)}, u32[]{:S(2)}) copy-start(bf16[2,4,256,704]{3,2,1,0:T(8,128)(2,1)} %get-tuple-element.67) | copy-start | bytes 8650756
  175.6 1.0 copy-start.10
  176.6 1.0 copy-start.11
  325.4 5.2 %copy-start.9 = (bf16[128,1024]{1,0:T(8,128)(2,1)S(1)}, bf16[128,1024]{1,0:T(8,128)(2,1)}, u32[]{:S(2)}) copy-start(bf16[128,1024]{1,0:T(8,128)(2,1)} %get-tuple-element.122) | copy-start | bytes 786436
  325.4 5.9 %copy-start.8 = (f32[128,1024]{1,0:T(8,128)S(1)}, f32[128,1024]{1,0:T(8,128)}, u32[]{:S(2)}) copy-start(f32[128,1024]{1,0:T(8,128)} %get-tuple-element.123) | copy-start | bytes 1572868
  325.4 6.7 %copy-start.4 = (f32[1024,768]{1,0:T(8,128)S(1)}, f32[1024,768]{1,0:T(8,128)}, u32[]{:S(2)}) copy-start(f32[1024,768]{1,0:T(8,128)} %get-tuple-element.125) | copy-start | bytes 9437188
  332.2 1.7 copy-start.7
  332.2 3.1 copy-start.6
  333.8 2.8 copy-start.5

commit v4 on v3

--- a/solution.py
+++ b/solution.py
@@ -1,3 +1,5 @@
+import functools
+
 import jax
 import jax.numpy as jnp
 import numpy as np
@@ -1021,14 +1023,28 @@
     kept_far,
     got_x_far,
     got_y_far,
+    attended_far,
+    normed_latent_far,
+    narrow_far,
+    home_far,
+    back_far,
+    shared_far,
+    premix_far,
+    router_far,
     input_grad_ref,
+    output_ref,
+    small_ref,
+    shared_sum,
+    queries_out,
+    combine_out,
+    expand_out,
+    compress_out,
     branch_ref,
     query_grad_ref,
     expanded_ref,
     own_latent_ref,
     scaling_rows,
     rescale_rows,
-    shared_sum,
     combine,
     query_ref,
     key_ref,
@@ -1048,6 +1064,14 @@
     middle,
     second,
     result,
+    attended,
+    normed_latent,
+    narrow,
+    home,
+    back_ref,
+    shared_ref,
+    premix_rows,
+    router_rows,
     stat_to,
     stat_from,
     grad_own,
@@ -1084,6 +1108,21 @@
     rest_sent,
     rest_arrived,
     rest_sem,
+    reply_coming,
+    small_to,
+    small_from,
+    small_line,
+    small_square,
+    small_own,
+    expand_other,
+    store_sem,
+    reply_sent,
+    reply_arrived,
+    pair_sent,
+    pair_arrived,
+    small_sent,
+    small_arrived,
+    *sums_scratch,
 ):
     place, row, col = lax.axis_index("dp"), lax.axis_index("row"), lax.axis_index("col")
     other = 1 - col
@@ -1116,6 +1155,14 @@
                 (kept_far, kept),
                 (got_x_far, got.at[0]),
                 (got_y_far, got.at[1]),
+                (attended_far, attended),
+                (normed_latent_far, normed_latent),
+                (narrow_far, narrow),
+                (home_far, home),
+                (back_far, back_ref),
+                (shared_far, shared_ref),
+                (premix_far, premix_rows),
+                (router_far, router_rows),
             ]
         )
     ]
@@ -1156,6 +1203,161 @@
 
     rest = SquareRest(place, kept, got, middle, second, result, rest_sent, rest_arrived)
 
+    line_sums = SumLine(
+        row, part, leaving, reply_coming, reply_sent, reply_arrived
+    )
+    experts = router_rows.shape[0]
+    kinds = [sums_scratch[7 * i : 7 * i + 7] for i in range(4)]
+    parts = [scratch[0] for scratch in kinds]
+    plan = [(kind, chunk) for kind in range(4) for chunk in range(parts[kind].shape[0])]
+    pieces_of = [
+        SquareSum(place, *[ref.at[chunk] for ref in kinds[kind]]) for kind, chunk in plan
+    ]
+    count = len(plan)
+
+    def begin(index):
+        kind, chunk = plan[index]
+        part_ref = parts[kind]
+        if kind == 0 and chunk == 0:
+            loads[17].wait()
+        if kind == 2:
+            loads[18].wait()
+        if kind < 2:
+            left, right = ((attended, branch_ref), (one_ref, query_grad_ref))[kind]
+            height = 8 * part_ref.shape[2]
+            piece = left[:, :, chunk * height : (chunk + 1) * height].reshape(seq, height)
+            grad = tn(piece, right[...].reshape(seq, right.shape[2]))
+        elif kind == 2:
+            grad = tn(
+                normed_latent[...].reshape(seq, RANK),
+                expanded_ref[...].reshape(seq, expanded_ref.shape[2]),
+            )
+        else:
+            grad = nn(own_latent_ref[...], one_ref[...].reshape(seq, width)).astype(bf16)
+            for piece in range(8):
+                part_ref[0, piece] = grad[:, piece * (width // 8) : (piece + 1) * (width // 8)]
+        if kind < 3:
+            part_ref[chunk] = grad.astype(bf16).reshape(part_ref.shape[1:])
+        pieces_of[index].run(0)
+
+    stores = []
+
+    def store(source, target):
+        copy = pltpu.make_async_copy(source, target, store_sem.at[len(stores)])
+        copy.start()
+        stores.append(copy)
+
+    def pair_copy():
+        return remote(kinds[2][4].at[0], expand_other, pair_sent.at[0], pair_arrived.at[0], sibling)
+
+    def expand_lanes(half):
+        wide = expand_other.shape[2]
+        return expand_out.at[:, :, pl.ds(pl.multiple_of(half * wide, 128), wide)]
+
+    def put(index):
+        kind, chunk = plan[index]
+        done = kinds[kind][4]
+        if kind < 2:
+            store(done.at[chunk], (combine_out, queries_out)[kind].at[chunk])
+        elif kind == 2:
+            store(done.at[0], expand_lanes(col))
+            pair_copy().start()
+        else:
+            lanes = width // 8
+            for piece in range(8):
+                store(done.at[0, piece], compress_out.at[:, piece * lanes : (piece + 1) * lanes])
+
+    def advance(turn):
+        for phase in (1, 2, 3, 4):
+            index = turn - phase
+            if 0 <= index < count:
+                pieces_of[index].run(phase)
+                if phase == 4:
+                    put(index)
+        if 2 <= turn < count:
+            begin(turn)
+
+    def reply_add(turn, carried):
+        block = block_at(row, ROWS - 1 - turn)
+        part[block] = nn(back_ref[block], home[block]) + nn(shared_ref[block], narrow[...])
+        line_sums.begin(block)
+        return carried
+
+    def small_copy(step):
+        if step == 0:
+            return remote(small_to, small_from, small_sent.at[0], small_arrived.at[0], sibling)
+        if step < ROWS:
+            return remote(
+                small_own,
+                small_line.at[step],
+                small_sent.at[step],
+                small_arrived.at[step],
+                {"row": lax.rem(row + step, ROWS)},
+            )
+        shift = step - ROWS + 1
+        return remote(
+            small_ref,
+            small_square.at[shift],
+            small_sent.at[step],
+            small_arrived.at[step],
+            {"dp": partner(place, shift)},
+        )
+
+    def small_begin():
+        loads[23].wait()
+        loads[24].wait()
+        rescale_row = jnp.sum(rescale_rows[...], axis=0, keepdims=True)
+        empty = jnp.zeros((small_own.shape[0] - experts, width), f32)
+        small_to[0:experts] = router_rows[:, pl.ds(pl.multiple_of(other * width, width), width)]
+        small_to[experts:] = empty
+        small_to[experts + 2 : experts + 3, 0:RANK] = rescale_row
+        small_copy(0).start()
+        small_own[0:experts] = router_rows[:, pl.ds(pl.multiple_of(col * width, width), width)]
+        small_own[experts:] = empty
+        small_own[experts : experts + 1] = (
+            jnp.sum(premix_rows[...], axis=0, keepdims=True) / premix_ref[...]
+        )
+        small_own[experts + 1 : experts + 2] = (
+            jnp.sum(scaling_rows[...], axis=0, keepdims=True) / scaling_ref[...]
+        )
+        small_own[experts + 2 : experts + 3, 0:RANK] = rescale_row
+
+    def small_line_begin():
+        small_copy(0).wait_recv()
+        small_own[...] += small_from[...]
+        for step in range(1, ROWS):
+            small_copy(step).start()
+
+    def small_square_begin():
+        for step in range(1, ROWS):
+            small_copy(step).wait_recv()
+        small_ref[...] = small_own[...] + small_line[1] + small_line[2] + small_line[3]
+        for step in range(ROWS, ROWS + SQUARE - 1):
+            small_copy(step).start()
+
+    def small_end():
+        for step in range(ROWS, ROWS + SQUARE - 1):
+            small_copy(step).wait_recv()
+        for step in range(ROWS, ROWS + SQUARE - 1):
+            small_copy(step).wait_send()
+        small_ref[...] += small_square[1] + small_square[2] + small_square[3]
+
+    def reply_begin():
+        for load in loads[19:23]:
+            load.wait()
+        lax.fori_loop(0, ROWS, reply_add, 0)
+
+    def reply_pass():
+        lax.fori_loop(0, 3, line_pass, 0)
+
+    def reply_end():
+        line_sums.total(total)
+        output_ref[...] = (total[...] + residual_ref[...]).astype(bf16)
+
+    def line_pass(turn, carried):
+        line_sums.pass_on(block_at(row, jnp.where(turn == 0, 3, turn)))
+        return carried
+
     def grad_copy(block):
         return remote(
             grad_to.at[block],
@@ -1188,7 +1390,7 @@
 
         @pl.when(step == 0)
         def _():
-            for load in loads[14:]:
+            for load in loads[14:17]:
                 load.wait()
             rest.run(1)
             loads[0].wait()
@@ -1256,6 +1458,8 @@
     lax.fori_loop(0, ROWS + 1, turn, 0)
     for load in loads[8:14]:
         load.wait()
+    begin(0)
+    begin(1)
 
     def latents(turn, carried):
         block = block_at(row, ROWS - 1 - turn)
@@ -1324,11 +1528,10 @@
     for step in range(1, ROWS):
         turned_copy(step).start()
 
-    def hand_on(turn, carried):
-        sums.pass_on(block_at(row, jnp.where(turn == 0, 3, turn)))
-        return carried
-
-    lax.fori_loop(0, 3, hand_on, 0)
+    advance(1)
+    for turn in range(3):
+        sums.pass_on(block_at(row, 3 if turn == 0 else turn))
+        advance(turn + 2)
     for step in range(1, ROWS):
         turned_copy(step).wait_recv()
     half = pl.ds(pl.multiple_of(col * (seq // COLS), 128), seq // COLS)
@@ -1344,7 +1547,15 @@
         return remote(here, here, own_sent.at[0], own_arrived.at[0], sibling)
 
     own_copy(col).start()
+    advance(5)
     sums.total(total)
+    input_grad_ref[...] += norm_grad(
+        act_ref[...].astype(f32), scale_one_ref[...], scaling_ref[...], total[...], 1
+    )
+    sums.finish()
+    reply_begin()
+    small_begin()
+    advance(6)
     rest.run(4)
     pieces = [
         pltpu.make_async_copy(
@@ -1354,11 +1565,19 @@
     ]
     for piece in pieces:
         piece.start()
-    input_grad_ref[...] += norm_grad(
-        act_ref[...].astype(f32), scale_one_ref[...], scaling_ref[...], total[...], 1
-    )
+    small_line_begin()
     own_copy(other).wait_recv()
     own_copy(col).wait_send()
+    advance(7)
+    advance(8)
+    reply_pass()
+    small_square_begin()
+    for turn in range(9, count + 5):
+        advance(turn)
+    reply_end()
+    small_end()
+    pair_copy().wait_recv()
+    store(expand_other, expand_lanes(other))
 
     def ended(block, carried):
         grad_copy(block).wait_send()
@@ -1373,8 +1592,15 @@
     stat_copy(1).wait_send()
     for piece in pieces:
         piece.wait()
+    for copy in stores:
+        copy.wait()
+    pair_copy().wait_send()
+    for step in range(ROWS):
+        small_copy(step).wait_send()
+    for one_sum in pieces_of:
+        one_sum.finish()
+    line_sums.finish()
     rest.finish()
-    sums.finish()
     line.finish()
 
 
@@ -1400,6 +1626,7 @@
     expand,
     combine,
     shared,
+    more,
 ):
     tokens, width = activations.shape
     seq = ROWS * tokens
@@ -1414,6 +1641,9 @@
         return jax.ShapeDtypeStruct(dims, dtype)
 
     kept, got_x, got_y = shared
+    heads = more[0].shape[2]
+    own_heads = 2 * (NOPE + HEADV)
+    small = (24, width)
     piece = kept.shape[1:3] + (kept.shape[3] // 2,)
     loaded = (
         combine,
@@ -1436,23 +1666,30 @@
         name="attend_back",
         out_shape=(
             shape(tokens, width, dtype=f32),
-            shape(ROWS, tokens, width),
-            shape(ROWS, tokens, COLS * mine),
-            shape(ROWS, tokens, 2 * (NOPE + HEADV)),
-            shape(sliced, seq),
-            shape(8, width, dtype=f32),
-            shape(8, RANK, dtype=f32),
+            shape(tokens, width),
+            shape(*small, dtype=f32),
             shape(*kept.shape[1:3], width),
+            shape(4, 8, width // 32, COLS * mine),
+            shape(2, 8, heads // 16, width),
+            shape(8, RANK // 8, COLS * own_heads),
+            shape(sliced, width),
         ),
-        in_specs=[whole] * 9 + [far] * 17,
-        out_specs=(whole,) * 7 + (far,),
+        in_specs=[whole] * 9 + [far] * 25,
+        out_specs=(whole,) * 3 + (far,) * 5,
         scratch_shapes=[
+            VMEM((ROWS, tokens, width), bf16),
+            VMEM((ROWS, tokens, COLS * mine), bf16),
+            VMEM((ROWS, tokens, own_heads), bf16),
+            VMEM((sliced, seq), bf16),
+            VMEM((8, width), f32),
+            VMEM((8, RANK), f32),
             *[VMEM(value.shape, value.dtype) for value in loaded],
             VMEM(kept.shape, bf16),
             VMEM(kept.shape, bf16),
             VMEM((2,) + piece, bf16),
             VMEM((2,) + piece, bf16),
             VMEM((8,) + piece, bf16),
+            *[VMEM(value.shape, value.dtype) for value in more],
             VMEM((2, tokens, 128), f32),
             VMEM((2, tokens, 128), f32),
             VMEM((ROWS, tokens, 2 * HEADV), f32),
@@ -1469,7 +1706,7 @@
             VMEM((ROWS, tokens, width), bf16),
             VMEM((2, ROWS, tokens, width), bf16),
             VMEM((tokens, width), f32),
-            DMA((17,)),
+            DMA((25,)),
             DMA((2,)),
             DMA((2,)),
             *line_sems(),
@@ -1482,9 +1719,26 @@
             DMA((8,)),
             DMA((8,)),
             DMA((8,)),
+            VMEM((2, ROWS, tokens, width), bf16),
+            VMEM(small, f32),
+            VMEM(small, f32),
+            VMEM((ROWS,) + small, f32),
+            VMEM((SQUARE,) + small, f32),
+            VMEM(small, f32),
+            VMEM((8, RANK // 8, own_heads), bf16),
+            DMA((16,)),
+            *sum_sems(),
+            DMA((1,)),
+            DMA((1,)),
+            DMA((ROWS + SQUARE - 1,)),
+            DMA((ROWS + SQUARE - 1,)),
+            *square_scratch((2, heads // 16, width)),
+            *square_scratch((4, width // 32, COLS * mine)),
+            *square_scratch((1, RANK // 8, own_heads)),
+            *square_scratch((1, sliced, width // 8)),
         ],
         compiler_params=pltpu.CompilerParams(
-            collective_id=3, has_side_effects=True, vmem_limit_bytes=56 * MIB
+            collective_id=3, has_side_effects=True, vmem_limit_bytes=62 * MIB
         ),
         cost_estimate=pl.CostEstimate(
             flops=40 * 1024**3, bytes_accessed=32 * MIB, transcendentals=0
@@ -1503,6 +1757,7 @@
         kept,
         got_x,
         got_y,
+        *more,
     )
 
 
@@ -2090,360 +2345,50 @@
     ]
 
 
-def finish_kernel(
-    own_latent_ref,
-    back_ref,
-    shared_ref,
-    residual_ref,
-    premix_rows,
-    scaling_rows,
-    rescale_rows,
-    router_rows,
-    premix_ref,
-    scaling_ref,
-    home_ref,
-    one_ref,
-    query_grad_ref,
-    attended_ref,
-    branch_ref,
-    latent_ref,
-    expanded_ref,
-    narrow_ref,
-    output_ref,
-    queries_out,
-    combine_out,
-    expand_out,
-    compress_out,
-    small_ref,
-    home,
-    one,
-    query_grad,
-    attended,
-    branch,
-    latent,
-    expanded,
-    narrow,
-    part,
-    leaving,
-    coming,
-    total,
-    queries_wide,
-    combine_wide,
-    expand_wide,
-    compress_wide,
-    small_to,
-    small_from,
-    small_line,
-    small_square,
-    small_own,
-    load_sem,
-    store_sem,
-    sum_sent,
-    sum_arrived,
-    pair_sent,
-    pair_arrived,
-    small_sent,
-    small_arrived,
-    *sums_scratch,
-):
-    place, row, col = lax.axis_index("dp"), lax.axis_index("row"), lax.axis_index("col")
-    other = 1 - col
-    sibling = {"col": other}
-    tokens, width = output_ref.shape
-    seq = ROWS * tokens
-    experts = router_rows.shape[0]
+def write_kernel(count, plan, *refs):
+    sources, targets = refs[:count], refs[count : count + len(plan)]
+    rest = refs[count + len(plan) :]
+    held, wide = rest[:count], rest[count : count + len(plan)]
+    load_sem, store_sem = rest[count + len(plan) :]
     loads = [
-        pltpu.make_async_copy(source, target, load_sem.at[i])
-        for i, (source, target) in enumerate(
-            [
-                (narrow_ref, narrow),
-                (home_ref, home),
-                (one_ref, one),
-                (query_grad_ref, query_grad),
-                (attended_ref, attended),
-                (branch_ref, branch),
-                (latent_ref, latent),
-                (expanded_ref, expanded),
-            ]
-        )
+        pltpu.make_async_copy(sources[i], held[i], load_sem.at[i]) for i in range(count)
+    ]
+    stores = [
+        pltpu.make_async_copy(wide[i], targets[i], store_sem.at[i]) for i in range(len(plan))
     ]
     for load in loads:
         load.start()
-    greet(row, place, col, line=True, square=True)
-    line_sums = SumLine(row, part, leaving, coming, sum_sent, sum_arrived)
-
-    def reply_add(turn, carried):
-        block = block_at(row, ROWS - 1 - turn)
-        part[block] = nn(back_ref[block], home[block]) + nn(shared_ref[block], narrow[...])
-        line_sums.begin(block)
-        return carried
-
-    kinds = [sums_scratch[7 * i : 7 * i + 7] for i in range(4)]
-    sums = []
-    for scratch in kinds:
-        for index in range(scratch[0].shape[0]):
-            sums.append(SquareSum(place, *[ref.at[index] for ref in scratch]))
-    parts = [scratch[0] for scratch in kinds]
-    counts = [ref.shape[0] for ref in parts]
-    def begin(index):
-        kind, chunk = 0, index
-        while chunk >= counts[kind]:
-            chunk -= counts[kind]
-            kind += 1
-        if chunk == 0:
-            for load in loads[2 + 2 * min(kind, 3) :][: 2 if kind < 3 else 0]:
-                load.wait()
-        if kind < 2:
-            left, right = ((one, query_grad), (attended, branch))[kind]
-            height = 8 * parts[kind].shape[2]
-            piece = left[:, :, chunk * height : (chunk + 1) * height].reshape(seq, height)
-            grad = tn(piece, right[...].reshape(seq, right.shape[2]))
-        elif kind == 2:
-            grad = tn(latent[...].reshape(seq, RANK), expanded[...].reshape(seq, expanded.shape[2]))
-        else:
-            grad = nn(own_latent_ref[...], one[...].reshape(seq, width)).astype(bf16)
-            for piece in range(8):
-                parts[3][0, piece] = grad[:, piece * (width // 8) : (piece + 1) * (width // 8)]
-        if kind < 3:
-            parts[kind][chunk] = grad.astype(bf16).reshape(parts[kind].shape[1:])
-        sums[index].run(0)
-
-    ahead = 3
-    for index in range(ahead):
-        begin(index)
-
-    def small_copy(step):
-        if step == 0:
-            return remote(small_to, small_from, small_sent.at[0], small_arrived.at[0], sibling)
-        if step < ROWS:
-            return remote(
-                small_own,
-                small_line.at[step],
-                small_sent.at[step],
-                small_arrived.at[step],
-                {"row": lax.rem(row + step, ROWS)},
-            )
-        shift = step - ROWS + 1
-        return remote(
-            small_ref,
-            small_square.at[shift],
-            small_sent.at[step],
-            small_arrived.at[step],
-            {"dp": partner(place, shift)},
-        )
-
-    def small_begin():
-        rescale_row = jnp.sum(rescale_rows[...], axis=0, keepdims=True)
-        empty = jnp.zeros((small_own.shape[0] - experts, width), f32)
-        small_to[0:experts] = router_rows[:, pl.ds(pl.multiple_of(other * width, width), width)]
-        small_to[experts:] = empty
-        small_to[experts + 2 : experts + 3, 0:RANK] = rescale_row
-        small_copy(0).start()
-        small_own[0:experts] = router_rows[:, pl.ds(pl.multiple_of(col * width, width), width)]
-        small_own[experts:] = empty
-        small_own[experts : experts + 1] = (
-            jnp.sum(premix_rows[...], axis=0, keepdims=True) / premix_ref[...]
-        )
-        small_own[experts + 1 : experts + 2] = (
-            jnp.sum(scaling_rows[...], axis=0, keepdims=True) / scaling_ref[...]
-        )
-        small_own[experts + 2 : experts + 3, 0:RANK] = rescale_row
-
-    def small_line_begin():
-        small_copy(0).wait_recv()
-        small_own[...] += small_from[...]
-        for step in range(1, ROWS):
-            small_copy(step).start()
-
-    def small_square_begin():
-        for step in range(1, ROWS):
-            small_copy(step).wait_recv()
-        small_ref[...] = small_own[...] + small_line[1] + small_line[2] + small_line[3]
-        for step in range(ROWS, ROWS + SQUARE - 1):
-            small_copy(step).start()
-
-    def small_end():
-        for step in range(ROWS, ROWS + SQUARE - 1):
-            small_copy(step).wait_recv()
-        for step in range(ROWS, ROWS + SQUARE - 1):
-            small_copy(step).wait_send()
-        small_ref[...] += small_square[1] + small_square[2] + small_square[3]
-
-    def reply_begin():
-        loads[0].wait()
-        loads[1].wait()
-        lax.fori_loop(0, ROWS, reply_add, 0)
-
-    def reply_pass():
-        lax.fori_loop(0, 3, line_pass, 0)
-
-    def reply_end():
-        line_sums.total(total)
-        output_ref[...] = (total[...] + residual_ref[...]).astype(bf16)
-
-    def line_pass(turn, carried):
-        line_sums.pass_on(block_at(row, jnp.where(turn == 0, 3, turn)))
-        return carried
-
-    stores = []
-
-    def store(source, target):
-        copy = pltpu.make_async_copy(source, target, store_sem.at[len(stores)])
-        copy.start()
-        stores.append(copy)
-
-    def pair_copy(half):
-        here = expand_wide.at[half]
-        return remote(here, here, pair_sent.at[0], pair_arrived.at[0], sibling)
-
-    def put(index):
-        kind, chunk = 0, index
-        while chunk >= counts[kind]:
-            chunk -= counts[kind]
-            kind += 1
-        result = kinds[kind][4][chunk]
-        pieces, rows, lanes = result.shape
-        if kind < 2:
-            wide, out = ((queries_wide, queries_out), (combine_wide, combine_out))[kind]
-            here = pl.ds(chunk * pieces * rows, pieces * rows)
-            wide[here] = result.astype(f32).reshape(pieces * rows, lanes)
-            store(wide.at[here], out.at[here])
-        elif kind == 2:
-            expand_wide[col] = result.astype(f32).reshape(pieces * rows, lanes)
-            pair_copy(col).start()
-        else:
-            for piece in range(pieces):
-                compress_wide[:, piece * lanes : (piece + 1) * lanes] = result[piece].astype(f32)
-            store(compress_wide, compress_out)
-
-    count = len(sums)
-    between = {
-        0: (reply_begin, small_begin),
-        1: (small_line_begin,),
-        4: (reply_pass,),
-        5: (small_square_begin,),
-        count - 1: (reply_end,),
-        count + 1: (small_end,),
-    }
-    for turn in range(count + 3):
-        if turn < count:
-            sums[turn].run(1)
-        if turn + ahead < count:
-            begin(turn + ahead)
-        for phase in (2, 3, 4):
-            index = turn + 1 - phase
-            if 0 <= index < count:
-                sums[index].run(phase)
-                if phase == 4:
-                    put(index)
-        for act in between.get(turn, ()):
-            act()
-
-    pair_copy(other).wait_recv()
-    store(expand_wide.at[0], expand_out.at[:, 0 : expand_wide.shape[2]])
-    store(expand_wide.at[1], expand_out.at[:, expand_wide.shape[2] :])
-    for copy in stores:
-        copy.wait()
-    pair_copy(col).wait_send()
-    for step in range(ROWS):
-        small_copy(step).wait_send()
-    for one_sum in sums:
-        one_sum.finish()
-    line_sums.finish()
-
-
-def run_finish(
-    own_latent,
-    back,
-    shared,
-    residual,
-    premix_rows,
-    scaling_rows,
-    rescale_rows,
-    router_rows,
-    premix,
-    scaling,
-    home,
-    one,
-    query_grad,
-    attended,
-    branch,
-    latent,
-    expanded,
-    narrow,
-):
-    tokens, width = residual.shape
-    sliced = own_latent.shape[0]
-    wide = query_grad.shape[2]
-    heads = attended.shape[2]
-    own_heads = expanded.shape[2]
-    small = (24, width)
-    whole = pl.BlockSpec(memory_space=VMEM)
+    waited = set()
+    for i, (source, where) in enumerate(plan):
+        if source not in waited:
+            loads[source].wait()
+            waited.add(source)
+        wide[i][...] = held[source][where].astype(wide[i].dtype)
+        stores[i].start()
+    for store in stores:
+        store.wait()
+
+
+def write_out(arrays, plan):
     far = pl.BlockSpec(memory_space=pl.ANY)
-
-    def shape(*dims, dtype=f32):
-        return jax.ShapeDtypeStruct(dims, dtype)
-
-    loaded = (home, one, query_grad, attended, branch, latent, expanded, narrow)
+    shapes = [jax.ShapeDtypeStruct(shape, dtype) for _, _, shape, dtype in plan]
     return pl.pallas_call(
-        finish_kernel,
-        name="finish",
-        out_shape=(
-            shape(tokens, width, dtype=bf16),
-            shape(width, wide),
-            shape(heads, width),
-            shape(RANK, COLS * own_heads),
-            shape(sliced, width),
-            shape(*small),
+        functools.partial(
+            write_kernel, len(arrays), [(source, where) for source, where, _, _ in plan]
         ),
-        in_specs=[whole] * 10 + [far] * 8,
-        out_specs=(whole, far, far, far, far, whole),
+        name="write_out",
+        out_shape=shapes,
+        in_specs=[far] * len(arrays),
+        out_specs=[far] * len(plan),
         scratch_shapes=[
-            *[VMEM(value.shape, bf16) for value in loaded],
-            VMEM((ROWS, tokens, width), f32),
-            VMEM((ROWS, tokens, width), bf16),
-            VMEM((2, ROWS, tokens, width), bf16),
-            VMEM((tokens, width), f32),
-            VMEM((width, wide), f32),
-            VMEM((heads, width), f32),
-            VMEM((COLS, RANK, own_heads), f32),
-            VMEM((sliced, width), f32),
-            VMEM(small, f32),
-            VMEM(small, f32),
-            VMEM((ROWS,) + small, f32),
-            VMEM((SQUARE,) + small, f32),
-            VMEM(small, f32),
-            DMA((len(loaded),)),
-            DMA((10,)),
-            *sum_sems(),
-            DMA((1,)),
-            DMA((1,)),
-            DMA((ROWS + SQUARE - 1,)),
-            DMA((ROWS + SQUARE - 1,)),
-            *square_scratch((4, width // 32, wide)),
-            *square_scratch((2, heads // 16, width)),
-            *square_scratch((1, RANK // 8, own_heads)),
-            *square_scratch((1, sliced, width // 8)),
+            *[VMEM(array.shape, array.dtype) for array in arrays],
+            *[VMEM(shape.shape, shape.dtype) for shape in shapes],
+            DMA((len(arrays),)),
+            DMA((len(plan),)),
         ],
-        compiler_params=pltpu.CompilerParams(
-            collective_id=4, has_side_effects=True, vmem_limit_bytes=60 * MIB
-        ),
-        cost_estimate=pl.CostEstimate(
-            flops=40 * 1024**3, bytes_accessed=64 * MIB, transcendentals=0
-        ),
-    )(
-        own_latent,
-        back,
-        shared,
-        residual,
-        premix_rows,
-        scaling_rows,
-        rescale_rows,
-        router_rows,
-        premix.reshape(1, width),
-        scaling.reshape(1, width),
-        *loaded,
-    )
+        compiler_params=pltpu.CompilerParams(vmem_limit_bytes=62 * MIB),
+        cost_estimate=pl.CostEstimate(flops=0, bytes_accessed=24 * MIB, transcendentals=0),
+    )(*arrays)
 
 
 def product_kernel(left_ref, right_ref, out_ref, turned):
@@ -2585,13 +2530,13 @@
     )
     (
         input_grad,
-        branch_blocks,
-        query_grad,
-        expanded_grad,
-        own_latent_grad,
-        scaling_rows,
-        rescale_rows,
+        layer_output,
+        small,
         shared_sum,
+        queries_sum,
+        combine_sum,
+        expand_sum,
+        compress_sum,
     ) = run_attention_back(
         normed_grad,
         residual,
@@ -2614,40 +2559,71 @@
         expand,
         combine,
         (shared_kept, got_x, got_y),
-    )
-    layer_output, queries_sum, combine_sum, expand_sum, compress_sum, small = run_finish(
-        own_latent_grad,
-        back,
-        hidden_blocks,
-        residual,
-        premix_rows,
-        scaling_rows,
-        rescale_rows,
-        router_rows,
-        premix,
-        scaling,
-        reply_blocks,
-        one,
-        query_grad,
-        attended,
-        branch_blocks,
-        latent_normed,
-        expanded_grad,
-        narrowing,
+        (
+            attended,
+            latent_normed,
+            narrowing,
+            reply_blocks,
+            back,
+            hidden_blocks,
+            premix_rows,
+            router_rows,
+        ),
+    )
+    everything = slice(None)
+    share = narrowing.shape[0]
+    (
+        widening_grad,
+        narrowing_grad,
+        queries_grad,
+        combine_grad,
+        expand_grad,
+        compress_grad,
+        input_grad,
+        layer_output,
+        router_grad,
+        premix_grad,
+        scaling_grad,
+        rescale_grad,
+    ) = write_out(
+        (
+            shared_sum,
+            queries_sum.reshape(queries.shape),
+            combine_sum.reshape(combine.shape),
+            expand_sum.reshape(expand.shape),
+            compress_sum,
+            input_grad,
+            layer_output,
+            small,
+        ),
+        (
+            (0, slice(1, 3), (2, share, col_width), f32),
+            (0, 0, (share, col_width), f32),
+            (1, everything, queries.shape, f32),
+            (2, everything, combine.shape, f32),
+            (3, everything, expand.shape, f32),
+            (4, everything, compress_sum.shape, f32),
+            (5, everything, input_grad.shape, f32),
+            (6, everything, layer_output.shape, bf16),
+            (7, slice(0, expert_total), (expert_total, col_width), f32),
+            (7, slice(expert_total, expert_total + 1), (1, col_width), f32),
+            (7, slice(expert_total + 1, expert_total + 2), (1, col_width), f32),
+            (7, (slice(expert_total + 2, expert_total + 3), slice(0, RANK)), (1, RANK), f32),
+        ),
     )
     return (
         layer_output,
         input_grad,
-        small[expert_total + 1],
-        queries_sum,
-        compress_sum.T,
-        small[expert_total + 2, :RANK],
-        expand_sum,
-        combine_sum,
-        small[expert_total],
-        small[:expert_total].T,
-        shared_sum[1:].astype(f32).transpose(0, 2, 1),
-        shared_sum[0].astype(f32),
+        scaling_grad.reshape(col_width),
+        queries_grad,
+        compress_grad.T,
+        rescale_grad.reshape(RANK),
+        expand_grad,
+        combine_grad,
+        premix_grad.reshape(col_width),
+        router_grad.T,
+        widening_grad.transpose(0, 2, 1),
+        narrowing_grad,
         fanout_grad.transpose(0, 2, 1)[None],
         funnel_grad,
     )

time: 340 us -> 323 us (0.950)
  local copies, waits for them, and re-layouts: 16.1 us -> 3.61 us
  other arithmetic: 8.51 us -> 0 us
  Pallas kernels: 308 us -> 312 us
    pallas_call x1, Pallas kernels: 67.4 us -> 136 us  [run_attention_back(): pl.pallas_call(attend_back_kernel, name='attend_back', out_shape=(shape(t...]
    pallas_call x1, Pallas kernels: 72.9 us -> 8.8 us  [write_out(): pl.pallas_call(functools.partial(write_kernel, len(arrays), [(source, whe...]
    unnamed x30 -> x10, local copies, waits for them, and re-layouts: 11.9 us -> 3.61 us
    transpose x1 -> x0, other arithmetic: 5.21 us -> none  [local_square(): shared_sum[1:].astype(f32).transpose(0, 2, 1)]
  transfers between devices with their start and end apart: 2 -> 2, of which waited for: 2 -> 2; matrix products, arithmetic and copies ran while one was open for 0% -> 0% of each run, Pallas kernels for 5% -> 6%
where the time goes in v4:
time: 323 us; the launch traced here: 321 us
  Pallas kernels  312 us (97%)
  local copies, waits for them, and re-layouts  3.61 us (1%)
    pallas_call x1, Pallas kernels, run_attention_back(): pl.pallas_call(attend_back_kernel, name='attend_back', out_shape=(shape(t...  136 us
    pallas_call x1, Pallas kernels, run_experts(): pl.pallas_call(expert_kernel, name='experts', out_shape=(shape(tokens, wi...  85.7 us
    pallas_call x1, Pallas kernels, run_attention(): pl.pallas_call(attend_kernel, name='attend', out_shape=(*kept, shape(toke...  64.2 us
    pallas_call x2, Pallas kernels, slot_products(): pl.pallas_call(product_kernel, name='slot_products', grid=(kinds, halves)...  18 us
    pallas_call x1, Pallas kernels, write_out(): pl.pallas_call(functools.partial(write_kernel, len(arrays), [(source, whe...  8.8 us
  transfers between devices with their start and end apart: 2, of which 2 were waited for; matrix products, arithmetic and copies ran while one was open for 0% of the time, Pallas kernels for 6%

profile of v4, /device:TPU:9, one launch (start us, length us, event | category | flops | bytes accessed | tf_op | source)
XLA Modules:
  0.0 321.5 jit_solution(9880508179515794294)
XLA Ops:
  0.6 64.2 %attend.1 = (bf16[4,128,1024]{2,1,0:T(8,128)(2,1)}, bf16[4,128,384]{2,1,0:T(8,128)(2,1)}, bf16[2,4,128,256]{3,2,1,0:T(8,128)(2,1)}, bf16[2,4,128,128]{3,2,1,0:T(...) custom-call(bf16[128,1024]{1,0:T(8,128)(2,1)} %act_ref.3, ...), custom_call_target="tpu_custom_call" | custom-call | flops 42949672960 | bytes 33554432 | tf_op jit(solution)/shard_map/attend/pallas_call | solution.py:926
  64.8 85.7 %experts.1 = (f32[128,1024]{1,0:T(8,128)}, bf16[4,128,1024]{2,1,0:T(8,128)(2,1)}, bf16[2,4,256,1024]{3,2,1,0:T(8,128)(2,1)}, bf16[2,4,256,704]{3,2,1,0:T(8,128)(...) custom-call(bf16[128,1024]{1,0:T(8,128)(2,1)} %get-tuple-element.66., ...), custom_call_target="tpu_custom_call" | custom-call | flops 64424509440 | bytes 67108864 | tf_op jit(solution)/shard_map/experts/pallas_call | solution.py:2206
  150.5 1.3 collective-permute-start
  151.9 0.3 collective-permute-start.1
  152.2 0.0 copy-start
  152.2 2.2 copy-done
  154.4 0.0 copy-start.1
  154.4 1.4 copy-done.1
  155.8 0.0 copy-start.2
  155.8 0.0 copy-start.3
  155.8 6.5 %slot_products.3 = f32[1,704,2048]{2,1,0:T(8,128)} custom-call(bf16[1,1024,704]{2,1,0:T(8,128)(2,1)S(1)} %bitcast.29, bf16[2,1024,1024]{2,1,0:T(8,128)(2,1)S(1)} %bitcast.28), custom_call_target="tpu_custom_call" | custom-call | flops 2952790016 | bytes 5767168 | tf_op jit(solution)/shard_map/slot_products/pallas_call | solution.py:2412
  162.3 0.0 copy-done.2
  162.3 0.0 copy-done.3
  162.3 11.5 %slot_products.2 = f32[2,704,2048]{2,1,0:T(8,128)} custom-call(bf16[2,1024,704]{2,1,0:T(8,128)(2,1)S(1)} %bitcast.31, bf16[2,1024,1024]{2,1,0:T(8,128)(2,1)S(1)} %bitcast.30), custom_call_target="tpu_custom_call" | custom-call | flops 5905580032 | bytes 11534336 | tf_op jit(solution)/shard_map/slot_products/pallas_call | solution.py:2412
  173.8 1.9 collective-permute-done.got_x_far
  175.7 0.0 copy-start.4
  175.7 1.0 collective-permute-done.1.got_y_far
  176.7 0.0 copy-done.4
  176.7 135.7 %attend_back.1 = (f32[128,1024]{1,0:T(8,128)}, bf16[128,1024]{1,0:T(8,128)(2,1)}, f32[24,1024]{1,0:T(8,128)}, bf16[3,704,1024]{2,1,0:T(8,128)(2,1)}, bf16[4,8,32...) custom-call(f32[128,1024]{1,0:T(8,128)} %get-tuple-element.76.normed, ...), custom_call_target="tpu_custom_call" | custom-call | flops 42949672960 | bytes 33554432 | tf_op jit(solution)/shard_map/attend_back/pallas_call | solution.py:1664
  312.5 8.8 %write_out.1 = (f32[2,704,1024]{2,1,0:T(8,128)}, f32[704,1024]{1,0:T(8,128)}, f32[1024,768]{1,0:T(8,128)}, f32[512,1024]{1,0:T(8,128)}, f32[512,1024]{1,0:T(8,12...) custom-call(bf16[3,704,1024]{2,1,0:T(8,128)(2,1)} %get-tuple-element, ...), custom_call_target="tpu_custom_call" | custom-call | bytes 25165824 | tf_op jit(solution)/shard_map/write_out/pallas_call | solution.py:2375
Async XLA Ops:
  150.5 25.2 %collective-permute-start = (bf16[3,704,256]{2,1,0:T(8,128)(2,1)}, bf16[3,704,256]{2,1,0:T(8,128)(2,1)S(1)}, u32[]{:S(2)}, u32[]{:S(2)}) collective-permute-start(bf16[3,704,256]{2,1,0:T(8,128)(2,1)} %get-tuple-element.88), channel_id=1, source_target_pairs={{0,8},{8,0},{16,24},{24,16},{1,9},{9,1},{17,25},{25,17},{2,10},{10... | collective-permute-start | bytes 3244040 | tf_op jit(solution)/shard_map/ppermute | solution.py:2524
  151.9 24.8 %collective-permute-start.1 = (bf16[3,704,256]{2,1,0:T(8,128)(2,1)}, bf16[3,704,256]{2,1,0:T(8,128)(2,1)}, u32[]{:S(2)}, u32[]{:S(2)}) collective-permute-start(bf16[3,704,256]{2,1,0:T(8,128)(2,1)} %get-tuple-element.89), channel_id=1, source_target_pairs={{0,16},{8,24},{16,0},{24,8},{1,17},{9,25},{17,1},{25,9},{2,18},{10... | collective-permute-start | bytes 3244040 | tf_op jit(solution)/shard_map/ppermute | solution.py:2525
  152.2 2.2 copy-start
  154.4 1.4 copy-start.1
  155.8 6.5 %copy-start.2 = (bf16[2,4,256,1024]{3,2,1,0:T(8,128)(2,1)S(1)}, bf16[2,4,256,1024]{3,2,1,0:T(8,128)(2,1)}, u32[]{:S(2)}) copy-start(bf16[2,4,256,1024]{3,2,1,0:T(8,128)(2,1)} %get-tuple-element.74) | copy-start | bytes 12582916
  155.8 6.5 %copy-start.3 = (bf16[2,4,256,704]{3,2,1,0:T(8,128)(2,1)S(1)}, bf16[2,4,256,704]{3,2,1,0:T(8,128)(2,1)}, u32[]{:S(2)}) copy-start(bf16[2,4,256,704]{3,2,1,0:T(8,128)(2,1)} %get-tuple-element.73) | copy-start | bytes 8650756
  175.7 1.0 copy-start.4

commit v5 on v4

--- a/solution.py
+++ b/solution.py
@@ -225,25 +225,27 @@
 
 
 class SquareRest:
-    def __init__(self, place, kept, got, middle, second, result, sent, arrived):
-        self.x, self.y = lax.rem(place, 2), lax.div(place, 2)
+    def __init__(self, place, which, kept, got, middle, second, result, sent, arrived):
+        self.x, self.y, self.which = lax.rem(place, 2), lax.div(place, 2), which
         self.to_x, self.to_y = {"dp": partner(place, 1)}, {"dp": partner(place, 2)}
         self.kept, self.got = kept, got
         self.middle, self.second, self.result = middle, second, result
-        self.sent, self.arrived = sent, arrived
+        self.sent, self.arrived = sent.at[which], arrived.at[which]
 
     def copies(self, phase):
-        x, y = self.x, self.y
+        x, y, which = self.x, self.y, self.which
         if phase == 1:
             plan = (
-                (self.middle.at[0], self.second.at[0], self.to_y),
-                (self.middle.at[1], self.second.at[1], self.to_x),
+                (self.middle.at[0, which], self.second.at[0, which], self.to_y),
+                (self.middle.at[1, which], self.second.at[1, which], self.to_x),
             )
         elif phase == 2:
-            one, two = self.result.at[2 * x + y], self.result.at[4 + 2 * y + x]
+            one = self.result.at[2 * x + y, which]
+            two = self.result.at[4 + 2 * y + x, which]
             plan = ((one, one, self.to_y), (two, two, self.to_x))
         else:
-            one, two = self.result.at[pl.ds(2 * x, 2)], self.result.at[pl.ds(4 + 2 * y, 2)]
+            one = self.result.at[pl.ds(2 * x, 2), which]
+            two = self.result.at[pl.ds(4 + 2 * y, 2), which]
             plan = ((one, one, self.to_x), (two, two, self.to_y))
         return [
             remote(source, target, self.sent.at[2 * phase + i], self.arrived.at[2 * phase + i], to)
@@ -253,20 +255,24 @@
     def sum_of(self, half, side):
         wide = self.middle.shape[3]
         lanes = pl.ds(pl.multiple_of(side * wide, 128), wide)
-        return self.kept[half, :, :, lanes].astype(f32) + self.got[half, :, :, lanes].astype(f32)
+        which = self.which
+        kept, got = self.kept[half, which, :, lanes], self.got[half, which, :, lanes]
+        return kept.astype(f32) + got.astype(f32)
 
     def run(self, phase):
-        x, y = self.x, self.y
+        x, y, which = self.x, self.y, self.which
         if phase > 1:
             for copy in self.copies(phase - 1):
                 copy.wait_recv()
         if phase == 1:
-            self.middle[0] = self.sum_of(0, 1 - y).astype(bf16)
-            self.middle[1] = self.sum_of(1, 1 - x).astype(bf16)
+            self.middle[0, which] = self.sum_of(0, 1 - y).astype(bf16)
+            self.middle[1, which] = self.sum_of(1, 1 - x).astype(bf16)
         if phase == 2:
-            self.result[2 * x + y] = (self.sum_of(0, y) + self.second[0].astype(f32)).astype(bf16)
-            self.result[4 + 2 * y + x] = (
-                self.sum_of(1, x) + self.second[1].astype(f32)
+            self.result[2 * x + y, which] = (
+                self.sum_of(0, y) + self.second[0, which].astype(f32)
+            ).astype(bf16)
+            self.result[4 + 2 * y + x, which] = (
+                self.sum_of(1, x) + self.second[1, which].astype(f32)
             ).astype(bf16)
         if phase < 4:
             for copy in self.copies(phase):
@@ -326,12 +332,13 @@
                 self.copy(block, index, way).wait_recv()
                 piece = self.piece(index)
                 self.leaving[block, piece] = (
-                    self.part[block, piece] + self.coming[way, block, piece].astype(f32)
+                    self.part[block, piece].astype(f32)
+                    + self.coming[way, block, piece].astype(f32)
                 ).astype(bf16)
                 self.send(block, index)
 
     def total(self, target):
-        target[...] = self.part[self.row]
+        target[...] = self.part[self.row].astype(f32)
         for way, there in ((0, self.row > 0), (1, self.row < ROWS - 1)):
 
             @pl.when(there)
@@ -428,6 +435,8 @@
     routes,
     staged,
     marks,
+    raw,
+    scales,
     load_sem,
     store_sem,
     rows_sem,
@@ -457,6 +466,8 @@
     pair_arrived,
     router_sent,
     router_arrived,
+    scale_sent,
+    scale_arrived,
 ):
     place, row, col = lax.axis_index("dp"), lax.axis_index("row"), lax.axis_index("col")
     other = 1 - col
@@ -552,7 +563,8 @@
             {"dp": partner(place, step)},
         )
 
-    line = Line(row, one_ref, line_sent, line_arrived)
+    line = Line(row, raw, line_sent, line_arrived)
+    scale_line = Line(row, scales, scale_sent, scale_arrived)
     cot_line = Line(row, cot_all, cot_sent, cot_arrived)
     route_line = Line(row, routes, route_sent, route_arrived)
     sums = SumLine(row, part, leaving, coming, sum_sent, sum_arrived)
@@ -563,22 +575,22 @@
         (compress_all.shape[0] - ROWS * sliced, width), bf16
     )
     comp_each(row, lambda copy: copy.start())
+    raw[pl.ds(row, 1)] = act_ref[...].reshape(1, tokens, width)
+    line.pass_on(row)
 
     def router_copy(half):
         here = router_all.at[:, pl.ds(pl.multiple_of(half * width, width), width)]
         return remote(here, here, router_sent.at[0], router_arrived.at[0], sibling)
 
-    router_all[:, pl.ds(pl.multiple_of(col * width, width), width)] = router_ref[...]
     inputs = act_ref[...].astype(f32)
     scale_one = scale_of(inputs, 0)
     scale_one_ref[...] = scale_one
-    one_ref[pl.ds(row, 1)] = (
-        (inputs * scale_one * scaling_ref[...]).astype(bf16).reshape(1, tokens, width)
-    )
+    scales[pl.ds(row, 1)] = jnp.broadcast_to(scale_one, (tokens, 128)).T[0:8].reshape(1, 8, tokens)
+    scale_line.pass_on(row)
+    router_all[:, pl.ds(pl.multiple_of(col * width, width), width)] = router_ref[...]
+    router_copy(col).start()
     cot_all[pl.ds(row, 1)] = cot_ref[...].reshape(1, tokens, width)
     routes[pl.ds(row, 1)] = route_ref[...].reshape((1,) + route_ref.shape)
-    line.pass_on(row)
-    router_copy(col).start()
 
     @pl.when(jnp.logical_not(inner))
     def _():
@@ -612,27 +624,117 @@
         here = attended_ref.at[block, :, pl.ds(pl.multiple_of(half * 2 * HEADV, 128), 2 * HEADV)]
         return remote(here, here, att_sent.at[block], att_arrived.at[block], sibling)
 
-    def gather(step, carried):
+    def comp_relay(step):
         block = block_at(row, step)
-
-        @pl.when(step > 0)
-        def _():
-            comp_copy(block, 0).wait_recv()
-            comp_each(block, lambda copy: copy.start())
-            for shift in (3, 2, 1):
-                comp_out(block, shift, place).start()
-            line.wait(block)
-            line.pass_on(block)
-
-        tokens_here = one_ref[block]
+        comp_copy(block, 0).wait_recv()
+        comp_each(block, lambda copy: copy.start())
+        for shift in (3, 2, 1):
+            comp_out(block, shift, place).start()
+
+    def relay_one(step):
+        block = block_at(row, step)
+        line.wait(block)
+        line.pass_on(block)
+        scale_line.wait(block)
+        scale_line.pass_on(block)
+
+    def normalise(step):
+        block = block_at(row, step)
+        scale = scales[block].T[:, 0:1]
+        normed = (raw[block].astype(f32) * scale * scaling_ref[...]).astype(bf16)
+        one_ref[block] = normed
         query_to[block] = nn(
-            tokens_here, queries[:, pl.ds(pl.multiple_of(other * mine, 128), mine)]
+            normed, queries[:, pl.ds(pl.multiple_of(other * mine, 128), mine)]
         ).astype(bf16)
         query_copy(block).start()
-        query_own[block] = nn(tokens_here, queries[:, pl.ds(pl.multiple_of(col * mine, 128), mine)])
+        query_own[block] = nn(normed, queries[:, pl.ds(pl.multiple_of(col * mine, 128), mine)])
+
+    def latents(step):
+        block = block_at(row, step)
+        value = nt(one_ref[block], compress_all[...])
+        latent_to[block] = value
+        latent_copy(block).start()
+        latent_ref[block] = value
+
+    def keys(step):
+        block = block_at(row, step)
+        latent_copy(block).wait_recv()
+        latent = latent_ref[block] + latent_from[block]
+        latent_ref[block] = latent
+        plain = latent[:, :RANK]
+        scale = lax.rsqrt(jnp.mean(plain * plain, axis=1, keepdims=True) + epsilon)
+        normed = (plain * scale * rescale_ref[...]).astype(bf16)
+        normed_latent_ref[block] = normed
+        own = 2 * (NOPE + HEADV)
+        expanded = nn(normed, expand[:, pl.ds(pl.multiple_of(col * own, 128), own)])
+        rope = latent[:, RANK:]
+        rope = rope * key_cos_ref[block] + swap_halves(rope) * key_sin_ref[block]
+        first = jnp.concatenate([expanded[:, :NOPE], rope], axis=1)
+        second = jnp.concatenate([expanded[:, 2 * NOPE : 3 * NOPE], rope], axis=1)
+        key_ref[0, block] = first.astype(bf16)
+        key_ref[1, block] = pltpu.roll(second, ROPE, 1).astype(bf16)
+        value_ref[0, block] = expanded[:, NOPE : 2 * NOPE].astype(bf16)
+        value_ref[1, block] = expanded[:, 3 * NOPE :].astype(bf16)
+        query_copy(block).wait_recv()
+        query = query_own[block] + query_from[block].astype(f32)
+        query_ref[block] = (
+            query * cos_ref[block] + swap_halves(query) * sin_ref[block]
+        ).astype(bf16)
+
+    def gather(step, carried):
+        @pl.when(step > 0)
+        def _():
+            relay_one(step)
+
+        normalise(step)
+
+        @pl.when(step < 2)
+        def _():
+            comp_relay(step + 1)
+
+        @pl.when(step == 1)
+        def _():
+            comp_relay(3)
+
         return carried
 
-    lax.fori_loop(0, ROWS, gather, 0)
+    lax.fori_loop(0, ROWS - 1, gather, 0)
+
+    @pl.when(inner)
+    def _():
+        relay_one(ROWS - 1)
+
+    def comp_arrive(block, carried):
+        @pl.when(block != row)
+        def _():
+            for shift in range(1, SQUARE):
+                comp_out(block, shift, partner(place, shift)).wait_recv()
+
+        return carried
+
+    lax.fori_loop(0, ROWS, comp_arrive, 0)
+    loads[1].wait()
+
+    def middle(step, carried):
+        @pl.when(jnp.logical_and(step == ROWS - 1, jnp.logical_not(inner)))
+        def _():
+            relay_one(step)
+
+        @pl.when(step == ROWS - 1)
+        def _():
+            normalise(step)
+
+        @pl.when(step < ROWS)
+        def _():
+            latents(step)
+
+        @pl.when(step > 0)
+        def _():
+            keys(step - 1)
+
+        return carried
+
+    lax.fori_loop(0, ROWS - 1, middle, 0)
 
     @pl.when(inner)
     def _():
@@ -696,59 +798,14 @@
             out_copy(block, shift).wait_recv()
         pair_copy(block, col).start()
 
-    def comp_arrive(block, carried):
-        @pl.when(block != row)
-        def _():
-            for shift in range(1, SQUARE):
-                comp_out(block, shift, partner(place, shift)).wait_recv()
-
-        return carried
-
-    lax.fori_loop(0, ROWS, comp_arrive, 0)
-
-    def latents(block, carried):
-        value = nt(one_ref[block], compress_all[...])
-        latent_to[block] = value
-        latent_copy(block).start()
-        latent_ref[block] = value
-        return carried
-
-    lax.fori_loop(0, ROWS, latents, 0)
     take(0)
+    lax.fori_loop(ROWS - 1, ROWS + 1, middle, 0)
 
     @pl.when(inner)
     def _():
         relay(1)
         relay(2)
 
-    loads[1].wait()
-
-    def keys(block, carried):
-        latent_copy(block).wait_recv()
-        latent = latent_ref[block] + latent_from[block]
-        latent_ref[block] = latent
-        plain = latent[:, :RANK]
-        scale = lax.rsqrt(jnp.mean(plain * plain, axis=1, keepdims=True) + epsilon)
-        normed = (plain * scale * rescale_ref[...]).astype(bf16)
-        normed_latent_ref[block] = normed
-        own = 2 * (NOPE + HEADV)
-        expanded = nn(normed, expand[:, pl.ds(pl.multiple_of(col * own, 128), own)])
-        rope = latent[:, RANK:]
-        rope = rope * key_cos_ref[block] + swap_halves(rope) * key_sin_ref[block]
-        first = jnp.concatenate([expanded[:, :NOPE], rope], axis=1)
-        second = jnp.concatenate([expanded[:, 2 * NOPE : 3 * NOPE], rope], axis=1)
-        key_ref[0, block] = first.astype(bf16)
-        key_ref[1, block] = pltpu.roll(second, ROPE, 1).astype(bf16)
-        value_ref[0, block] = expanded[:, NOPE : 2 * NOPE].astype(bf16)
-        value_ref[1, block] = expanded[:, 3 * NOPE :].astype(bf16)
-        query_copy(block).wait_recv()
-        query = query_own[block] + query_from[block].astype(f32)
-        query_ref[block] = (
-            query * cos_ref[block] + swap_halves(query) * sin_ref[block]
-        ).astype(bf16)
-        return carried
-
-    lax.fori_loop(0, ROWS, keys, 0)
     for index in range(7):
         stores[index].start()
     seq = ROWS * tokens
@@ -838,6 +895,7 @@
     stat_copy(1).wait_send()
     sums.finish()
     line.finish()
+    scale_line.finish()
     cot_line.finish()
     route_line.finish()
 
@@ -954,6 +1012,8 @@
             VMEM((ROWS,) + routes.shape, jnp.int32),
             VMEM((ROWS, picked, width), bf16),
             VMEM((ROWS, tokens, 8), f32),
+            VMEM((ROWS, tokens, width), bf16),
+            VMEM((ROWS, 8, tokens), f32),
             DMA((3,)),
             DMA((12,)),
             DMA((ROWS,)),
@@ -972,6 +1032,7 @@
             *pair_sems(),
             DMA((1,)),
             DMA((1,)),
+            *line_sems(),
         ],
         compiler_params=pltpu.CompilerParams(
             collective_id=1, has_side_effects=True, vmem_limit_bytes=56 * MIB
@@ -1108,6 +1169,8 @@
     rest_sent,
     rest_arrived,
     rest_sem,
+    reply_part,
+    reply_leaving,
     reply_coming,
     small_to,
     small_from,
@@ -1138,6 +1201,9 @@
         pltpu.make_async_copy(source, target, load_sem.at[i])
         for i, (source, target) in enumerate(
             [
+                (kept_far, kept),
+                (got_x_far, got.at[0]),
+                (got_y_far, got.at[1]),
                 (combine_far, combine),
                 (query_far, query_ref),
                 (key_far, key_ref),
@@ -1152,9 +1218,6 @@
                 (key_sin_far, key_sin_ref),
                 (compress_far, compress_all),
                 (one_far, one_ref),
-                (kept_far, kept),
-                (got_x_far, got.at[0]),
-                (got_y_far, got.at[1]),
                 (attended_far, attended),
                 (normed_latent_far, normed_latent),
                 (narrow_far, narrow),
@@ -1181,15 +1244,26 @@
             sibling,
         )
 
-    def norm_grad(values, scale, gain, upstream, index):
+    def norm_begin(values, gain, upstream, index):
         weighted = upstream * gain
         own = jnp.sum(weighted * values, axis=1, keepdims=True)
         stat_to[index] = jnp.broadcast_to(own, (tokens, 128))
         stat_copy(index).start()
+
+    def norm_grad(values, scale, gain, upstream, index):
         stat_copy(index).wait_recv()
-        inner = (own + stat_from[index][:, 0:1]) / D
-        return weighted * scale - values * (scale * scale * scale * inner)
-
+        inner = (stat_to[index][:, 0:1] + stat_from[index][:, 0:1]) / D
+        return upstream * gain * scale - values * (scale * scale * scale * inner)
+
+    norm_begin(residual_ref[...], premix_ref[...], normed_grad_ref[...], 0)
+    for load in loads[0:3]:
+        load.wait()
+    rests = [
+        SquareRest(place, which, kept, got, middle, second, result, rest_sent, rest_arrived)
+        for which in range(kept.shape[1])
+    ]
+    for rest in rests:
+        rest.run(1)
     residual_grad = cot_ref[...].astype(f32) + norm_grad(
         residual_ref[...], scale_two_ref[...], premix_ref[...], normed_grad_ref[...], 0
     )
@@ -1201,10 +1275,8 @@
     scaling_rows[...] = jnp.zeros_like(scaling_rows)
     rescale_rows[...] = jnp.zeros_like(rescale_rows)
 
-    rest = SquareRest(place, kept, got, middle, second, result, rest_sent, rest_arrived)
-
     line_sums = SumLine(
-        row, part, leaving, reply_coming, reply_sent, reply_arrived
+        row, reply_part, reply_leaving, reply_coming, reply_sent, reply_arrived
     )
     experts = router_rows.shape[0]
     kinds = [sums_scratch[7 * i : 7 * i + 7] for i in range(4)]
@@ -1279,7 +1351,9 @@
 
     def reply_add(turn, carried):
         block = block_at(row, ROWS - 1 - turn)
-        part[block] = nn(back_ref[block], home[block]) + nn(shared_ref[block], narrow[...])
+        reply_part[block] = (
+            nn(back_ref[block], home[block]) + nn(shared_ref[block], narrow[...])
+        ).astype(bf16)
         line_sums.begin(block)
         return carried
 
@@ -1390,10 +1464,7 @@
 
         @pl.when(step == 0)
         def _():
-            for load in loads[14:17]:
-                load.wait()
-            rest.run(1)
-            loads[0].wait()
+            loads[3].wait()
 
         grads = branch_ref[block]
         grad_to[block] = nt(
@@ -1407,7 +1478,7 @@
 
         @pl.when(step == 0)
         def _():
-            for load in loads[1:7]:
+            for load in loads[4:10]:
                 load.wait()
 
         grad_copy(block).wait_recv()
@@ -1437,7 +1508,7 @@
 
         @pl.when(step == 0)
         def _():
-            loads[7].wait()
+            loads[10].wait()
 
         query_copy(block, other).wait_recv()
         part[block] = nt(query_grad_ref[block], queries[...])
@@ -1449,17 +1520,29 @@
             def _(delay=delay, stage=stage):
                 stage(step - delay)
 
+        @pl.when(step == 1)
+        def _():
+            rests[0].run(2)
+            rests[1].run(2)
+
         @pl.when(step == 2)
         def _():
-            rest.run(2)
+            rests[2].run(2)
+            rests[0].run(3)
+
+        @pl.when(step == 3)
+        def _():
+            rests[1].run(3)
+            rests[2].run(3)
 
         return carried
 
     lax.fori_loop(0, ROWS + 1, turn, 0)
-    for load in loads[8:14]:
+    for load in loads[11:17]:
         load.wait()
     begin(0)
     begin(1)
+    reply_begin()
 
     def latents(turn, carried):
         block = block_at(row, ROWS - 1 - turn)
@@ -1492,7 +1575,6 @@
 
     lax.fori_loop(0, ROWS, latents, 0)
     project(ROWS - 1)
-    rest.run(3)
 
     def turned_piece(member):
         return turned.at[
@@ -1549,14 +1631,15 @@
     own_copy(col).start()
     advance(5)
     sums.total(total)
+    norm_begin(act_ref[...].astype(f32), scaling_ref[...], total[...], 1)
     input_grad_ref[...] += norm_grad(
         act_ref[...].astype(f32), scale_one_ref[...], scaling_ref[...], total[...], 1
     )
-    sums.finish()
-    reply_begin()
     small_begin()
     advance(6)
-    rest.run(4)
+    reply_pass()
+    for rest in rests:
+        rest.run(4)
     pieces = [
         pltpu.make_async_copy(
             result.at[i], shared_sum.at[:, :, i * 128 : (i + 1) * 128], rest_sem.at[i]
@@ -1570,11 +1653,10 @@
     own_copy(col).wait_send()
     advance(7)
     advance(8)
-    reply_pass()
     small_square_begin()
+    reply_end()
     for turn in range(9, count + 5):
         advance(turn)
-    reply_end()
     small_end()
     pair_copy().wait_recv()
     store(expand_other, expand_lanes(other))
@@ -1600,7 +1682,9 @@
     for one_sum in pieces_of:
         one_sum.finish()
     line_sums.finish()
-    rest.finish()
+    for rest in rests:
+        rest.finish()
+    sums.finish()
     line.finish()
 
 
@@ -1716,9 +1800,11 @@
             *pair_sems(),
             *pair_sems(),
             *sum_sems(),
+            DMA((kept.shape[1], 8)),
+            DMA((kept.shape[1], 8)),
             DMA((8,)),
-            DMA((8,)),
-            DMA((8,)),
+            VMEM((ROWS, tokens, width), bf16),
+            VMEM((ROWS, tokens, width), bf16),
             VMEM((2, ROWS, tokens, width), bf16),
             VMEM(small, f32),
             VMEM(small, f32),
@@ -1945,6 +2031,9 @@
             out_copy(block, shift).start()
         rows[col, block, 0:slots] = staged[block, 0:slots]
 
+    def shared_begin(step):
+        block = block_at(row, step)
+
         @pl.when(step == 0)
         def _():
             loads[0].wait()
@@ -2032,6 +2121,9 @@
         router_rows[:, width:] += tn(logit_grad, right)
         for copy in stores(step):
             copy.start()
+
+    def send_home(step):
+        block = block_at(row, step)
         for shift in range(1, SQUARE):
             out_copy(block, shift).wait_send()
         half_copy(step).wait_recv()
@@ -2079,38 +2171,51 @@
         reply_ref[block, 0:slots] = staged[block, 0:slots]
 
     def turn(step, carried):
+        @pl.when(jnp.logical_and(step == 2, inner))
+        def _():
+            relay(3)
+
         @pl.when(step < ROWS)
         def _():
             take(step)
+
+        @pl.when(jnp.logical_and(step >= 1, step <= ROWS))
+        def _():
+            forward(step - 1)
+
+        @pl.when(step < ROWS)
+        def _():
+            shared_begin(step)
 
         @pl.when(jnp.logical_and(step == 0, inner))
         def _():
             relay(1)
             relay(2)
 
-        @pl.when(jnp.logical_and(step >= 1, step < ROWS))
-        def _():
-            forward(step - 1)
-
-        @pl.when(jnp.logical_and(step >= 2, step < ROWS + 2))
-        def _():
-            experts_of(step - 2)
+        @pl.when(step >= 2)
+        def _():
+            shared(step - 2)
+            send_home(step - 2)
 
         @pl.when(step == ROWS)
         def _():
-            forward(ROWS - 1)
-
-        @pl.when(jnp.logical_or(step == 1, step >= 3))
-        def _():
-            shared(jnp.where(step == 1, 0, step - 2))
-
-        @pl.when(jnp.logical_and(step == 1, inner))
-        def _():
-            relay(3)
-
-        @pl.when(step >= 3)
-        def _():
-            add_up(step - 3)
+            reply(0)
+
+        @pl.when(step == ROWS + 1)
+        def _():
+            reply_home(0)
+
+        @pl.when(step >= ROWS)
+        def _():
+            add_up(2 * step - 2 * ROWS)
+
+        @pl.when(step == ROWS)
+        def _():
+            add_up(1)
+
+        @pl.when(jnp.logical_and(step >= 1, step <= ROWS))
+        def _():
+            experts_of(step - 1)
 
         return carried
 
@@ -2121,13 +2226,13 @@
         def _():
             reply(step)
 
-        @pl.when(step > 0)
+        @pl.when(step > 1)
         def _():
             reply_home(step - 1)
 
         return carried
 
-    lax.fori_loop(0, ROWS + 1, replies, 0)
+    lax.fori_loop(1, ROWS + 1, replies, 0)
     add_up(ROWS - 1)
 
     def hand_on(turn, carried):

time: 323 us -> 311 us (0.963)
  Pallas kernels: 312 us -> 302 us
    pallas_call x1, Pallas kernels: 136 us -> 126 us  [run_attention_back(): pl.pallas_call(attend_back_kernel, name='attend_back', out_shape=(shape(t...]
where the time goes in v5:
time: 311 us; the launch traced here: 310 us
  Pallas kernels  302 us (97%)
  local copies, waits for them, and re-layouts  4.38 us (1%)
    pallas_call x1, Pallas kernels, run_attention_back(): pl.pallas_call(attend_back_kernel, name='attend_back', out_shape=(shape(t...  126 us
    pallas_call x1, Pallas kernels, run_experts(): pl.pallas_call(expert_kernel, name='experts', out_shape=(shape(tokens, wi...  83.4 us
    pallas_call x1, Pallas kernels, run_attention(): pl.pallas_call(attend_kernel, name='attend', out_shape=(*kept, shape(toke...  65.9 us
    pallas_call x2, Pallas kernels, slot_products(): pl.pallas_call(product_kernel, name='slot_products', grid=(kinds, halves)...  18 us
    pallas_call x1, Pallas kernels, write_out(): pl.pallas_call(functools.partial(write_kernel, len(arrays), [(source, whe...  8.8 us
  transfers between devices with their start and end apart: 2, of which 2 were waited for; matrix products, arithmetic and copies ran while one was open for 0% of the time, Pallas kernels for 6%

profile of v5, /device:TPU:9, one launch (start us, length us, event | category | flops | bytes accessed | tf_op | source)
XLA Modules:
  0.0 310.3 jit_solution(6810945379993461843)
XLA Ops:
  0.6 65.9 %attend.1 = (bf16[4,128,1024]{2,1,0:T(8,128)(2,1)}, bf16[4,128,384]{2,1,0:T(8,128)(2,1)}, bf16[2,4,128,256]{3,2,1,0:T(8,128)(2,1)}, bf16[2,4,128,128]{3,2,1,0:T(...) custom-call(bf16[128,1024]{1,0:T(8,128)(2,1)} %act_ref.3, ...), custom_call_target="tpu_custom_call" | custom-call | flops 42949672960 | bytes 33554432 | tf_op jit(solution)/shard_map/attend/pallas_call | solution.py:984
  66.5 83.4 %experts.1 = (f32[128,1024]{1,0:T(8,128)}, bf16[4,128,1024]{2,1,0:T(8,128)(2,1)}, bf16[2,4,256,1024]{3,2,1,0:T(8,128)(2,1)}, bf16[2,4,256,704]{3,2,1,0:T(8,128)(...) custom-call(bf16[128,1024]{1,0:T(8,128)(2,1)} %get-tuple-element.66., ...), custom_call_target="tpu_custom_call" | custom-call | flops 64424509440 | bytes 67108864 | tf_op jit(solution)/shard_map/experts/pallas_call | solution.py:2311
  149.9 0.2 collective-permute-start
  150.0 1.7 collective-permute-start.1
  151.7 0.0 copy-start
  151.7 2.2 copy-done
  153.9 0.0 copy-start.1
  153.9 1.4 copy-done.1
  155.3 0.0 copy-start.2
  155.3 0.0 copy-start.3
  155.3 6.5 %slot_products.3 = f32[1,704,2048]{2,1,0:T(8,128)} custom-call(bf16[1,1024,704]{2,1,0:T(8,128)(2,1)S(1)} %bitcast.29, bf16[2,1024,1024]{2,1,0:T(8,128)(2,1)S(1)} %bitcast.28), custom_call_target="tpu_custom_call" | custom-call | flops 2952790016 | bytes 5767168 | tf_op jit(solution)/shard_map/slot_products/pallas_call | solution.py:2517
  161.8 0.0 copy-done.2
  161.8 0.0 copy-done.3
  161.9 11.5 %slot_products.2 = f32[2,704,2048]{2,1,0:T(8,128)} custom-call(bf16[2,1024,704]{2,1,0:T(8,128)(2,1)S(1)} %bitcast.31, bf16[2,1024,1024]{2,1,0:T(8,128)(2,1)S(1)} %bitcast.30), custom_call_target="tpu_custom_call" | custom-call | flops 5905580032 | bytes 11534336 | tf_op jit(solution)/shard_map/slot_products/pallas_call | solution.py:2517
  173.3 1.2 collective-permute-done.got_x_far
  174.5 0.0 copy-start.4
  174.5 0.2 collective-permute-done.1.got_y_far
  174.7 0.8 copy-done.4
  175.5 125.9 %attend_back.1 = (f32[128,1024]{1,0:T(8,128)}, bf16[128,1024]{1,0:T(8,128)(2,1)}, f32[24,1024]{1,0:T(8,128)}, bf16[3,704,1024]{2,1,0:T(8,128)(2,1)}, bf16[4,8,32...) custom-call(f32[128,1024]{1,0:T(8,128)} %get-tuple-element.76.normed, ...), custom_call_target="tpu_custom_call" | custom-call | flops 42949672960 | bytes 33554432 | tf_op jit(solution)/shard_map/attend_back/pallas_call | solution.py:1748
  301.3 8.8 %write_out.1 = (f32[2,704,1024]{2,1,0:T(8,128)}, f32[704,1024]{1,0:T(8,128)}, f32[1024,768]{1,0:T(8,128)}, f32[512,1024]{1,0:T(8,128)}, f32[512,1024]{1,0:T(8,12...) custom-call(bf16[3,704,1024]{2,1,0:T(8,128)(2,1)} %get-tuple-element, ...), custom_call_target="tpu_custom_call" | custom-call | bytes 25165824 | tf_op jit(solution)/shard_map/write_out/pallas_call | solution.py:2480
Async XLA Ops:
  149.9 24.6 %collective-permute-start = (bf16[3,704,256]{2,1,0:T(8,128)(2,1)}, bf16[3,704,256]{2,1,0:T(8,128)(2,1)S(1)}, u32[]{:S(2)}, u32[]{:S(2)}) collective-permute-start(bf16[3,704,256]{2,1,0:T(8,128)(2,1)} %get-tuple-element.88), channel_id=1, source_target_pairs={{0,8},{8,0},{16,24},{24,16},{1,9},{9,1},{17,25},{25,17},{2,10},{10... | collective-permute-start | bytes 3244040 | tf_op jit(solution)/shard_map/ppermute | solution.py:2629
  150.0 24.6 %collective-permute-start.1 = (bf16[3,704,256]{2,1,0:T(8,128)(2,1)}, bf16[3,704,256]{2,1,0:T(8,128)(2,1)}, u32[]{:S(2)}, u32[]{:S(2)}) collective-permute-start(bf16[3,704,256]{2,1,0:T(8,128)(2,1)} %get-tuple-element.89), channel_id=1, source_target_pairs={{0,16},{8,24},{16,0},{24,8},{1,17},{9,25},{17,1},{25,9},{2,18},{10... | collective-permute-start | bytes 3244040 | tf_op jit(solution)/shard_map/ppermute | solution.py:2630
  151.7 2.2 copy-start
  153.9 1.4 copy-start.1
  155.3 6.5 %copy-start.2 = (bf16[2,4,256,1024]{3,2,1,0:T(8,128)(2,1)S(1)}, bf16[2,4,256,1024]{3,2,1,0:T(8,128)(2,1)}, u32[]{:S(2)}) copy-start(bf16[2,4,256,1024]{3,2,1,0:T(8,128)(2,1)} %get-tuple-element.74) | copy-start | bytes 12582916
  155.3 6.5 %copy-start.3 = (bf16[2,4,256,704]{3,2,1,0:T(8,128)(2,1)S(1)}, bf16[2,4,256,704]{3,2,1,0:T(8,128)(2,1)}, u32[]{:S(2)}) copy-start(bf16[2,4,256,704]{3,2,1,0:T(8,128)(2,1)} %get-tuple-element.73) | copy-start | bytes 8650756
  174.5 1.0 copy-start.4

commit v6 on v5

--- a/solution.py
+++ b/solution.py
@@ -189,7 +189,11 @@
             )
         met = met + SQUARE - 1
     pl.semaphore_signal(barrier, inc=1, device_id={"col": 1 - col}, device_id_type=MESH)
-    pl.semaphore_wait(barrier, met)
+    return met
+
+
+def meet(met):
+    pl.semaphore_wait(pltpu.get_barrier_semaphore(), met)
 
 
 class Line:
@@ -259,14 +263,15 @@
         kept, got = self.kept[half, which, :, lanes], self.got[half, which, :, lanes]
         return kept.astype(f32) + got.astype(f32)
 
+    def prepare(self):
+        self.middle[0, self.which] = self.sum_of(0, 1 - self.y).astype(bf16)
+        self.middle[1, self.which] = self.sum_of(1, 1 - self.x).astype(bf16)
+
     def run(self, phase):
         x, y, which = self.x, self.y, self.which
         if phase > 1:
             for copy in self.copies(phase - 1):
                 copy.wait_recv()
-        if phase == 1:
-            self.middle[0, which] = self.sum_of(0, 1 - y).astype(bf16)
-            self.middle[1, which] = self.sum_of(1, 1 - x).astype(bf16)
         if phase == 2:
             self.result[2 * x + y, which] = (
                 self.sum_of(0, y) + self.second[0, which].astype(f32)
@@ -377,10 +382,6 @@
     compress_ref,
     rescale_ref,
     premix_ref,
-    cos_ref,
-    sin_ref,
-    key_cos_ref,
-    key_sin_ref,
     mark_ref,
     cot_ref,
     route_ref,
@@ -388,6 +389,10 @@
     queries_ref,
     expand_ref,
     combine_ref,
+    cos_far,
+    sin_far,
+    key_cos_far,
+    key_sin_far,
     one_out,
     query_out,
     key_out,
@@ -422,6 +427,10 @@
     queries,
     expand,
     combine,
+    cos_ref,
+    sin_ref,
+    key_cos_ref,
+    key_sin_ref,
     stat_to,
     stat_from,
     query_own,
@@ -482,7 +491,15 @@
     loads = [
         pltpu.make_async_copy(source, target, load_sem.at[i])
         for i, (source, target) in enumerate(
-            [(queries_ref, queries), (expand_ref, expand), (combine_ref, combine)]
+            [
+                (queries_ref, queries),
+                (expand_ref, expand),
+                (combine_ref, combine),
+                (cos_far, cos_ref),
+                (sin_far, sin_ref),
+                (key_cos_far, key_cos_ref),
+                (key_sin_far, key_sin_ref),
+            ]
         )
     ]
     for load in loads:
@@ -569,13 +586,14 @@
     route_line = Line(row, routes, route_sent, route_arrived)
     sums = SumLine(row, part, leaving, coming, sum_sent, sum_arrived)
 
-    greet(row, place, col)
+    met = greet(row, place, col)
     compress_all[pl.ds(pl.multiple_of(row * sliced, 16), sliced)] = compress_ref[...]
     compress_all[ROWS * sliced :] = jnp.zeros(
         (compress_all.shape[0] - ROWS * sliced, width), bf16
     )
+    raw[pl.ds(row, 1)] = act_ref[...].reshape(1, tokens, width)
+    meet(met)
     comp_each(row, lambda copy: copy.start())
-    raw[pl.ds(row, 1)] = act_ref[...].reshape(1, tokens, width)
     line.pass_on(row)
 
     def router_copy(half):
@@ -713,7 +731,8 @@
         return carried
 
     lax.fori_loop(0, ROWS, comp_arrive, 0)
-    loads[1].wait()
+    for load in loads[1:2] + loads[3:]:
+        load.wait()
 
     def middle(step, carried):
         @pl.when(jnp.logical_and(step == ROWS - 1, jnp.logical_not(inner)))
@@ -799,12 +818,13 @@
         pair_copy(block, col).start()
 
     take(0)
-    lax.fori_loop(ROWS - 1, ROWS + 1, middle, 0)
 
     @pl.when(inner)
     def _():
         relay(1)
         relay(2)
+
+    lax.fori_loop(ROWS - 1, ROWS + 1, middle, 0)
 
     for index in range(7):
         stores[index].start()
@@ -992,13 +1012,14 @@
             shape(tokens, 1, dtype=f32),
             shape(router.shape[1], COLS * width),
         ),
-        in_specs=[whole] * 13 + [far] * 3,
+        in_specs=[whole] * 9 + [far] * 7,
         out_specs=(far,) * 13 + (whole,) * 5,
         scratch_shapes=[
             *[VMEM(value.shape, value.dtype) for value in kept],
             VMEM(queries.shape, bf16),
             VMEM(expand.shape, bf16),
             VMEM(combine.shape, bf16),
+            *[VMEM(table.shape, f32) for table in tables],
             VMEM((2, tokens, 128), f32),
             VMEM((2, tokens, 128), f32),
             VMEM((ROWS, tokens, mine), f32),
@@ -1014,7 +1035,7 @@
             VMEM((ROWS, tokens, 8), f32),
             VMEM((ROWS, tokens, width), bf16),
             VMEM((ROWS, 8, tokens), f32),
-            DMA((3,)),
+            DMA((7,)),
             DMA((12,)),
             DMA((ROWS,)),
             DMA((2,)),
@@ -1046,7 +1067,6 @@
         compress.T,
         rescale.reshape(1, RANK),
         premix.reshape(1, width),
-        *tables,
         segments.reshape(1, seq),
         cotangent,
         routes,
@@ -1054,6 +1074,7 @@
         queries,
         expand,
         combine,
+        *tables,
     )
 
 
@@ -1233,7 +1254,7 @@
         load.start()
     line = Line(row, branch_ref, line_sent, line_arrived)
     sums = SumLine(row, part, leaving, coming, sum_sent, sum_arrived)
-    greet(row, place, col, line=True)
+    met = greet(row, place, col, line=True)
 
     def stat_copy(index):
         return remote(
@@ -1255,13 +1276,16 @@
         inner = (stat_to[index][:, 0:1] + stat_from[index][:, 0:1]) / D
         return upstream * gain * scale - values * (scale * scale * scale * inner)
 
-    norm_begin(residual_ref[...], premix_ref[...], normed_grad_ref[...], 0)
     for load in loads[0:3]:
         load.wait()
     rests = [
         SquareRest(place, which, kept, got, middle, second, result, rest_sent, rest_arrived)
         for which in range(kept.shape[1])
     ]
+    for rest in rests:
+        rest.prepare()
+    meet(met)
+    norm_begin(residual_ref[...], premix_ref[...], normed_grad_ref[...], 0)
     for rest in rests:
         rest.run(1)
     residual_grad = cot_ref[...].astype(f32) + norm_grad(
@@ -1514,26 +1538,31 @@
         part[block] = nt(query_grad_ref[block], queries[...])
 
     def turn(step, carried):
-        for delay, stage in ((0, arrive), (1, heads), (2, project)):
-
-            @pl.when(jnp.logical_and(step >= delay, step < delay + ROWS))
-            def _(delay=delay, stage=stage):
-                stage(step - delay)
+        @pl.when(step < ROWS)
+        def _():
+            arrive(step)
 
         @pl.when(step == 1)
         def _():
-            rests[0].run(2)
-            rests[1].run(2)
+            for rest in rests:
+                rest.run(2)
 
         @pl.when(step == 2)
         def _():
-            rests[2].run(2)
             rests[0].run(3)
 
         @pl.when(step == 3)
         def _():
             rests[1].run(3)
             rests[2].run(3)
+
+        @pl.when(step >= 1)
+        def _():
+            heads(step - 1)
+
+        @pl.when(step >= 2)
+        def _():
+            project(step - 2)
 
         return carried
 
@@ -1611,9 +1640,12 @@
         turned_copy(step).start()
 
     advance(1)
+    small_begin()
     for turn in range(3):
         sums.pass_on(block_at(row, 3 if turn == 0 else turn))
         advance(turn + 2)
+        if turn == 0:
+            small_line_begin()
     for step in range(1, ROWS):
         turned_copy(step).wait_recv()
     half = pl.ds(pl.multiple_of(col * (seq // COLS), 128), seq // COLS)
@@ -1635,7 +1667,6 @@
     input_grad_ref[...] += norm_grad(
         act_ref[...].astype(f32), scale_one_ref[...], scaling_ref[...], total[...], 1
     )
-    small_begin()
     advance(6)
     reply_pass()
     for rest in rests:
@@ -1648,12 +1679,11 @@
     ]
     for piece in pieces:
         piece.start()
-    small_line_begin()
     own_copy(other).wait_recv()
     own_copy(col).wait_send()
     advance(7)
+    small_square_begin()
     advance(8)
-    small_square_begin()
     reply_end()
     for turn in range(9, count + 5):
         advance(turn)
@@ -1855,26 +1885,29 @@
 def expert_kernel(
     normed_ref,
     pick_ref,
-    back_ref,
-    cot_ref,
     router_ref,
+    back_far,
+    cot_far,
     cot_rows_ref,
     fan_ref,
     fun_ref,
     wide_ref,
     narrow_ref,
     sum_ref,
-    gathered_ref,
     rows_out,
     gu_out,
     hidden_out,
     shared_x,
     shared_y,
     shared_kept,
-    shared_out,
+    shared_far,
+    reply_ref,
     premix_ref,
     router_rows,
-    reply_ref,
+    gathered_ref,
+    shared_out,
+    back_ref,
+    cot_ref,
     fan,
     fun,
     wide,
@@ -1916,6 +1949,7 @@
     reply_sent,
     reply_arrived,
     grad_sem,
+    late_sem,
 ):
     place, row, col = lax.axis_index("dp"), lax.axis_index("row"), lax.axis_index("col")
     other = 1 - col
@@ -1934,13 +1968,19 @@
                 (fan_ref, fan),
                 (cot_rows_ref, cot_rows),
                 (fun_ref, fun),
+                (cot_far, cot_ref),
+                (back_far, back_ref),
             ]
         )
     ]
     for load in loads:
         load.start()
-    greet(row, place, col)
+    met = greet(row, place, col)
     gathered_ref[pl.ds(row, 1)] = normed_ref[...].reshape(1, tokens, width)
+    staged[pl.ds(row, 1)] = (
+        nn(pick_ref[row], normed_ref[...]).astype(bf16).reshape(1, picked, width)
+    )
+    meet(met)
     line = Line(row, gathered_ref, line_sent, line_arrived)
     line.pass_on(row)
     premix_ref[...] = jnp.zeros_like(premix_ref)
@@ -1969,6 +2009,12 @@
 
     def reply_copy(block, step):
         return square_copy(staged, reply_ref, reply_sent, reply_arrived, block, step)
+
+    def keep_copy(block):
+        own = pl.ds(0, slots)
+        return pltpu.make_async_copy(
+            staged.at[block, own], reply_ref.at[block, own], reply_arrived.at[block, 0]
+        )
 
     def fwd_copy(block, half):
         here = rows.at[half, block]
@@ -2026,7 +2072,10 @@
         def _():
             relay(step)
 
-        staged[block] = nn(pick_ref[block], gathered_ref[block]).astype(bf16)
+        @pl.when(step > 0)
+        def _():
+            staged[block] = nn(pick_ref[block], gathered_ref[block]).astype(bf16)
+
         for shift in (3, 2, 1):
             out_copy(block, shift).start()
         rows[col, block, 0:slots] = staged[block, 0:slots]
@@ -2038,6 +2087,7 @@
         def _():
             loads[0].wait()
             loads[1].wait()
+            loads[5].wait()
 
         for index, value in enumerate(
             (
@@ -2075,7 +2125,7 @@
 
         @pl.when(step == 0)
         def _():
-            for load in loads[2:]:
+            for load in loads[2:5] + loads[6:]:
                 load.wait()
 
         @pl.when(step > 1)
@@ -2168,7 +2218,7 @@
         staged[block] = (own + pair_from[came].astype(f32)).astype(bf16)
         for shift in (3, 2, 1):
             reply_copy(block, shift).start()
-        reply_ref[block, 0:slots] = staged[block, 0:slots]
+        keep_copy(block).start()
 
     def turn(step, carried):
         @pl.when(jnp.logical_and(step == 2, inner))
@@ -2232,6 +2282,14 @@
 
         return carried
 
+    late = [
+        pltpu.make_async_copy(source, target, late_sem.at[i])
+        for i, (source, target) in enumerate(
+            [(shared_out, shared_far)]
+        )
+    ]
+    for copy in late:
+        copy.start()
     lax.fori_loop(1, ROWS + 1, replies, 0)
     add_up(ROWS - 1)
 
@@ -2276,6 +2334,7 @@
         for shift in range(1, SQUARE):
             reply_copy(block, shift).wait_recv()
             reply_copy(block, shift).wait_send()
+        keep_copy(block).wait()
         copies = stores(step)
         copies[0].wait()
         copies[2].wait()
@@ -2288,7 +2347,7 @@
         return carried
 
     lax.fori_loop(0, ROWS, ended, 0)
-    for copy in grad_copies:
+    for copy in grad_copies + late:
         copy.wait()
     sums.finish()
     line.finish()
@@ -2313,7 +2372,6 @@
         name="experts",
         out_shape=(
             shape(tokens, width, dtype=f32),
-            shape(ROWS, tokens, width),
             shape(COLS, ROWS, picked, width),
             shape(2, ROWS, picked, hid),
             shape(ROWS, picked, hid),
@@ -2321,13 +2379,17 @@
             shape(3, share, width // SQUARE),
             shape(2, 3, share, width // SQUARE),
             shape(ROWS, tokens, share),
+            shape(ROWS, picked, width),
             shape(8, width, dtype=f32),
             shape(experts, COLS * width, dtype=f32),
-            shape(ROWS, picked, width),
         ),
-        in_specs=[whole] * 5 + [far] * 5,
-        out_specs=(whole, whole) + (far,) * 6 + (whole,) * 4,
+        in_specs=[whole] * 3 + [far] * 7,
+        out_specs=(whole,) + (far,) * 8 + (whole,) * 2,
         scratch_shapes=[
+            VMEM((ROWS, tokens, width), bf16),
+            VMEM((ROWS, tokens, share), bf16),
+            VMEM(back.shape, bf16),
+            VMEM(cot_all.shape, bf16),
             VMEM(fan.shape, bf16),
             VMEM(fun.shape, bf16),
             VMEM(wide.shape, bf16),
@@ -2348,7 +2410,7 @@
             VMEM((2, ROWS, tokens, width), bf16),
             VMEM((2, ROWS, tokens, share), bf16),
             VMEM((3, share, width), bf16),
-            DMA((5,)),
+            DMA((7,)),
             DMA((3, ROWS)),
             *line_sems(),
             *square_sems(),
@@ -2360,6 +2422,7 @@
             *pair_sems(),
             *square_sems(),
             DMA((4,)),
+            DMA((1,)),
         ],
         compiler_params=pltpu.CompilerParams(
             collective_id=2, has_side_effects=True, vmem_limit_bytes=62 * MIB
@@ -2367,7 +2430,7 @@
         cost_estimate=pl.CostEstimate(
             flops=60 * 1024**3, bytes_accessed=64 * MIB, transcendentals=0
         ),
-    )(normed, pick, back, cot_all, router_all, cot_rows, fan, fun, wide, narrow)
+    )(normed, pick, router_all, back, cot_all, cot_rows, fan, fun, wide, narrow)
 
 
 class SquareSum:
@@ -2599,7 +2662,6 @@
     )
     (
         normed_grad,
-        two_blocks,
         expert_rows,
         expert_gu_grad,
         expert_hidden,
@@ -2607,9 +2669,9 @@
         shared_y,
         shared_kept,
         hidden_blocks,
+        reply_blocks,
         premix_rows,
         router_rows,
-        reply_blocks,
     ) = run_experts(
         normed_two,
         pick,

time: 311 us -> 307 us (0.987)
  Pallas kernels: 302 us -> 298 us
  transfers between devices with their start and end apart: 2 -> 2, of which waited for: 2 -> 1; matrix products, arithmetic and copies ran while one was open for 0% -> 0% of each run, Pallas kernels for 6% -> 6%
where the time goes in v6:
time: 307 us
  Pallas kernels  298 us (97%)
  local copies, waits for them, and re-layouts  4.58 us (1%)
    pallas_call x1, Pallas kernels, run_attention_back(): pl.pallas_call(attend_back_kernel, name='attend_back', out_shape=(shape(t...  125 us
    pallas_call x1, Pallas kernels, run_experts(): pl.pallas_call(expert_kernel, name='experts', out_shape=(shape(tokens, wi...  81.5 us
    pallas_call x1, Pallas kernels, run_attention(): pl.pallas_call(attend_kernel, name='attend', out_shape=(*kept, shape(toke...  65.2 us
    pallas_call x2, Pallas kernels, slot_products(): pl.pallas_call(product_kernel, name='slot_products', grid=(kinds, halves)...  18 us
    pallas_call x1, Pallas kernels, write_out(): pl.pallas_call(functools.partial(write_kernel, len(arrays), [(source, whe...  8.8 us
  transfers between devices with their start and end apart: 2, of which 1 were waited for; matrix products, arithmetic and copies ran while one was open for 0% of the time, Pallas kernels for 6%

profile of v6, /device:TPU:9, one launch (start us, length us, event | category | flops | bytes accessed | tf_op | source)
XLA Modules:
  0.0 306.9 jit_solution(9001235541658954540)
XLA Ops:
  0.6 65.2 %attend.1 = (bf16[4,128,1024]{2,1,0:T(8,128)(2,1)}, bf16[4,128,384]{2,1,0:T(8,128)(2,1)}, bf16[2,4,128,256]{3,2,1,0:T(8,128)(2,1)}, bf16[2,4,128,128]{3,2,1,0:T(...) custom-call(bf16[128,1024]{1,0:T(8,128)(2,1)} %act_ref.3, ...), custom_call_target="tpu_custom_call" | custom-call | flops 42949672960 | bytes 33554432 | tf_op jit(solution)/shard_map/attend/pallas_call | solution.py:1004
  65.9 81.5 %experts.1 = (f32[128,1024]{1,0:T(8,128)}, bf16[2,4,256,1024]{3,2,1,0:T(8,128)(2,1)}, bf16[2,4,256,704]{3,2,1,0:T(8,128)(2,1)}, bf16[4,256,704]{2,1,0:T(8,128)(2...) custom-call(bf16[128,1024]{1,0:T(8,128)(2,1)} %get-tuple-element.66., ...), custom_call_target="tpu_custom_call" | custom-call | flops 64424509440 | bytes 67108864 | tf_op jit(solution)/shard_map/experts/pallas_call | solution.py:2370
  147.4 0.4 collective-permute-start
  147.8 1.2 collective-permute-start.1
  149.0 0.0 copy-start
  149.0 2.2 copy-done
  151.2 0.0 copy-start.1
  151.2 1.4 copy-done.1
  152.6 0.0 copy-start.2
  152.6 0.0 copy-start.3
  152.6 6.5 %slot_products.3 = f32[1,704,2048]{2,1,0:T(8,128)} custom-call(bf16[1,1024,704]{2,1,0:T(8,128)(2,1)S(1)} %bitcast.29, bf16[2,1024,1024]{2,1,0:T(8,128)(2,1)S(1)} %bitcast.28), custom_call_target="tpu_custom_call" | custom-call | flops 2952790016 | bytes 5767168 | tf_op jit(solution)/shard_map/slot_products/pallas_call | solution.py:2580
  159.1 0.0 copy-done.2
  159.1 0.0 copy-done.3
  159.1 11.5 %slot_products.2 = f32[2,704,2048]{2,1,0:T(8,128)} custom-call(bf16[2,1024,704]{2,1,0:T(8,128)(2,1)S(1)} %bitcast.31, bf16[2,1024,1024]{2,1,0:T(8,128)(2,1)S(1)} %bitcast.30), custom_call_target="tpu_custom_call" | custom-call | flops 5905580032 | bytes 11534336 | tf_op jit(solution)/shard_map/slot_products/pallas_call | solution.py:2580
  170.6 1.6 collective-permute-done.got_x_far
  172.2 0.0 copy-start.4
  172.2 0.0 collective-permute-done.1.got_y_far
  172.2 1.0 copy-done.4
  173.1 124.8 %attend_back.1 = (f32[128,1024]{1,0:T(8,128)}, bf16[128,1024]{1,0:T(8,128)(2,1)}, f32[24,1024]{1,0:T(8,128)}, bf16[3,704,1024]{2,1,0:T(8,128)(2,1)}, bf16[4,8,32...) custom-call(f32[128,1024]{1,0:T(8,128)} %get-tuple-element.76.normed, ...), custom_call_target="tpu_custom_call" | custom-call | flops 42949672960 | bytes 33554432 | tf_op jit(solution)/shard_map/attend_back/pallas_call | solution.py:1778
  297.9 8.8 %write_out.1 = (f32[2,704,1024]{2,1,0:T(8,128)}, f32[704,1024]{1,0:T(8,128)}, f32[1024,768]{1,0:T(8,128)}, f32[512,1024]{1,0:T(8,128)}, f32[512,1024]{1,0:T(8,12...) custom-call(bf16[3,704,1024]{2,1,0:T(8,128)(2,1)} %get-tuple-element, ...), custom_call_target="tpu_custom_call" | custom-call | bytes 25165824 | tf_op jit(solution)/shard_map/write_out/pallas_call | solution.py:2543
Async XLA Ops:
  147.4 24.7 %collective-permute-start = (bf16[3,704,256]{2,1,0:T(8,128)(2,1)}, bf16[3,704,256]{2,1,0:T(8,128)(2,1)S(1)}, u32[]{:S(2)}, u32[]{:S(2)}) collective-permute-start(bf16[3,704,256]{2,1,0:T(8,128)(2,1)} %get-tuple-element.88), channel_id=1, source_target_pairs={{0,8},{8,0},{16,24},{24,16},{1,9},{9,1},{17,25},{25,17},{2,10},{10... | collective-permute-start | bytes 3244040 | tf_op jit(solution)/shard_map/ppermute | solution.py:2691
  147.8 24.4 %collective-permute-start.1 = (bf16[3,704,256]{2,1,0:T(8,128)(2,1)}, bf16[3,704,256]{2,1,0:T(8,128)(2,1)}, u32[]{:S(2)}, u32[]{:S(2)}) collective-permute-start(bf16[3,704,256]{2,1,0:T(8,128)(2,1)} %get-tuple-element.89), channel_id=1, source_target_pairs={{0,16},{8,24},{16,0},{24,8},{1,17},{9,25},{17,1},{25,9},{2,18},{10... | collective-permute-start | bytes 3244040 | tf_op jit(solution)/shard_map/ppermute | solution.py:2692
  149.0 2.2 copy-start
  151.2 1.4 copy-start.1
  152.6 6.5 %copy-start.2 = (bf16[2,4,256,1024]{3,2,1,0:T(8,128)(2,1)S(1)}, bf16[2,4,256,1024]{3,2,1,0:T(8,128)(2,1)}, u32[]{:S(2)}) copy-start(bf16[2,4,256,1024]{3,2,1,0:T(8,128)(2,1)} %get-tuple-element.74) | copy-start | bytes 12582916
  152.6 6.5 %copy-start.3 = (bf16[2,4,256,704]{3,2,1,0:T(8,128)(2,1)S(1)}, bf16[2,4,256,704]{3,2,1,0:T(8,128)(2,1)}, u32[]{:S(2)}) copy-start(bf16[2,4,256,704]{3,2,1,0:T(8,128)(2,1)} %get-tuple-element.73) | copy-start | bytes 8650756
  172.2 1.0 copy-start.4

commit v7 on v6

--- a/solution.py
+++ b/solution.py
@@ -146,6 +146,10 @@
     across = lax.rem(across + step % 2, 2)
     along = lax.rem(along + step // 2, 2)
     return along * 2 + across
+
+
+def beside(row, way):
+    return lax.rem(row + ROWS + 1 - 2 * way, ROWS)
 
 
 def remote(source, target, sent, arrived, where):
@@ -201,9 +205,9 @@
         self.row, self.buffer, self.sent, self.arrived = row, buffer, sent, arrived
 
     def copy(self, block, way):
-        to = self.row + 1 if way == 0 else self.row - 1
         here = self.buffer.at[block]
-        return remote(here, here, self.sent.at[block, way], self.arrived.at[block], {"row": to})
+        to = {"row": beside(self.row, way)}
+        return remote(here, here, self.sent.at[block, way], self.arrived.at[block], to)
 
     def each(self, block, act):
         @pl.when(jnp.logical_and(block <= self.row, self.row < ROWS - 1))
@@ -304,7 +308,7 @@
             self.coming.at[way, block, self.piece(index)],
             self.sent.at[block, index],
             self.arrived.at[way, block, index],
-            {"row": self.row + 1 - 2 * way},
+            {"row": beside(self.row, way)},
         )
 
     def send(self, block, index):
@@ -558,7 +562,7 @@
             here,
             comp_sent.at[block, way],
             comp_arrived.at[block],
-            {"row": row + 1 - 2 * way},
+            {"row": beside(row, way)},
         )
 
     def comp_each(block, act):

time: 307 us -> 307 us (level)
  transfers between devices with their start and end apart: 2 -> 2, of which waited for: 1 -> 2; matrix products, arithmetic and copies ran while one was open for 0% -> 0% of each run, Pallas kernels for 6% -> 6%
where the time goes in v7:
time: 307 us
  Pallas kernels  299 us (97%)
  local copies, waits for them, and re-layouts  4.46 us (1%)
    pallas_call x1, Pallas kernels, run_attention_back(): pl.pallas_call(attend_back_kernel, name='attend_back', out_shape=(shape(t...  125 us
    pallas_call x1, Pallas kernels, run_experts(): pl.pallas_call(expert_kernel, name='experts', out_shape=(shape(tokens, wi...  81.4 us
    pallas_call x1, Pallas kernels, run_attention(): pl.pallas_call(attend_kernel, name='attend', out_shape=(*kept, shape(toke...  65.2 us
    pallas_call x2, Pallas kernels, slot_products(): pl.pallas_call(product_kernel, name='slot_products', grid=(kinds, halves)...  18 us
    pallas_call x1, Pallas kernels, write_out(): pl.pallas_call(functools.partial(write_kernel, len(arrays), [(source, whe...  8.8 us
  transfers between devices with their start and end apart: 2, of which 2 were waited for; matrix products, arithmetic and copies ran while one was open for 0% of the time, Pallas kernels for 6%

profile of v7, /device:TPU:9, one launch (start us, length us, event | category | flops | bytes accessed | tf_op | source)
XLA Modules:
  0.0 307.2 jit_solution(8521474876866655629)
XLA Ops:
  0.6 65.2 %attend.1 = (bf16[4,128,1024]{2,1,0:T(8,128)(2,1)}, bf16[4,128,384]{2,1,0:T(8,128)(2,1)}, bf16[2,4,128,256]{3,2,1,0:T(8,128)(2,1)}, bf16[2,4,128,128]{3,2,1,0:T(...) custom-call(bf16[128,1024]{1,0:T(8,128)(2,1)} %act_ref.3, ...), custom_call_target="tpu_custom_call" | custom-call | flops 42949672960 | bytes 33554432 | tf_op jit(solution)/shard_map/attend/pallas_call | solution.py:1008
  65.9 81.4 %experts.1 = (f32[128,1024]{1,0:T(8,128)}, bf16[2,4,256,1024]{3,2,1,0:T(8,128)(2,1)}, bf16[2,4,256,704]{3,2,1,0:T(8,128)(2,1)}, bf16[4,256,704]{2,1,0:T(8,128)(2...) custom-call(bf16[128,1024]{1,0:T(8,128)(2,1)} %get-tuple-element.66., ...), custom_call_target="tpu_custom_call" | custom-call | flops 64424509440 | bytes 67108864 | tf_op jit(solution)/shard_map/experts/pallas_call | solution.py:2374
  147.3 0.5 collective-permute-start
  147.8 1.1 collective-permute-start.1
  149.0 0.0 copy-start
  149.0 2.2 copy-done
  151.1 0.0 copy-start.1
  151.1 1.4 copy-done.1
  152.5 0.0 copy-start.2
  152.5 0.0 copy-start.3
  152.6 6.5 %slot_products.3 = f32[1,704,2048]{2,1,0:T(8,128)} custom-call(bf16[1,1024,704]{2,1,0:T(8,128)(2,1)S(1)} %bitcast.29, bf16[2,1024,1024]{2,1,0:T(8,128)(2,1)S(1)} %bitcast.28), custom_call_target="tpu_custom_call" | custom-call | flops 2952790016 | bytes 5767168 | tf_op jit(solution)/shard_map/slot_products/pallas_call | solution.py:2584
  159.1 0.0 copy-done.2
  159.1 0.0 copy-done.3
  159.1 11.5 %slot_products.2 = f32[2,704,2048]{2,1,0:T(8,128)} custom-call(bf16[2,1024,704]{2,1,0:T(8,128)(2,1)S(1)} %bitcast.31, bf16[2,1024,1024]{2,1,0:T(8,128)(2,1)S(1)} %bitcast.30), custom_call_target="tpu_custom_call" | custom-call | flops 5905580032 | bytes 11534336 | tf_op jit(solution)/shard_map/slot_products/pallas_call | solution.py:2584
  170.5 1.4 collective-permute-done.got_x_far
  171.9 0.0 copy-start.4
  171.9 0.1 collective-permute-done.1.got_y_far
  172.0 0.9 copy-done.4
  172.9 125.3 %attend_back.1 = (f32[128,1024]{1,0:T(8,128)}, bf16[128,1024]{1,0:T(8,128)(2,1)}, f32[24,1024]{1,0:T(8,128)}, bf16[3,704,1024]{2,1,0:T(8,128)(2,1)}, bf16[4,8,32...) custom-call(f32[128,1024]{1,0:T(8,128)} %get-tuple-element.76.normed, ...), custom_call_target="tpu_custom_call" | custom-call | flops 42949672960 | bytes 33554432 | tf_op jit(solution)/shard_map/attend_back/pallas_call | solution.py:1782
  298.2 8.8 %write_out.1 = (f32[2,704,1024]{2,1,0:T(8,128)}, f32[704,1024]{1,0:T(8,128)}, f32[1024,768]{1,0:T(8,128)}, f32[512,1024]{1,0:T(8,128)}, f32[512,1024]{1,0:T(8,12...) custom-call(bf16[3,704,1024]{2,1,0:T(8,128)(2,1)} %get-tuple-element, ...), custom_call_target="tpu_custom_call" | custom-call | bytes 25165824 | tf_op jit(solution)/shard_map/write_out/pallas_call | solution.py:2547
Async XLA Ops:
  147.3 24.6 %collective-permute-start = (bf16[3,704,256]{2,1,0:T(8,128)(2,1)}, bf16[3,704,256]{2,1,0:T(8,128)(2,1)S(1)}, u32[]{:S(2)}, u32[]{:S(2)}) collective-permute-start(bf16[3,704,256]{2,1,0:T(8,128)(2,1)} %get-tuple-element.88), channel_id=1, source_target_pairs={{0,8},{8,0},{16,24},{24,16},{1,9},{9,1},{17,25},{25,17},{2,10},{10... | collective-permute-start | bytes 3244040 | tf_op jit(solution)/shard_map/ppermute | solution.py:2695
  147.8 24.2 %collective-permute-start.1 = (bf16[3,704,256]{2,1,0:T(8,128)(2,1)}, bf16[3,704,256]{2,1,0:T(8,128)(2,1)}, u32[]{:S(2)}, u32[]{:S(2)}) collective-permute-start(bf16[3,704,256]{2,1,0:T(8,128)(2,1)} %get-tuple-element.89), channel_id=1, source_target_pairs={{0,16},{8,24},{16,0},{24,8},{1,17},{9,25},{17,1},{25,9},{2,18},{10... | collective-permute-start | bytes 3244040 | tf_op jit(solution)/shard_map/ppermute | solution.py:2696
  149.0 2.2 copy-start
  151.1 1.4 copy-start.1
  152.5 6.5 %copy-start.2 = (bf16[2,4,256,1024]{3,2,1,0:T(8,128)(2,1)S(1)}, bf16[2,4,256,1024]{3,2,1,0:T(8,128)(2,1)}, u32[]{:S(2)}) copy-start(bf16[2,4,256,1024]{3,2,1,0:T(8,128)(2,1)} %get-tuple-element.74) | copy-start | bytes 12582916
  152.5 6.5 %copy-start.3 = (bf16[2,4,256,704]{3,2,1,0:T(8,128)(2,1)S(1)}, bf16[2,4,256,704]{3,2,1,0:T(8,128)(2,1)}, u32[]{:S(2)}) copy-start(bf16[2,4,256,704]{3,2,1,0:T(8,128)(2,1)} %get-tuple-element.73) | copy-start | bytes 8650756
  171.9 1.0 copy-start.4

commit v8 on v7

--- a/solution.py
+++ b/solution.py
@@ -1286,12 +1286,13 @@
         SquareRest(place, which, kept, got, middle, second, result, rest_sent, rest_arrived)
         for which in range(kept.shape[1])
     ]
-    for rest in rests:
+    rests[0].prepare()
+    meet(met)
+    rests[0].run(1)
+    for rest in rests[1:]:
         rest.prepare()
-    meet(met)
+        rest.run(1)
     norm_begin(residual_ref[...], premix_ref[...], normed_grad_ref[...], 0)
-    for rest in rests:
-        rest.run(1)
     residual_grad = cot_ref[...].astype(f32) + norm_grad(
         residual_ref[...], scale_two_ref[...], premix_ref[...], normed_grad_ref[...], 0
     )

time: 307 us -> 306 us (level)
  no operation moved by 1% of the time
where the time goes in v8:
time: 306 us
  Pallas kernels  297 us (97%)
  local copies, waits for them, and re-layouts  4.46 us (1%)
    pallas_call x1, Pallas kernels, run_attention_back(): pl.pallas_call(attend_back_kernel, name='attend_back', out_shape=(shape(t...  124 us
    pallas_call x1, Pallas kernels, run_experts(): pl.pallas_call(expert_kernel, name='experts', out_shape=(shape(tokens, wi...  81.4 us
    pallas_call x1, Pallas kernels, run_attention(): pl.pallas_call(attend_kernel, name='attend', out_shape=(*kept, shape(toke...  65.2 us
    pallas_call x2, Pallas kernels, slot_products(): pl.pallas_call(product_kernel, name='slot_products', grid=(kinds, halves)...  18 us
    pallas_call x1, Pallas kernels, write_out(): pl.pallas_call(functools.partial(write_kernel, len(arrays), [(source, whe...  8.8 us
  transfers between devices with their start and end apart: 2, of which 2 were waited for; matrix products, arithmetic and copies ran while one was open for 0% of the time, Pallas kernels for 6%

profile of v8, /device:TPU:9, one launch (start us, length us, event | category | flops | bytes accessed | tf_op | source)
XLA Modules:
  0.0 305.5 jit_solution(10506789151726776123)
XLA Ops:
  0.6 65.2 %attend.1 = (bf16[4,128,1024]{2,1,0:T(8,128)(2,1)}, bf16[4,128,384]{2,1,0:T(8,128)(2,1)}, bf16[2,4,128,256]{3,2,1,0:T(8,128)(2,1)}, bf16[2,4,128,128]{3,2,1,0:T(...) custom-call(bf16[128,1024]{1,0:T(8,128)(2,1)} %act_ref.3, ...), custom_call_target="tpu_custom_call" | custom-call | flops 42949672960 | bytes 33554432 | tf_op jit(solution)/shard_map/attend/pallas_call | solution.py:1008
  65.9 81.4 %experts.1 = (f32[128,1024]{1,0:T(8,128)}, bf16[2,4,256,1024]{3,2,1,0:T(8,128)(2,1)}, bf16[2,4,256,704]{3,2,1,0:T(8,128)(2,1)}, bf16[4,256,704]{2,1,0:T(8,128)(2...) custom-call(bf16[128,1024]{1,0:T(8,128)(2,1)} %get-tuple-element.66., ...), custom_call_target="tpu_custom_call" | custom-call | flops 64424509440 | bytes 67108864 | tf_op jit(solution)/shard_map/experts/pallas_call | solution.py:2375
  147.3 0.5 collective-permute-start
  147.8 1.1 collective-permute-start.1
  149.0 0.0 copy-start
  149.0 2.2 copy-done
  151.1 0.0 copy-start.1
  151.1 1.4 copy-done.1
  152.5 0.0 copy-start.2
  152.5 0.0 copy-start.3
  152.6 6.5 %slot_products.3 = f32[1,704,2048]{2,1,0:T(8,128)} custom-call(bf16[1,1024,704]{2,1,0:T(8,128)(2,1)S(1)} %bitcast.29, bf16[2,1024,1024]{2,1,0:T(8,128)(2,1)S(1)} %bitcast.28), custom_call_target="tpu_custom_call" | custom-call | flops 2952790016 | bytes 5767168 | tf_op jit(solution)/shard_map/slot_products/pallas_call | solution.py:2585
  159.1 0.0 copy-done.2
  159.1 0.0 copy-done.3
  159.1 11.5 %slot_products.2 = f32[2,704,2048]{2,1,0:T(8,128)} custom-call(bf16[2,1024,704]{2,1,0:T(8,128)(2,1)S(1)} %bitcast.31, bf16[2,1024,1024]{2,1,0:T(8,128)(2,1)S(1)} %bitcast.30), custom_call_target="tpu_custom_call" | custom-call | flops 5905580032 | bytes 11534336 | tf_op jit(solution)/shard_map/slot_products/pallas_call | solution.py:2585
  170.5 1.4 collective-permute-done.got_x_far
  171.9 0.0 copy-start.4
  171.9 0.1 collective-permute-done.1.got_y_far
  172.0 0.9 copy-done.4
  172.9 123.7 %attend_back.1 = (f32[128,1024]{1,0:T(8,128)}, bf16[128,1024]{1,0:T(8,128)(2,1)}, f32[24,1024]{1,0:T(8,128)}, bf16[3,704,1024]{2,1,0:T(8,128)(2,1)}, bf16[4,8,32...) custom-call(f32[128,1024]{1,0:T(8,128)} %get-tuple-element.76.normed, ...), custom_call_target="tpu_custom_call" | custom-call | flops 42949672960 | bytes 33554432 | tf_op jit(solution)/shard_map/attend_back/pallas_call | solution.py:1783
  296.5 8.8 %write_out.1 = (f32[2,704,1024]{2,1,0:T(8,128)}, f32[704,1024]{1,0:T(8,128)}, f32[1024,768]{1,0:T(8,128)}, f32[512,1024]{1,0:T(8,128)}, f32[512,1024]{1,0:T(8,12...) custom-call(bf16[3,704,1024]{2,1,0:T(8,128)(2,1)} %get-tuple-element, ...), custom_call_target="tpu_custom_call" | custom-call | bytes 25165824 | tf_op jit(solution)/shard_map/write_out/pallas_call | solution.py:2548
Async XLA Ops:
  147.3 24.6 %collective-permute-start = (bf16[3,704,256]{2,1,0:T(8,128)(2,1)}, bf16[3,704,256]{2,1,0:T(8,128)(2,1)S(1)}, u32[]{:S(2)}, u32[]{:S(2)}) collective-permute-start(bf16[3,704,256]{2,1,0:T(8,128)(2,1)} %get-tuple-element.88), channel_id=1, source_target_pairs={{0,8},{8,0},{16,24},{24,16},{1,9},{9,1},{17,25},{25,17},{2,10},{10... | collective-permute-start | bytes 3244040 | tf_op jit(solution)/shard_map/ppermute | solution.py:2696
  147.8 24.2 %collective-permute-start.1 = (bf16[3,704,256]{2,1,0:T(8,128)(2,1)}, bf16[3,704,256]{2,1,0:T(8,128)(2,1)}, u32[]{:S(2)}, u32[]{:S(2)}) collective-permute-start(bf16[3,704,256]{2,1,0:T(8,128)(2,1)} %get-tuple-element.89), channel_id=1, source_target_pairs={{0,16},{8,24},{16,0},{24,8},{1,17},{9,25},{17,1},{25,9},{2,18},{10... | collective-permute-start | bytes 3244040 | tf_op jit(solution)/shard_map/ppermute | solution.py:2697
  149.0 2.2 copy-start
  151.1 1.4 copy-start.1
  152.5 6.5 %copy-start.2 = (bf16[2,4,256,1024]{3,2,1,0:T(8,128)(2,1)S(1)}, bf16[2,4,256,1024]{3,2,1,0:T(8,128)(2,1)}, u32[]{:S(2)}) copy-start(bf16[2,4,256,1024]{3,2,1,0:T(8,128)(2,1)} %get-tuple-element.74) | copy-start | bytes 12582916
  152.5 6.5 %copy-start.3 = (bf16[2,4,256,704]{3,2,1,0:T(8,128)(2,1)S(1)}, bf16[2,4,256,704]{3,2,1,0:T(8,128)(2,1)}, u32[]{:S(2)}) copy-start(bf16[2,4,256,704]{3,2,1,0:T(8,128)(2,1)} %get-tuple-element.73) | copy-start | bytes 8650756
  171.9 1.0 copy-start.4
